TPU v7x, 256 devices: a whole 4x4x8 slice. The times are simulated.
256 devices in a mesh: ctx: 16 (over x_lo, y, core), ch: 16 (over x_hi, z).
Axes of the slice: x: 4 (x_hi: 2, x_lo: 2; x = x_hi * 2 + x_lo), y: 4, z: 8, core: 2. Of those that a mesh axis runs over, the one named last changes fastest.
Arguments:
- inputs: bfloat16 [1024, 32768], P('ch', 'ctx'), may hold values from -6 to 6
- cotangent: bfloat16 [1024, 32768], P('ch', 'ctx'), may hold values from -0.03125 to 0.03125
- features: float32 [64, 4096], P(None, 'ctx'), may hold values from -6 to 6
- projection: float32 [64, 1024], P(None, 'ch'), may hold values from -0.75 to 0.75
- decay_rates: float32 [1024], P('ch'), may hold values from 0.5 to 8
Outputs:
- x_grad: bfloat16 [1024, 32768], P('ch', 'ctx')
- filter_grad: float32 [1024, 4096], P('ch', 'ctx')
- feature_grad: float32 [64, 4096], P(None, 'ctx')
All inputs are finite; a program needn't handle non-finite values.
Results may differ from a plain program's by a relative error of at most 0.001.
Values may be sent and summed in bfloat16 or wider, within the bound.
No kernel may reach another device: no remote copies, remote signals or barrier semaphores. Data moves between devices by JAX's collectives and lax.ppermute only.
A program may use at most 128 MiB of HBM per device.

v0:
```python
import math

import jax
import jax.numpy as jnp
import numpy as np
from jax import lax
from jax.experimental import pallas as pl
from jax.experimental.pallas import tpu as pltpu
from jax.sharding import PartitionSpec as P

SUB = 256
LANES = 128
F32 = jnp.float32
BF16 = jnp.bfloat16
VMEM_LIMIT = 40 * 1024 * 1024


def dft_tables():
    order = np.concatenate([np.arange(0, SUB, 2), np.arange(1, SUB, 2)])
    angles = 2.0 * np.pi * np.arange(SUB)[:, None] * (order[None, :] + 0.5) / (2 * SUB)
    forward = np.concatenate([np.cos(angles), -np.sin(angles)], axis=1)
    pair = []
    for table in (forward, forward.T / SUB):
        high = table.astype(jnp.bfloat16)
        low = (table - high.astype(np.float64)).astype(jnp.bfloat16)
        pair.append(jnp.asarray(np.stack([high, low])))
    return pair


def dot(left, right):
    return jnp.dot(left, right, preferred_element_type=F32)


def two_terms(values):
    high = values.astype(BF16)
    return high, (values - high.astype(F32)).astype(BF16)


def dot_terms(values, table):
    high, low = two_terms(values)
    return dot(high, table[0]) + dot(high, table[1]) + dot(low, table[0])


def pack_kernel(groups, taps, cot_ref, in_ref, feat_ref, proj_ref, rate_ref, pay_ref, decay_ref, rows, frows):
    channels, block_len = cot_ref.shape
    per = channels // groups
    subs = block_len // SUB
    for which, ref in enumerate((cot_ref, in_ref)):
        for sub in range(subs):
            for half in range(2):
                start = sub * SUB + half * LANES
                rows[2 * which + half, pl.ds(sub, channels, stride=subs), :] = ref[:, start : start + LANES].astype(F32)
    span = per * subs
    for part in range(4):
        for group in range(groups):
            pay_ref[group, part * span : (part + 1) * span, :] = rows[part, group * span : (group + 1) * span, :].astype(BF16)
    tap_rows = feat_ref.shape[1]
    first = lax.axis_index("ctx") * tap_rows
    positions = (first + lax.broadcasted_iota(jnp.int32, (1, tap_rows), 1)).astype(F32)
    diagonal = lax.broadcasted_iota(jnp.int32, (channels, channels), 0) == lax.broadcasted_iota(
        jnp.int32, (channels, channels), 1
    )
    rates = jnp.sum(jnp.where(diagonal, rate_ref[...], 0.0), axis=1, keepdims=True)
    decay = jnp.exp(-rates * (positions / taps))
    decay_ref[...] = decay
    product = lax.dot_general(
        proj_ref[...],
        feat_ref[...],
        (((0,), (0,)), ((), ())),
        precision=lax.Precision.HIGHEST,
        preferred_element_type=F32,
    )
    high, low = two_terms(decay * product)
    high = high.astype(F32)
    low = low.astype(F32)
    for group in range(groups):
        own = slice(group * per, (group + 1) * per)
        for half in range(2):
            lanes = slice(half * LANES, (half + 1) * LANES)
            base = half * 2 * per
            frows[group, base : base + per, :] = high[own, lanes]
            frows[group, base + per : base + 2 * per, :] = low[own, lanes]
    pay_ref[:, 4 * span :, :] = frows[...].astype(BF16)


def block_spectra(recv_ref, base, table_ref, store):
    groups = recv_ref.shape[0]
    span = 32
    per, subs = 4, 8
    step = 4
    for first in range(0, groups, step):
        halves = [
            recv_ref[first : first + step, base + half * span : base + (half + 1) * span, :].reshape(step * span, LANES)
            for half in range(2)
        ]
        left = jnp.concatenate(halves, axis=1)
        result = dot(left, table_ref[0]) + dot(left, table_ref[1])
        for src in range(step):
            for chan in range(per):
                row = (src * per + chan) * subs
                for tile in range(4):
                    store(chan, tile, (first + src) * subs, result[row : row + subs, tile * LANES : (tile + 1) * LANES])


def taps_kernel(recv_ref, fwd_ref, inv_ref, win_ref, grad_ref, cot_spec, in_spec, sums, spec):
    groups = recv_ref.shape[0]
    per, subs, lags = 4, 8, 16
    blocks = groups * subs

    def store_cot(chan, tile, row, value):
        cot_spec[chan, tile, row : row + subs, :] = value

    def store_in(chan, tile, row, value):
        in_spec[chan, tile, row : row + subs, :] = value

    block_spectra(recv_ref, 0, fwd_ref, store_cot)
    cot_spec[:, :, blocks:, :] = jnp.zeros((per, 4, subs, LANES), F32)
    block_spectra(recv_ref, 64, fwd_ref, store_in)
    win_ref[:, :, blocks:, :] = jnp.zeros((per, 4, lags, LANES), F32)
    for chan in range(per):
        now = [cot_spec[chan, tile, 0:blocks, :] for tile in range(4)]
        nxt = [cot_spec[chan, tile, 1 : blocks + 1, :] for tile in range(4)]
        win_ref[chan, 0, 0:blocks, :] = now[0] + nxt[2]
        win_ref[chan, 1, 0:blocks, :] = now[1] - nxt[3]
        win_ref[chan, 2, 0:blocks, :] = now[2] - nxt[0]
        win_ref[chan, 3, 0:blocks, :] = now[3] + nxt[1]

    def one(index, carry):
        chan = index // 2
        half = index % 2
        acc_re = [None] * lags
        acc_im = [None] * lags
        for src in range(groups):
            left_re = in_spec[chan, half, src * subs : (src + 1) * subs, :]
            left_im = in_spec[chan, 2 + half, src * subs : (src + 1) * subs, :]
            for lag in range(lags):
                row = src * subs + lag
                win_re = win_ref[chan, half, row : row + subs, :]
                win_im = win_ref[chan, 2 + half, row : row + subs, :]
                term_re = left_re * win_re + left_im * win_im
                term_im = left_re * win_im - left_im * win_re
                acc_re[lag] = term_re if src == 0 else acc_re[lag] + term_re
                acc_im[lag] = term_im if src == 0 else acc_im[lag] + term_im
        for part, acc in enumerate((acc_re, acc_im)):
            for lag in range(lags):
                sums[part, lag * subs : (lag + 1) * subs, :] = acc[lag]
            total = sums[part, pl.ds(0, lags, stride=subs), :]
            for sub in range(1, subs):
                total = total + sums[part, pl.ds(sub, lags, stride=subs), :]
            spec[2 * part + half, pl.ds(chan, lags, stride=per), :] = total
        return carry

    lax.fori_loop(0, 2 * per, one, 0)
    left = jnp.concatenate([spec[tile] for tile in range(4)], axis=1)
    result = dot_terms(left, inv_ref)
    for lag in range(lags):
        own = slice(lag * per, (lag + 1) * per)
        grad_ref[lag, 0:per, :] = result[own, 0:LANES]
        grad_ref[lag, per : 2 * per, :] = result[own, LANES:]


def inputs_kernel(recv_ref, win_ref, fwd_ref, inv_ref, grad_ref, frows, fspec, spec):
    groups = recv_ref.shape[0]
    per, subs, lags = 4, 8, 16
    blocks = groups * subs
    frows[...] = recv_ref[:, 128:144, :].astype(F32).reshape(groups * 16, LANES)
    terms = []
    for term in range(2):
        chans = []
        for chan in range(per):
            halves = [frows[pl.ds(half * 2 * per + term * per + chan, lags, stride=16), :] for half in range(2)]
            chans.append(jnp.concatenate(halves, axis=1))
        terms.append(jnp.concatenate(chans, axis=0).astype(BF16))
    result = dot(terms[0], fwd_ref[0]) + dot(terms[0], fwd_ref[1]) + dot(terms[1], fwd_ref[0])
    for tile in range(4):
        for chan in range(per):
            fspec[chan, tile] = result[chan * lags : (chan + 1) * lags, tile * LANES : (tile + 1) * LANES]

    def one(index, carry):
        chan = index // 2
        half = index % 2
        filt_re = [jnp.broadcast_to(fspec[chan, half, lag : lag + 1, :], (subs, LANES)) for lag in range(lags)]
        filt_im = [jnp.broadcast_to(fspec[chan, 2 + half, lag : lag + 1, :], (subs, LANES)) for lag in range(lags)]
        for src in range(groups):
            acc_re = None
            acc_im = None
            for lag in range(lags):
                row = src * subs + lag
                win_re = win_ref[chan, half, row : row + subs, :]
                win_im = win_ref[chan, 2 + half, row : row + subs, :]
                term_re = filt_re[lag] * win_re + filt_im[lag] * win_im
                term_im = filt_re[lag] * win_im - filt_im[lag] * win_re
                acc_re = term_re if lag == 0 else acc_re + term_re
                acc_im = term_im if lag == 0 else acc_im + term_im
            spec[chan, half, src * subs : (src + 1) * subs, :] = acc_re
            spec[chan, 2 + half, src * subs : (src + 1) * subs, :] = acc_im
        return carry

    lax.fori_loop(0, 2 * per, one, 0)
    for first in range(0, per, 2):
        pair = []
        for chan in (first, first + 1):
            left = jnp.concatenate([spec[chan, tile] for tile in range(4)], axis=1)
            pair.append(dot_terms(left, inv_ref).reshape(groups, subs, SUB))
        both = jnp.concatenate(pair, axis=1)
        grad_ref[:, first * subs : (first + 2) * subs, :] = both.astype(BF16)


def features_kernel(grad_ref, decay_ref, proj_ref, out_ref, part_ref):
    groups = grad_ref.shape[0]
    per = grad_ref.shape[1] // 2
    for group in range(groups):
        own = slice(group * per, (group + 1) * per)
        out_ref[own, 0:LANES] = grad_ref[group, 0:per, :]
        out_ref[own, LANES:] = grad_ref[group, per : 2 * per, :]
    part_ref[...] = jnp.dot(
        proj_ref[...],
        decay_ref[...] * out_ref[...],
        precision=lax.Precision.HIGHEST,
        preferred_element_type=F32,
    )


def call(kernel, out, scratch, flops):
    return pl.pallas_call(
        kernel,
        out_shape=out,
        scratch_shapes=[pltpu.VMEM(shape, F32) for shape in scratch],
        compiler_params=pltpu.CompilerParams(vmem_limit_bytes=VMEM_LIMIT),
        cost_estimate=pl.CostEstimate(flops=flops, bytes_accessed=1 << 20, transcendentals=0),
    )


def shifted(values, axis, distance, ring):
    size = lax.axis_size(axis)
    route = [(i, i - i % ring + (i + distance) % ring) for i in range(size)]
    return lax.ppermute(values, axis, route)


def summed(values, axis):
    size = lax.axis_size(axis)
    half = size // 2
    values = values + lax.ppermute(values, axis, [(i, (i + half) % size) for i in range(size)])
    below = shifted(values, axis, 1, half)
    above = shifted(values, axis, -1, half)
    two = values + above
    three = two + below
    return three + shifted(three, axis, -3, half) + shifted(two, axis, 3, half)


def shards(inputs, cotangent, features, projection, decay_rates):
    channels, block_len = inputs.shape
    tap_rows = features.shape[1]
    groups = lax.axis_size("ctx")
    per = channels // groups
    subs = block_len // SUB
    taps = 2 * block_len
    lags = taps // SUB
    shape = jax.ShapeDtypeStruct
    forward, backward = dft_tables()

    def exchanged(values):
        return lax.all_to_all(values, "ctx", 0, 0, tiled=True)

    payload, decay = call(
        lambda *refs: pack_kernel(groups, taps, *refs),
        (shape((groups, 144, LANES), BF16), shape((channels, tap_rows), F32)),
        [(4, channels * subs, LANES), (groups, 16, LANES)],
        1 << 22,
    )(cotangent, inputs, features, projection, decay_rates.reshape(1, channels))
    received = exchanged(payload)
    blocks = groups * subs
    windows, tap_grads = call(
        taps_kernel,
        (shape((per, 4, blocks + lags, LANES), F32), shape((groups, 2 * per, LANES), F32)),
        [(per, 4, blocks + subs, LANES), (per, 4, blocks, LANES), (2, lags * subs, LANES), (4, per * lags, LANES)],
        1 << 32,
    )(received, forward, backward)
    tap_grads = exchanged(tap_grads)
    x_parts = call(
        inputs_kernel,
        shape((groups, per * subs, SUB), BF16),
        [(groups * 16, LANES), (per, 4, lags, LANES), (per, 4, blocks, LANES)],
        1 << 32,
    )(received, windows, forward, backward)
    x_grad = exchanged(x_parts).reshape(channels, block_len)
    filter_grad, part = call(
        features_kernel,
        (shape((channels, tap_rows), F32), shape((projection.shape[0], tap_rows), F32)),
        [],
        1 << 22,
    )(tap_grads, decay, projection)
    feature_grad = summed(part, "ch")
    return (x_grad, filter_grad, feature_grad)


def solution(mesh):
    placed = (P("ch", "ctx"), P("ch", "ctx"), P(None, "ctx"), P(None, "ch"), P("ch"))
    return jax.shard_map(
        shards,
        mesh=mesh,
        in_specs=placed,
        out_specs=(P("ch", "ctx"), P("ch", "ctx"), P(None, "ctx")),
        check_vma=False,
    )
```

profile of v0, /device:TPU:32, one launch (start us, length us, event | category | flops | bytes accessed | tf_op | source)
XLA Modules:
  0.0 68.1 jit_solution(4880779699892921628)
XLA Ops:
  0.6 0.9 %copy-done = bf16[64,2048]{1,0:T(8,128)(2,1)S(1)} copy-done((bf16[64,2048]{1,0:T(8,128)(2,1)S(1)}, bf16[64,2048]{1,0:T(8,128)(2,1)}, u32[]{:S(2)}) %copy-start) | copy-done | bytes 262168
  1.6 0.9 %copy-done.1 = bf16[64,2048]{1,0:T(8,128)(2,1)S(1)} copy-done((bf16[64,2048]{1,0:T(8,128)(2,1)S(1)}, bf16[64,2048]{1,0:T(8,128)(2,1)}, u32[]{:S(2)}) %copy-start.1) | copy-done | bytes 262168
  2.5 0.8 %copy-done.2 = f32[64,64]{1,0:T(8,128)S(1)} copy-done((f32[64,64]{1,0:T(8,128)S(1)}, f32[64,64]{1,0:T(8,128)}, u32[]{:S(2)}) %copy-start.2) | copy-done | bytes 16408
  3.3 0.8 %copy-done.4 = f32[64,256]{1,0:T(8,128)S(1)} copy-done((f32[64,256]{1,0:T(8,128)S(1)}, f32[64,256]{1,0:T(8,128)}, u32[]{:S(2)}) %copy-start.4) | copy-done | bytes 65560
  4.1 0.7 copy-done.5
  4.8 0.4 shard_map.94
  5.2 16.9 %all_to_all.15.recv_ref = bf16[16,144,128]{2,1,0:T(8,128)(2,1)S(1)} all-to-all(bf16[16,144,128]{2,1,0:T(8,128)(2,1)S(1)} %get-tuple-element.9), channel_id=1, replica_groups=mesh['ctx'=16,'ch'=16] {'ctx'}, dimensions={0} | all-to-all | bytes 1179648 | tf_op jit(solution)/shard_map/all_to_all | solution.py:263
  22.1 3.6 %shard_map.95 = (f32[4,4,144,128]{3,2,1,0:T(8,128)S(1)}, f32[16,8,128]{2,1,0:T(8,128)S(1)}) custom-call(bf16[16,144,128]{2,1,0:T(8,128)(2,1)S(1)} %all_to_all.15.recv_ref, bf16[2,256,512]{2,1,0:T(8,128)(2,1)S(1)} %copy-done.7, bf16[2,512,256]{2,1,0:T(8,128)(2,1)S(1)} %copy-done.6), custom_call_target="tpu_custom_call" | custom-call | flops 4294967296 | bytes 1048576 | tf_op jit(solution)/shard_map/pallas_call | solution.py:273
  25.7 8.7 %all_to_all.16.grad_ref = f32[16,8,128]{2,1,0:T(8,128)S(1)} all-to-all(f32[16,8,128]{2,1,0:T(8,128)S(1)} %get-tuple-element.11), channel_id=1, replica_groups=mesh['ctx'=16,'ch'=16] {'ctx'}, dimensions={0} | all-to-all | bytes 131072 | tf_op jit(solution)/shard_map/all_to_all | solution.py:263
  34.4 0.7 shard_map.97
  35.1 2.7 %collective-permute-start = (f32[64,256]{1,0:T(8,128)S(1)}, f32[64,256]{1,0:T(8,128)S(1)}, u32[]{:S(2)}, u32[]{:S(2)}) collective-permute-start(f32[64,256]{1,0:T(8,128)S(1)} %get-tuple-element.14), channel_id=1, source_target_pairs={{0,8},{1,9},{2,10},{3,11},{4,12},{5,13},{6,14},{7,15},{8,0},{9,1},... | collective-permute-start | bytes 196616 | tf_op jit(solution)/shard_map/ppermute | solution.py:243
  37.8 3.0 %collective-permute-done = f32[64,256]{1,0:T(8,128)S(1)} collective-permute-done((f32[64,256]{1,0:T(8,128)S(1)}, f32[64,256]{1,0:T(8,128)S(1)}, u32[]{:S(2)}, u32[]{:S(2)}) %collective-permute-start) | collective-permute-done | bytes 65568 | tf_op jit(solution)/shard_map/ppermute | solution.py:243
  40.9 2.0 %collective-permute-start.2 = (f32[64,256]{1,0:T(8,128)S(1)}, f32[64,256]{1,0:T(8,128)S(1)}, u32[]{:S(2)}, u32[]{:S(2)}) collective-permute-start(f32[64,256]{1,0:T(8,128)S(1)} %add.15), channel_id=1, source_target_pairs={{0,1},{1,2},{2,3},{3,4},{4,5},{5,6},{6,7},{7,0},{8,9},{9,10},{10,1... | collective-permute-start | bytes 196616 | tf_op jit(solution)/shard_map/ppermute | solution.py:237
  42.9 0.1 collective-permute-start.1
  43.0 4.2 %shard_map.96 = bf16[16,32,256]{2,1,0:T(8,128)(2,1)} custom-call(bf16[16,144,128]{2,1,0:T(8,128)(2,1)S(1)} %all_to_all.15.recv_ref, f32[4,4,144,128]{3,2,1,0:T(8,128)S(1)} %get-tuple-element.10.win_ref, bf16[2,256,512]{2,1,0:T(8,128)(2,1)S(1)} %copy-done.7, bf16[2,512,256]{2,1,0:T(8,128)(2,1)S(1)} %copy-done.6), custom_call_target="tpu_custom_call" | custom-call | flops 4294967296 | bytes 1048576 | tf_op jit(solution)/shard_map/pallas_call | solution.py:280
  47.2 3.5 %all-to-all-start.1 = ((bf16[16,32,256]{2,1,0:T(8,128)(2,1)}), bf16[16,32,256]{2,1,0:T(8,128)(2,1)S(1)}, u32[]{:S(2)}, u32[]{:S(2)}) async-start(bf16[16,32,256]{2,1,0:T(8,128)(2,1)} %shard_map.96), calls=%async_computation.1 | async-start | bytes 524288 | tf_op jit(solution)/shard_map/all_to_all | solution.py:263
  50.8 0.0 collective-permute-done.2
  50.8 0.0 collective-permute-done.1
  50.8 7.1 %collective-permute-start.4 = (f32[64,256]{1,0:T(8,128)S(1)}, f32[64,256]{1,0:T(8,128)S(1)}, u32[]{:S(2)}, u32[]{:S(2)}) collective-permute-start(f32[64,256]{1,0:T(8,128)S(1)} %get-tuple-element.16), channel_id=1, source_target_pairs={{0,3},{1,4},{2,5},{3,6},{4,7},{5,0},{6,1},{7,2},{8,11},{9,12},{10,... | collective-permute-start | bytes 196616 | tf_op jit(solution)/shard_map/ppermute | solution.py:237
  57.9 0.8 %all-to-all-done.1 = bf16[16,32,256]{2,1,0:T(8,128)(2,1)S(1)} async-done(((bf16[16,32,256]{2,1,0:T(8,128)(2,1)}), bf16[16,32,256]{2,1,0:T(8,128)(2,1)S(1)}, u32[]{:S(2)}, u32[]{:S(2)}) %all-to-all-start.1) | async-done | bytes 262176 | tf_op jit(solution)/shard_map/all_to_all | solution.py:263
  58.8 0.8 %reshape.13 = bf16[64,2048]{1,0:T(8,128)(2,1)} reshape(bf16[16,32,256]{2,1,0:T(8,128)(2,1)S(1)} %all-to-all-done.1) | data formatting | bytes 524288 | tf_op jit(solution)/shard_map/reshape | solution.py:286
  59.6 2.3 %collective-permute-done.4 = f32[64,256]{1,0:T(8,128)S(1)} collective-permute-done((f32[64,256]{1,0:T(8,128)S(1)}, f32[64,256]{1,0:T(8,128)S(1)}, u32[]{:S(2)}, u32[]{:S(2)}) %collective-permute-start.4) | collective-permute-done | bytes 65568 | tf_op jit(solution)/shard_map/ppermute | solution.py:237
  61.9 5.5 %collective-permute-done.3 = f32[64,256]{1,0:T(8,128)S(1)} collective-permute-done((f32[64,256]{1,0:T(8,128)S(1)}, f32[64,256]{1,0:T(8,128)S(1)}, u32[]{:S(2)}, u32[]{:S(2)}) %collective-permute-start.3) | collective-permute-done | bytes 65568 | tf_op jit(solution)/shard_map/ppermute | solution.py:237
  67.4 0.6 add_add_fusion
  (14 shorter events, 0.0 us)
Async XLA Ops:
  0.6 1.0 %copy-start = (bf16[64,2048]{1,0:T(8,128)(2,1)S(1)}, bf16[64,2048]{1,0:T(8,128)(2,1)}, u32[]{:S(2)}) copy-start(bf16[64,2048]{1,0:T(8,128)(2,1)} %refs_0_.1) | copy-start | bytes 786436
  1.6 0.9 %copy-start.1 = (bf16[64,2048]{1,0:T(8,128)(2,1)S(1)}, bf16[64,2048]{1,0:T(8,128)(2,1)}, u32[]{:S(2)}) copy-start(bf16[64,2048]{1,0:T(8,128)(2,1)} %refs_1_.1) | copy-start | bytes 786436
  2.5 0.8 %copy-start.2 = (f32[64,64]{1,0:T(8,128)S(1)}, f32[64,64]{1,0:T(8,128)}, u32[]{:S(2)}) copy-start(f32[64,64]{1,0:T(8,128)} %proj_ref.1) | copy-start | bytes 49156
  3.3 0.8 %copy-start.4 = (f32[64,256]{1,0:T(8,128)S(1)}, f32[64,256]{1,0:T(8,128)}, u32[]{:S(2)}) copy-start(f32[64,256]{1,0:T(8,128)} %refs_2_.1) | copy-start | bytes 196612
  4.1 0.7 copy-start.5
  4.8 17.4 %copy-start.6 = (bf16[2,512,256]{2,1,0:T(8,128)(2,1)S(1)}, bf16[2,512,256]{2,1,0:T(8,128)(2,1)}, u32[]{:S(2)}) copy-start(bf16[2,512,256]{2,1,0:T(8,128)(2,1)} %constant.5.clone.inv_ref) | copy-start | bytes 1572868
  4.8 17.4 %copy-start.7 = (bf16[2,256,512]{2,1,0:T(8,128)(2,1)S(1)}, bf16[2,256,512]{2,1,0:T(8,128)(2,1)}, u32[]{:S(2)}) copy-start(bf16[2,256,512]{2,1,0:T(8,128)(2,1)} %constant.4.clone.fwd_ref) | copy-start | bytes 1572868
  22.1 12.3 %copy-start.3 = (f32[64,64]{1,0:T(8,128)S(1)}, f32[64,64]{1,0:T(8,128)}, u32[]{:S(2)}) copy-start(f32[64,64]{1,0:T(8,128)} %proj_ref.1) | copy-start | bytes 49156
  35.1 5.8 %collective-permute-start = (f32[64,256]{1,0:T(8,128)S(1)}, f32[64,256]{1,0:T(8,128)S(1)}, u32[]{:S(2)}, u32[]{:S(2)}) collective-permute-start(f32[64,256]{1,0:T(8,128)S(1)} %get-tuple-element.14), channel_id=1, source_target_pairs={{0,8},{1,9},{2,10},{3,11},{4,12},{5,13},{6,14},{7,15},{8,0},{9,1},... | collective-permute-start | bytes 196616 | tf_op jit(solution)/shard_map/ppermute | solution.py:243
  40.9 9.9 %collective-permute-start.2 = (f32[64,256]{1,0:T(8,128)S(1)}, f32[64,256]{1,0:T(8,128)S(1)}, u32[]{:S(2)}, u32[]{:S(2)}) collective-permute-start(f32[64,256]{1,0:T(8,128)S(1)} %add.15), channel_id=1, source_target_pairs={{0,1},{1,2},{2,3},{3,4},{4,5},{5,6},{6,7},{7,0},{8,9},{9,10},{10,1... | collective-permute-start | bytes 196616 | tf_op jit(solution)/shard_map/ppermute | solution.py:237
  42.9 7.9 %collective-permute-start.1 = (f32[64,256]{1,0:T(8,128)S(1)}, f32[64,256]{1,0:T(8,128)S(1)}, u32[]{:S(2)}, u32[]{:S(2)}) collective-permute-start(f32[64,256]{1,0:T(8,128)S(1)} %add.15), channel_id=1, source_target_pairs={{0,7},{1,0},{2,1},{3,2},{4,3},{5,4},{6,5},{7,6},{8,15},{9,8},{10,9... | collective-permute-start | bytes 196616 | tf_op jit(solution)/shard_map/ppermute | solution.py:237
  47.2 11.6 %all-to-all-start.1 = ((bf16[16,32,256]{2,1,0:T(8,128)(2,1)}), bf16[16,32,256]{2,1,0:T(8,128)(2,1)S(1)}, u32[]{:S(2)}, u32[]{:S(2)}) async-start(bf16[16,32,256]{2,1,0:T(8,128)(2,1)} %shard_map.96), calls=%async_computation.1 | async-start | bytes 524288 | tf_op jit(solution)/shard_map/all_to_all | solution.py:263
  50.8 11.1 %collective-permute-start.4 = (f32[64,256]{1,0:T(8,128)S(1)}, f32[64,256]{1,0:T(8,128)S(1)}, u32[]{:S(2)}, u32[]{:S(2)}) collective-permute-start(f32[64,256]{1,0:T(8,128)S(1)} %get-tuple-element.16), channel_id=1, source_target_pairs={{0,3},{1,4},{2,5},{3,6},{4,7},{5,0},{6,1},{7,2},{8,11},{9,12},{10,... | collective-permute-start | bytes 196616 | tf_op jit(solution)/shard_map/ppermute | solution.py:237
  57.9 9.5 %collective-permute-start.3 = (f32[64,256]{1,0:T(8,128)S(1)}, f32[64,256]{1,0:T(8,128)S(1)}, u32[]{:S(2)}, u32[]{:S(2)}) collective-permute-start(f32[64,256]{1,0:T(8,128)S(1)} %get-tuple-element.15), channel_id=1, source_target_pairs={{0,5},{1,6},{2,7},{3,0},{4,1},{5,2},{6,3},{7,4},{8,13},{9,14},{10,... | collective-permute-start | bytes 196616 | tf_op jit(solution)/shard_map/ppermute | solution.py:237
where the time goes:
time: 68.7 us; the launch traced here: 68.1 us
  blocking collectives  25.6 us (37%)
  starting transfers between devices  15.5 us (23%)
  waiting for transfers between devices  11.7 us (17%)
  Pallas kernels  8.91 us (13%)
  local copies, waits for them, and re-layouts  4.98 us (7%)
  between operations  0.7 us (1%)
    all_to_all x2, blocking collectives, exchanged(): return lax.all_to_all(values, 'ctx', 0, 0, tiled=True)  25.6 us
    ppermute x4, starting transfers between devices, shifted(): return lax.ppermute(values, axis, route)  9.23 us
    ppermute x4, waiting for transfers between devices, shifted(): return lax.ppermute(values, axis, route)  7.81 us
    pallas_call x1, Pallas kernels, shards(): call(inputs_kernel, shape((groups, per * subs, SUB), BF16), [(groups * 16...  4.24 us
    unnamed x16, local copies, waits for them, and re-layouts  4.15 us
    pallas_call x1, Pallas kernels, shards(): call(taps_kernel, (shape((per, 4, blocks + lags, LANES), F32), shape((gro...  3.56 us
    all_to_all x1, starting transfers between devices, exchanged(): return lax.all_to_all(values, 'ctx', 0, 0, tiled=True)  3.53 us
    ppermute x1, waiting for transfers between devices, summed(): lax.ppermute(values, axis, [(i, (i + half) % size) for i in range(size)])  3.04 us
  transfers between devices with their start and end apart: 6, of which 4 were waited for; matrix products, arithmetic and copies ran while one was open for 1% of the time, Pallas kernels for 6%

commit v1 on v0

--- a/solution.py
+++ b/solution.py
@@ -41,19 +41,18 @@
     return dot(high, table[0]) + dot(high, table[1]) + dot(low, table[0])
 
 
-def pack_kernel(groups, taps, cot_ref, in_ref, feat_ref, proj_ref, rate_ref, pay_ref, decay_ref, rows, frows):
+def pack_kernel(groups, taps, *refs):
+    sources, (pay_ref, decay_ref, rows, frows), held, sems = refs[:5], refs[5:9], refs[9:14], refs[14]
+    copies = [pltpu.make_async_copy(src, dst, sems.at[i]) for i, (src, dst) in enumerate(zip(sources, held))]
+    for copy in copies:
+        copy.start()
+    feat_ref, proj_ref, rate_ref, cot_ref, in_ref = held
     channels, block_len = cot_ref.shape
+    for copy in copies[:3]:
+        copy.wait()
     per = channels // groups
     subs = block_len // SUB
-    for which, ref in enumerate((cot_ref, in_ref)):
-        for sub in range(subs):
-            for half in range(2):
-                start = sub * SUB + half * LANES
-                rows[2 * which + half, pl.ds(sub, channels, stride=subs), :] = ref[:, start : start + LANES].astype(F32)
     span = per * subs
-    for part in range(4):
-        for group in range(groups):
-            pay_ref[group, part * span : (part + 1) * span, :] = rows[part, group * span : (group + 1) * span, :].astype(BF16)
     tap_rows = feat_ref.shape[1]
     first = lax.axis_index("ctx") * tap_rows
     positions = (first + lax.broadcasted_iota(jnp.int32, (1, tap_rows), 1)).astype(F32)
@@ -81,6 +80,15 @@
             frows[group, base : base + per, :] = high[own, lanes]
             frows[group, base + per : base + 2 * per, :] = low[own, lanes]
     pay_ref[:, 4 * span :, :] = frows[...].astype(BF16)
+    for which, ref in enumerate((cot_ref, in_ref)):
+        copies[3 + which].wait()
+        for sub in range(subs):
+            for half in range(2):
+                start = sub * SUB + half * LANES
+                rows[2 * which + half, pl.ds(sub, channels, stride=subs), :] = ref[:, start : start + LANES].astype(F32)
+    for part in range(4):
+        for group in range(groups):
+            pay_ref[group, part * span : (part + 1) * span, :] = rows[part, group * span : (group + 1) * span, :].astype(BF16)
 
 
 def block_spectra(recv_ref, base, table_ref, store):
@@ -221,12 +229,19 @@
     )
 
 
-def call(kernel, out, scratch, flops):
+def call(kernel, out, scratch, flops, fetched=(), limit=VMEM_LIMIT):
+    scratch_shapes = [pltpu.VMEM(shape, F32) for shape in scratch]
+    specs = {}
+    if fetched:
+        scratch_shapes += [pltpu.VMEM(value.shape, value.dtype) for value in fetched]
+        scratch_shapes.append(pltpu.SemaphoreType.DMA((len(fetched),)))
+        specs["in_specs"] = [pl.BlockSpec(memory_space=pltpu.HBM)] * len(fetched)
     return pl.pallas_call(
         kernel,
         out_shape=out,
-        scratch_shapes=[pltpu.VMEM(shape, F32) for shape in scratch],
-        compiler_params=pltpu.CompilerParams(vmem_limit_bytes=VMEM_LIMIT),
+        scratch_shapes=scratch_shapes,
+        **specs,
+        compiler_params=pltpu.CompilerParams(vmem_limit_bytes=limit),
         cost_estimate=pl.CostEstimate(flops=flops, bytes_accessed=1 << 20, transcendentals=0),
     )
 
@@ -237,7 +252,7 @@
     return lax.ppermute(values, axis, route)
 
 
-def summed(values, axis):
+def summed(values, axis, other):
     size = lax.axis_size(axis)
     half = size // 2
     values = values + lax.ppermute(values, axis, [(i, (i + half) % size) for i in range(size)])
@@ -245,7 +260,9 @@
     above = shifted(values, axis, -1, half)
     two = values + above
     three = two + below
-    return three + shifted(three, axis, -3, half) + shifted(two, axis, 3, half)
+    far = (shifted(three, axis, -3, half), shifted(two, axis, 3, half))
+    far, other = lax.optimization_barrier((far, other))
+    return three + far[0] + far[1], other
 
 
 def shards(inputs, cotangent, features, projection, decay_rates):
@@ -267,7 +284,9 @@
         (shape((groups, 144, LANES), BF16), shape((channels, tap_rows), F32)),
         [(4, channels * subs, LANES), (groups, 16, LANES)],
         1 << 22,
-    )(cotangent, inputs, features, projection, decay_rates.reshape(1, channels))
+        (features, projection, decay_rates.reshape(1, channels), cotangent, inputs),
+        60 * 1024 * 1024,
+    )(features, projection, decay_rates.reshape(1, channels), cotangent, inputs)
     received = exchanged(payload)
     blocks = groups * subs
     windows, tap_grads = call(
@@ -283,14 +302,15 @@
         [(groups * 16, LANES), (per, 4, lags, LANES), (per, 4, blocks, LANES)],
         1 << 32,
     )(received, windows, forward, backward)
-    x_grad = exchanged(x_parts).reshape(channels, block_len)
+    tap_grads, x_parts = lax.optimization_barrier((tap_grads, x_parts))
     filter_grad, part = call(
         features_kernel,
         (shape((channels, tap_rows), F32), shape((projection.shape[0], tap_rows), F32)),
         [],
         1 << 22,
     )(tap_grads, decay, projection)
-    feature_grad = summed(part, "ch")
+    part, x_parts = lax.optimization_barrier((part, x_parts))
+    feature_grad, x_grad = summed(part, "ch", exchanged(x_parts).reshape(channels, block_len))
     return (x_grad, filter_grad, feature_grad)
 
 

time: 68.7 us -> 64.3 us (0.936)
  blocking collectives: 25.6 us -> 17.1 us
  local copies, waits for them, and re-layouts: 4.98 us -> 0.85 us
  starting transfers between devices: 15.5 us -> 19 us
  Pallas kernels: 8.91 us -> 11.5 us
  waiting for transfers between devices: 11.7 us -> 14.1 us
    all_to_all x2 -> x1, blocking collectives: 25.6 us -> 17.1 us  [exchanged(): return lax.all_to_all(values, 'ctx', 0, 0, tiled=True)]
    unnamed x16 -> x8, local copies, waits for them, and re-layouts: 4.15 us -> 0.03 us
    all_to_all x1 -> x2, starting transfers between devices: 3.53 us -> 7.32 us  [exchanged(): return lax.all_to_all(values, 'ctx', 0, 0, tiled=True)]
    pallas_call x1, Pallas kernels: 0.45 us -> 2.38 us  [shards(): call(lambda *refs: pack_kernel(groups, taps, *refs), (shape((groups, 144,...]
    all_to_all x1 -> x2, waiting for transfers between devices: 0.84 us -> 2.73 us  [exchanged(): return lax.all_to_all(values, 'ctx', 0, 0, tiled=True)]
  transfers between devices with their start and end apart: 6 -> 7, of which waited for: 4 -> 6; matrix products, arithmetic and copies ran while one was open for 1% -> 1% of each run, Pallas kernels for 6% -> 7%
where the time goes in v1:
time: 64.3 us; the launch traced here: 63.9 us
  starting transfers between devices  19 us (30%)
  blocking collectives  17.1 us (27%)
  waiting for transfers between devices  14.1 us (22%)
  Pallas kernels  11.5 us (18%)
  local copies, waits for them, and re-layouts  0.85 us (1%)
  between operations  0.71 us (1%)
  other arithmetic  0.67 us (1%)
    all_to_all x1, blocking collectives, exchanged(): return lax.all_to_all(values, 'ctx', 0, 0, tiled=True)  17.1 us
    ppermute x4, starting transfers between devices, shifted(): return lax.ppermute(values, axis, route)  8.92 us
    ppermute x4, waiting for transfers between devices, shifted(): return lax.ppermute(values, axis, route)  8.33 us
    all_to_all x2, starting transfers between devices, exchanged(): return lax.all_to_all(values, 'ctx', 0, 0, tiled=True)  7.32 us
    pallas_call x1, Pallas kernels, shards(): call(inputs_kernel, shape((groups, per * subs, SUB), BF16), [(groups * 16...  4.24 us
    pallas_call x1, Pallas kernels, shards(): call(taps_kernel, (shape((per, 4, blocks + lags, LANES), F32), shape((gro...  4.2 us
    ppermute x1, waiting for transfers between devices, summed(): lax.ppermute(values, axis, [(i, (i + half) % size) for i in range(size)])  3.04 us
    ppermute x1, starting transfers between devices, summed(): lax.ppermute(values, axis, [(i, (i + half) % size) for i in range(size)])  2.73 us
  transfers between devices with their start and end apart: 7, of which 6 were waited for; matrix products, arithmetic and copies ran while one was open for 1% of the time, Pallas kernels for 7%

profile of v1, /device:TPU:32, one launch (start us, length us, event | category | flops | bytes accessed | tf_op | source)
XLA Modules:
  0.0 63.9 jit_solution(13783702078038676135)
XLA Ops:
  0.6 0.0 copy-start.2
  0.6 0.0 copy-start.3
  0.7 2.4 %shard_map.94 = (bf16[16,144,128]{2,1,0:T(8,128)(2,1)}, f32[64,256]{1,0:T(8,128)}) custom-call(f32[64,256]{1,0:T(8,128)} %refs_0_.1, f32[64,64]{1,0:T(8,128)} %proj_ref.1, f32[1,64]{1,0:T(1,128)} %bitcast.1, bf16[64,2048]{1,0:T(8,128)(2,1)} %refs_3_.1, bf16[64,2048]{1,0:T(8,128)(2,1)} %refs_4_.1), custom_call_target="tpu_custom_call" | custom-call | flops 4194304 | bytes 1048576 | tf_op jit(solution)/shard_map/pallas_call | solution.py:282
  3.0 17.1 %all_to_all.15.recv_ref = bf16[16,144,128]{2,1,0:T(8,128)(2,1)S(1)} all-to-all(bf16[16,144,128]{2,1,0:T(8,128)(2,1)} %get-tuple-element.16), channel_id=1, replica_groups=mesh['ctx'=16,'ch'=16] {'ctx'}, dimensions={0} | all-to-all | bytes 1179648 | tf_op jit(solution)/shard_map/all_to_all | solution.py:280
  20.1 4.2 %shard_map.95 = (f32[4,4,144,128]{3,2,1,0:T(8,128)S(1)}, f32[16,8,128]{2,1,0:T(8,128)}) custom-call(bf16[16,144,128]{2,1,0:T(8,128)(2,1)S(1)} %all_to_all.15.recv_ref, bf16[2,256,512]{2,1,0:T(8,128)(2,1)S(1)} %copy-done.3, bf16[2,512,256]{2,1,0:T(8,128)(2,1)S(1)} %copy-done.2), custom_call_target="tpu_custom_call" | custom-call | flops 4294967296 | bytes 1048576 | tf_op jit(solution)/shard_map/pallas_call | solution.py:292
  24.4 3.5 %all-to-all-start.1 = ((f32[16,8,128]{2,1,0:T(8,128)}), f32[16,8,128]{2,1,0:T(8,128)S(1)}, u32[]{:S(2)}, u32[]{:S(2)}) async-start(f32[16,8,128]{2,1,0:T(8,128)} %get-tuple-element.17), calls=%async_computation.1 | async-start | bytes 131072 | tf_op jit(solution)/shard_map/all_to_all | solution.py:280
  27.9 0.0 copy-start
  27.9 0.0 copy-start.1
  27.9 4.2 %shard_map.96 = bf16[16,32,256]{2,1,0:T(8,128)(2,1)} custom-call(bf16[16,144,128]{2,1,0:T(8,128)(2,1)S(1)} %all_to_all.15.recv_ref, f32[4,4,144,128]{3,2,1,0:T(8,128)S(1)} %get-tuple-element.18.win_ref, bf16[2,256,512]{2,1,0:T(8,128)(2,1)S(1)} %copy-done.3, bf16[2,512,256]{2,1,0:T(8,128)(2,1)S(1)} %copy-done.2), custom_call_target="tpu_custom_call" | custom-call | flops 4294967296 | bytes 1048576 | tf_op jit(solution)/shard_map/pallas_call | solution.py:299
  32.1 1.8 %all-to-all-done.1.grad_ref = f32[16,8,128]{2,1,0:T(8,128)S(1)} async-done(((f32[16,8,128]{2,1,0:T(8,128)}), f32[16,8,128]{2,1,0:T(8,128)S(1)}, u32[]{:S(2)}, u32[]{:S(2)}) %all-to-all-start.1) | async-done | bytes 65568 | tf_op jit(solution)/shard_map/all_to_all | solution.py:280
  34.0 0.7 %shard_map.97 = (f32[64,256]{1,0:T(8,128)}, f32[64,256]{1,0:T(8,128)S(1)}) custom-call(f32[16,8,128]{2,1,0:T(8,128)S(1)} %all-to-all-done.1.grad_ref, f32[64,256]{1,0:T(8,128)S(1)} %copy-done.1, f32[64,64]{1,0:T(8,128)S(1)} %copy-done), custom_call_target="tpu_custom_call" | custom-call | flops 4194304 | bytes 1048576 | tf_op jit(solution)/shard_map/pallas_call | solution.py:306
  34.6 2.7 %collective-permute-start = (f32[64,256]{1,0:T(8,128)S(1)}, f32[64,256]{1,0:T(8,128)S(1)}, u32[]{:S(2)}, u32[]{:S(2)}) collective-permute-start(f32[64,256]{1,0:T(8,128)S(1)} %get-tuple-element.23), channel_id=1, source_target_pairs={{0,8},{1,9},{2,10},{3,11},{4,12},{5,13},{6,14},{7,15},{8,0},{9,1},... | collective-permute-start | bytes 196616 | tf_op jit(solution)/shard_map/ppermute | solution.py:258
  37.4 3.0 %collective-permute-done = f32[64,256]{1,0:T(8,128)S(1)} collective-permute-done((f32[64,256]{1,0:T(8,128)S(1)}, f32[64,256]{1,0:T(8,128)S(1)}, u32[]{:S(2)}, u32[]{:S(2)}) %collective-permute-start) | collective-permute-done | bytes 65568 | tf_op jit(solution)/shard_map/ppermute | solution.py:258
  40.4 2.0 %collective-permute-start.2 = (f32[64,256]{1,0:T(8,128)S(1)}, f32[64,256]{1,0:T(8,128)S(1)}, u32[]{:S(2)}, u32[]{:S(2)}) collective-permute-start(f32[64,256]{1,0:T(8,128)S(1)} %add.15), channel_id=1, source_target_pairs={{0,1},{1,2},{2,3},{3,4},{4,5},{5,6},{6,7},{7,0},{8,9},{9,10},{10,1... | collective-permute-start | bytes 196616 | tf_op jit(solution)/shard_map/ppermute | solution.py:252
  42.4 0.1 collective-permute-start.1
  42.5 3.8 %all-to-all-start.2 = ((bf16[16,32,256]{2,1,0:T(8,128)(2,1)}), bf16[16,32,256]{2,1,0:T(8,128)(2,1)S(1)}, u32[]{:S(2)}, u32[]{:S(2)}) async-start(bf16[16,32,256]{2,1,0:T(8,128)(2,1)} %shard_map.96), calls=%async_computation.2 | async-start | bytes 524288 | tf_op jit(solution)/shard_map/all_to_all | solution.py:280
  46.4 0.0 collective-permute-done.2
  46.4 0.3 collective-permute-done.1
  46.7 6.8 %collective-permute-start.4 = (f32[64,256]{1,0:T(8,128)S(1)}, f32[64,256]{1,0:T(8,128)S(1)}, u32[]{:S(2)}, u32[]{:S(2)}) collective-permute-start(f32[64,256]{1,0:T(8,128)S(1)} %get-tuple-element.30), channel_id=1, source_target_pairs={{0,3},{1,4},{2,5},{3,6},{4,7},{5,0},{6,1},{7,2},{8,11},{9,12},{10,... | collective-permute-start | bytes 196616 | tf_op jit(solution)/shard_map/ppermute | solution.py:252
  53.5 0.9 %all-to-all-done.2 = bf16[16,32,256]{2,1,0:T(8,128)(2,1)S(1)} async-done(((bf16[16,32,256]{2,1,0:T(8,128)(2,1)}), bf16[16,32,256]{2,1,0:T(8,128)(2,1)S(1)}, u32[]{:S(2)}, u32[]{:S(2)}) %all-to-all-start.2) | async-done | bytes 262176 | tf_op jit(solution)/shard_map/all_to_all | solution.py:280
  54.4 0.8 %reshape.13 = bf16[64,2048]{1,0:T(8,128)(2,1)} reshape(bf16[16,32,256]{2,1,0:T(8,128)(2,1)S(1)} %all-to-all-done.2) | data formatting | bytes 524288 | tf_op jit(solution)/shard_map/reshape | solution.py:313
  55.2 2.4 %collective-permute-done.4 = f32[64,256]{1,0:T(8,128)S(1)} collective-permute-done((f32[64,256]{1,0:T(8,128)S(1)}, f32[64,256]{1,0:T(8,128)S(1)}, u32[]{:S(2)}, u32[]{:S(2)}) %collective-permute-start.4) | collective-permute-done | bytes 65568 | tf_op jit(solution)/shard_map/ppermute | solution.py:252
  57.6 5.6 %collective-permute-done.3 = f32[64,256]{1,0:T(8,128)S(1)} collective-permute-done((f32[64,256]{1,0:T(8,128)S(1)}, f32[64,256]{1,0:T(8,128)S(1)}, u32[]{:S(2)}, u32[]{:S(2)}) %collective-permute-start.3) | collective-permute-done | bytes 65568 | tf_op jit(solution)/shard_map/ppermute | solution.py:252
  63.2 0.6 %add_add_fusion = f32[64,256]{1,0:T(8,128)} fusion(f32[64,256]{1,0:T(8,128)S(1)} %collective-permute-done.4, f32[64,256]{1,0:T(8,128)S(1)} %get-tuple-element.29, f32[64,256]{1,0:T(8,128)S(1)} %collective-permute-done.3), kind=kLoop, calls=%fused_computation | loop fusion | flops 32768 | bytes 262144 | tf_op jit(solution)/shard_map/add | solution.py:265
  (7 shorter events, 0.0 us)
Async XLA Ops:
  0.6 19.5 %copy-start.2 = (bf16[2,512,256]{2,1,0:T(8,128)(2,1)S(1)}, bf16[2,512,256]{2,1,0:T(8,128)(2,1)}, u32[]{:S(2)}) copy-start(bf16[2,512,256]{2,1,0:T(8,128)(2,1)} %constant.5.clone.inv_ref) | copy-start | bytes 1572868
  0.6 19.5 %copy-start.3 = (bf16[2,256,512]{2,1,0:T(8,128)(2,1)S(1)}, bf16[2,256,512]{2,1,0:T(8,128)(2,1)}, u32[]{:S(2)}) copy-start(bf16[2,256,512]{2,1,0:T(8,128)(2,1)} %constant.4.clone.fwd_ref) | copy-start | bytes 1572868
  24.4 9.6 %all-to-all-start.1 = ((f32[16,8,128]{2,1,0:T(8,128)}), f32[16,8,128]{2,1,0:T(8,128)S(1)}, u32[]{:S(2)}, u32[]{:S(2)}) async-start(f32[16,8,128]{2,1,0:T(8,128)} %get-tuple-element.17), calls=%async_computation.1 | async-start | bytes 131072 | tf_op jit(solution)/shard_map/all_to_all | solution.py:280
  27.9 6.1 %copy-start = (f32[64,64]{1,0:T(8,128)S(1)}, f32[64,64]{1,0:T(8,128)}, u32[]{:S(2)}) copy-start(f32[64,64]{1,0:T(8,128)} %proj_ref.1) | copy-start | bytes 49156
  27.9 6.1 %copy-start.1 = (f32[64,256]{1,0:T(8,128)S(1)}, f32[64,256]{1,0:T(8,128)}, u32[]{:S(2)}) copy-start(f32[64,256]{1,0:T(8,128)} %get-tuple-element.20.decay_ref) | copy-start | bytes 196612
  34.6 5.8 %collective-permute-start = (f32[64,256]{1,0:T(8,128)S(1)}, f32[64,256]{1,0:T(8,128)S(1)}, u32[]{:S(2)}, u32[]{:S(2)}) collective-permute-start(f32[64,256]{1,0:T(8,128)S(1)} %get-tuple-element.23), channel_id=1, source_target_pairs={{0,8},{1,9},{2,10},{3,11},{4,12},{5,13},{6,14},{7,15},{8,0},{9,1},... | collective-permute-start | bytes 196616 | tf_op jit(solution)/shard_map/ppermute | solution.py:258
  40.4 5.9 %collective-permute-start.2 = (f32[64,256]{1,0:T(8,128)S(1)}, f32[64,256]{1,0:T(8,128)S(1)}, u32[]{:S(2)}, u32[]{:S(2)}) collective-permute-start(f32[64,256]{1,0:T(8,128)S(1)} %add.15), channel_id=1, source_target_pairs={{0,1},{1,2},{2,3},{3,4},{4,5},{5,6},{6,7},{7,0},{8,9},{9,10},{10,1... | collective-permute-start | bytes 196616 | tf_op jit(solution)/shard_map/ppermute | solution.py:252
  42.4 4.3 %collective-permute-start.1 = (f32[64,256]{1,0:T(8,128)S(1)}, f32[64,256]{1,0:T(8,128)S(1)}, u32[]{:S(2)}, u32[]{:S(2)}) collective-permute-start(f32[64,256]{1,0:T(8,128)S(1)} %add.15), channel_id=1, source_target_pairs={{0,7},{1,0},{2,1},{3,2},{4,3},{5,4},{6,5},{7,6},{8,15},{9,8},{10,9... | collective-permute-start | bytes 196616 | tf_op jit(solution)/shard_map/ppermute | solution.py:252
  42.5 11.9 %all-to-all-start.2 = ((bf16[16,32,256]{2,1,0:T(8,128)(2,1)}), bf16[16,32,256]{2,1,0:T(8,128)(2,1)S(1)}, u32[]{:S(2)}, u32[]{:S(2)}) async-start(bf16[16,32,256]{2,1,0:T(8,128)(2,1)} %shard_map.96), calls=%async_computation.2 | async-start | bytes 524288 | tf_op jit(solution)/shard_map/all_to_all | solution.py:280
  46.7 10.9 %collective-permute-start.4 = (f32[64,256]{1,0:T(8,128)S(1)}, f32[64,256]{1,0:T(8,128)S(1)}, u32[]{:S(2)}, u32[]{:S(2)}) collective-permute-start(f32[64,256]{1,0:T(8,128)S(1)} %get-tuple-element.30), channel_id=1, source_target_pairs={{0,3},{1,4},{2,5},{3,6},{4,7},{5,0},{6,1},{7,2},{8,11},{9,12},{10,... | collective-permute-start | bytes 196616 | tf_op jit(solution)/shard_map/ppermute | solution.py:252
  53.5 9.7 %collective-permute-start.3 = (f32[64,256]{1,0:T(8,128)S(1)}, f32[64,256]{1,0:T(8,128)S(1)}, u32[]{:S(2)}, u32[]{:S(2)}) collective-permute-start(f32[64,256]{1,0:T(8,128)S(1)} %get-tuple-element.29), channel_id=1, source_target_pairs={{0,5},{1,6},{2,7},{3,0},{4,1},{5,2},{6,3},{7,4},{8,13},{9,14},{10,... | collective-permute-start | bytes 196616 | tf_op jit(solution)/shard_map/ppermute | solution.py:252

commit v2 on v1

--- a/solution.py
+++ b/solution.py
@@ -6,6 +6,7 @@
 from jax import lax
 from jax.experimental import pallas as pl
 from jax.experimental.pallas import tpu as pltpu
+from jax.sharding import Mesh
 from jax.sharding import PartitionSpec as P
 
 SUB = 256
@@ -41,8 +42,18 @@
     return dot(high, table[0]) + dot(high, table[1]) + dot(low, table[0])
 
 
+def decay_of(rates, tap_rows, taps):
+    channels = rates.shape[1]
+    first = lax.axis_index("ctx") * tap_rows
+    positions = (first + lax.broadcasted_iota(jnp.int32, (1, tap_rows), 1)).astype(F32)
+    across = lax.broadcasted_iota(jnp.int32, (channels, channels), 1)
+    diagonal = lax.broadcasted_iota(jnp.int32, (channels, channels), 0) == across
+    column = jnp.sum(jnp.where(diagonal, rates, 0.0), axis=1, keepdims=True)
+    return jnp.exp(-column * (positions / taps))
+
+
 def pack_kernel(groups, taps, *refs):
-    sources, (pay_ref, decay_ref, rows, frows), held, sems = refs[:5], refs[5:9], refs[9:14], refs[14]
+    sources, (pay_ref, both_ref, rows, frows), held, sems = refs[:5], refs[5:9], refs[9:14], refs[14]
     copies = [pltpu.make_async_copy(src, dst, sems.at[i]) for i, (src, dst) in enumerate(zip(sources, held))]
     for copy in copies:
         copy.start()
@@ -53,15 +64,10 @@
     per = channels // groups
     subs = block_len // SUB
     span = per * subs
-    tap_rows = feat_ref.shape[1]
-    first = lax.axis_index("ctx") * tap_rows
-    positions = (first + lax.broadcasted_iota(jnp.int32, (1, tap_rows), 1)).astype(F32)
-    diagonal = lax.broadcasted_iota(jnp.int32, (channels, channels), 0) == lax.broadcasted_iota(
-        jnp.int32, (channels, channels), 1
-    )
-    rates = jnp.sum(jnp.where(diagonal, rate_ref[...], 0.0), axis=1, keepdims=True)
-    decay = jnp.exp(-rates * (positions / taps))
-    decay_ref[...] = decay
+    decay = decay_of(rate_ref[...], feat_ref.shape[1], taps)
+    order = proj_ref.shape[0]
+    both_ref[0:order, :] = proj_ref[...]
+    both_ref[order:, :] = jnp.broadcast_to(rate_ref[...], (8, channels))
     product = lax.dot_general(
         proj_ref[...],
         feat_ref[...],
@@ -163,8 +169,9 @@
     result = dot_terms(left, inv_ref)
     for lag in range(lags):
         own = slice(lag * per, (lag + 1) * per)
-        grad_ref[lag, 0:per, :] = result[own, 0:LANES]
-        grad_ref[lag, per : 2 * per, :] = result[own, LANES:]
+        for copy in range(2):
+            grad_ref[2 * lag + copy, 0:per, :] = result[own, 0:LANES]
+            grad_ref[2 * lag + copy, per : 2 * per, :] = result[own, LANES:]
 
 
 def inputs_kernel(recv_ref, win_ref, fwd_ref, inv_ref, grad_ref, frows, fspec, spec):
@@ -214,19 +221,25 @@
         grad_ref[:, first * subs : (first + 2) * subs, :] = both.astype(BF16)
 
 
-def features_kernel(grad_ref, decay_ref, proj_ref, out_ref, part_ref):
-    groups = grad_ref.shape[0]
+def features_kernel(taps, grad_ref, mine_ref, other_ref, out_ref, part_ref, held):
+    groups = grad_ref.shape[0] // 2
     per = grad_ref.shape[1] // 2
+    channels, tap_rows = out_ref.shape
+    order = mine_ref.shape[0] - 8
+    me = lax.axis_index("x_hi")
     for group in range(groups):
         own = slice(group * per, (group + 1) * per)
-        out_ref[own, 0:LANES] = grad_ref[group, 0:per, :]
-        out_ref[own, LANES:] = grad_ref[group, per : 2 * per, :]
-    part_ref[...] = jnp.dot(
-        proj_ref[...],
-        decay_ref[...] * out_ref[...],
-        precision=lax.Precision.HIGHEST,
-        preferred_element_type=F32,
-    )
+        for ref, source in ((out_ref, 2 * group + me), (held, 2 * group + 1 - me)):
+            ref[own, 0:LANES] = grad_ref[source, 0:per, :]
+            ref[own, LANES:] = grad_ref[source, per : 2 * per, :]
+    total = None
+    for both, grads in ((mine_ref, out_ref), (other_ref, held)):
+        decay = decay_of(both[order : order + 1, :], tap_rows, taps)
+        left_high, left_low = two_terms(both[0:order, :])
+        high, low = two_terms(decay * grads[...])
+        term = dot(left_high, high) + dot(left_high, low) + dot(left_low, high)
+        total = term if total is None else total + term
+    part_ref[...] = total
 
 
 def call(kernel, out, scratch, flops, fetched=(), limit=VMEM_LIMIT):
@@ -246,23 +259,19 @@
     )
 
 
-def shifted(values, axis, distance, ring):
+def shifted(values, axis, distance):
     size = lax.axis_size(axis)
-    route = [(i, i - i % ring + (i + distance) % ring) for i in range(size)]
-    return lax.ppermute(values, axis, route)
-
-
-def summed(values, axis, other):
-    size = lax.axis_size(axis)
-    half = size // 2
-    values = values + lax.ppermute(values, axis, [(i, (i + half) % size) for i in range(size)])
-    below = shifted(values, axis, 1, half)
-    above = shifted(values, axis, -1, half)
+    return lax.ppermute(values, axis, [(i, (i + distance) % size) for i in range(size)])
+
+
+def summed(values, axis, beside):
+    below = shifted(values, axis, 1)
+    above = shifted(values, axis, -1)
     two = values + above
     three = two + below
-    far = (shifted(three, axis, -3, half), shifted(two, axis, 3, half))
-    far, other = lax.optimization_barrier((far, other))
-    return three + far[0] + far[1], other
+    far = (shifted(three, axis, -3), shifted(two, axis, 3))
+    far, beside = lax.optimization_barrier((far, beside))
+    return three + far[0] + far[1], beside
 
 
 def shards(inputs, cotangent, features, projection, decay_rates):
@@ -276,26 +285,28 @@
     shape = jax.ShapeDtypeStruct
     forward, backward = dft_tables()
 
-    def exchanged(values):
-        return lax.all_to_all(values, "ctx", 0, 0, tiled=True)
-
-    payload, decay = call(
+    def exchanged(values, axes):
+        return lax.all_to_all(values, axes, 0, 0, tiled=True)
+
+    order = projection.shape[0]
+    payload, both = call(
         lambda *refs: pack_kernel(groups, taps, *refs),
-        (shape((groups, 144, LANES), BF16), shape((channels, tap_rows), F32)),
+        (shape((groups, 144, LANES), BF16), shape((order + 8, channels), F32)),
         [(4, channels * subs, LANES), (groups, 16, LANES)],
         1 << 22,
         (features, projection, decay_rates.reshape(1, channels), cotangent, inputs),
         60 * 1024 * 1024,
     )(features, projection, decay_rates.reshape(1, channels), cotangent, inputs)
-    received = exchanged(payload)
+    other = lax.ppermute(both, "x_hi", [(0, 1), (1, 0)])
+    received, other = lax.optimization_barrier((exchanged(payload, "ctx"), other))
     blocks = groups * subs
     windows, tap_grads = call(
         taps_kernel,
-        (shape((per, 4, blocks + lags, LANES), F32), shape((groups, 2 * per, LANES), F32)),
+        (shape((per, 4, blocks + lags, LANES), F32), shape((2 * groups, 2 * per, LANES), F32)),
         [(per, 4, blocks + subs, LANES), (per, 4, blocks, LANES), (2, lags * subs, LANES), (4, per * lags, LANES)],
         1 << 32,
     )(received, forward, backward)
-    tap_grads = exchanged(tap_grads)
+    tap_grads = exchanged(tap_grads, ("ctx", "x_hi"))
     x_parts = call(
         inputs_kernel,
         shape((groups, per * subs, SUB), BF16),
@@ -304,22 +315,26 @@
     )(received, windows, forward, backward)
     tap_grads, x_parts = lax.optimization_barrier((tap_grads, x_parts))
     filter_grad, part = call(
-        features_kernel,
-        (shape((channels, tap_rows), F32), shape((projection.shape[0], tap_rows), F32)),
-        [],
+        lambda *refs: features_kernel(taps, *refs),
+        (shape((channels, tap_rows), F32), shape((order, tap_rows), F32)),
+        [(channels, tap_rows)],
         1 << 22,
-    )(tap_grads, decay, projection)
+    )(tap_grads, both, other)
     part, x_parts = lax.optimization_barrier((part, x_parts))
-    feature_grad, x_grad = summed(part, "ch", exchanged(x_parts).reshape(channels, block_len))
+    x_grad = exchanged(x_parts, "ctx").reshape(channels, block_len)
+    feature_grad, x_grad = summed(part, "z", x_grad)
     return (x_grad, filter_grad, feature_grad)
 
 
 def solution(mesh):
-    placed = (P("ch", "ctx"), P("ch", "ctx"), P(None, "ctx"), P(None, "ch"), P("ch"))
+    whole = mesh.shape["ch"]
+    mesh = Mesh(mesh.devices.reshape(mesh.shape["ctx"], 2, whole // 2), ("ctx", "x_hi", "z"))
+    split = ("x_hi", "z")
+    placed = (P(split, "ctx"), P(split, "ctx"), P(None, "ctx"), P(None, split), P(split))
     return jax.shard_map(
         shards,
         mesh=mesh,
         in_specs=placed,
-        out_specs=(P("ch", "ctx"), P("ch", "ctx"), P(None, "ctx")),
+        out_specs=(P(split, "ctx"), P(split, "ctx"), P(None, "ctx")),
         check_vma=False,
     )

time: 64.3 us -> 62 us (0.964)
  blocking collectives: 17.1 us -> 0 us
  waiting for transfers between devices: 14.1 us -> 22.1 us
  starting transfers between devices: 19 us -> 25.4 us
    all_to_all x1 -> x0, blocking collectives: 17.1 us -> none  [exchanged(): return lax.all_to_all(values, 'ctx', 0, 0, tiled=True)]
    all_to_all x2 -> x3, starting transfers between devices: 7.32 us -> 14 us  [exchanged(): return lax.all_to_all(values, axes, 0, 0, tiled=True)]
    ppermute x5, waiting for transfers between devices: 11.4 us -> 17 us  [the longest x1 8.56 us: shards(): other = lax.ppermute(both, 'x_hi', [(0, 1), (1, 0)])]
    all_to_all x2 -> x3, waiting for transfers between devices: 2.73 us -> 5.15 us  [exchanged(): return lax.all_to_all(values, axes, 0, 0, tiled=True)]
  transfers between devices with their start and end apart: 7 -> 8, of which waited for: 6 -> 7; matrix products, arithmetic and copies ran while one was open for 1% -> 1% of each run, Pallas kernels for 7% -> 7%
where the time goes in v2:
time: 62 us; the launch traced here: 61.4 us
  starting transfers between devices  25.4 us (41%)
  waiting for transfers between devices  22.1 us (36%)
  Pallas kernels  11.7 us (19%)
  local copies, waits for them, and re-layouts  0.85 us (1%)
  between operations  0.72 us (1%)
  other arithmetic  0.66 us (1%)
    all_to_all x3, starting transfers between devices, exchanged(): return lax.all_to_all(values, axes, 0, 0, tiled=True)  14 us
    ppermute x1, waiting for transfers between devices, shards(): other = lax.ppermute(both, 'x_hi', [(0, 1), (1, 0)])  8.56 us
    ppermute x4, starting transfers between devices, shifted(): lax.ppermute(values, axis, [(i, (i + distance) % size) for i in range(siz...  8.56 us
    ppermute x4, waiting for transfers between devices, shifted(): lax.ppermute(values, axis, [(i, (i + distance) % size) for i in range(siz...  8.42 us
    all_to_all x3, waiting for transfers between devices, exchanged(): return lax.all_to_all(values, axes, 0, 0, tiled=True)  5.15 us
    pallas_call x1, Pallas kernels, shards(): call(taps_kernel, (shape((per, 4, blocks + lags, LANES), F32), shape((2 *...  4.28 us
    pallas_call x1, Pallas kernels, shards(): call(inputs_kernel, shape((groups, per * subs, SUB), BF16), [(groups * 16...  4.24 us
    ppermute x1, starting transfers between devices, shards(): other = lax.ppermute(both, 'x_hi', [(0, 1), (1, 0)])  2.82 us
  transfers between devices with their start and end apart: 8, of which 7 were waited for; matrix products, arithmetic and copies ran while one was open for 1% of the time, Pallas kernels for 7%

profile of v2, /device:TPU:32, one launch (start us, length us, event | category | flops | bytes accessed | tf_op | source)
XLA Modules:
  0.0 61.4 jit_solution(14820494707288930866)
XLA Ops:
  0.6 0.0 copy-start.1
  0.6 0.0 copy-start.2
  0.7 2.4 %shard_map.94 = (bf16[16,144,128]{2,1,0:T(8,128)(2,1)}, f32[72,64]{1,0:T(8,128)}) custom-call(f32[64,256]{1,0:T(8,128)} %refs_0_.1, f32[64,64]{1,0:T(8,128)} %refs_1_.1, f32[1,64]{1,0:T(1,128)} %bitcast.1, bf16[64,2048]{1,0:T(8,128)(2,1)} %refs_3_.1, bf16[64,2048]{1,0:T(8,128)(2,1)} %refs_4_.1), custom_call_target="tpu_custom_call" | custom-call | flops 4194304 | bytes 1048576 | tf_op jit(solution)/shard_map/pallas_call | solution.py:292
  3.1 0.0 copy-start
  3.1 5.5 %all-to-all-start = ((bf16[16,144,128]{2,1,0:T(8,128)(2,1)}), bf16[16,144,128]{2,1,0:T(8,128)(2,1)S(1)}, u32[]{:S(2)}, u32[]{:S(2)}) async-start(bf16[16,144,128]{2,1,0:T(8,128)(2,1)} %get-tuple-element.18), calls=%async_computation | async-start | bytes 1179648 | tf_op jit(solution)/shard_map/all_to_all | solution.py:289
  8.6 2.8 %collective-permute-start = (f32[72,64]{1,0:T(8,128)S(1)}, f32[72,64]{1,0:T(8,128)S(1)}, u32[]{:S(2)}, u32[]{:S(2)}) collective-permute-start(f32[72,64]{1,0:T(8,128)S(1)} %copy-done), channel_id=1, source_target_pairs={{0,8},{8,0},{1,9},{9,1},{2,10},{10,2},{3,11},{11,3},{4,12},{12,4},... | collective-permute-start | bytes 55304 | tf_op jit(solution)/shard_map/ppermute | solution.py:300
  11.4 8.6 %collective-permute-done.refs_2_ = f32[72,64]{1,0:T(8,128)S(1)} collective-permute-done((f32[72,64]{1,0:T(8,128)S(1)}, f32[72,64]{1,0:T(8,128)S(1)}, u32[]{:S(2)}, u32[]{:S(2)}) %collective-permute-start) | collective-permute-done | bytes 18464 | tf_op jit(solution)/shard_map/ppermute | solution.py:300
  20.0 0.6 all-to-all-done.recv_ref
  20.6 4.3 %shard_map.95 = (f32[4,4,144,128]{3,2,1,0:T(8,128)S(1)}, f32[32,8,128]{2,1,0:T(8,128)}) custom-call(bf16[16,144,128]{2,1,0:T(8,128)(2,1)S(1)} %all-to-all-done.recv_ref, bf16[2,256,512]{2,1,0:T(8,128)(2,1)S(1)} %copy-done.2, bf16[2,512,256]{2,1,0:T(8,128)(2,1)S(1)} %copy-done.1), custom_call_target="tpu_custom_call" | custom-call | flops 4294967296 | bytes 1048576 | tf_op jit(solution)/shard_map/pallas_call | solution.py:303
  24.9 5.0 %all-to-all-start.1 = ((f32[32,8,128]{2,1,0:T(8,128)}), f32[32,8,128]{2,1,0:T(8,128)S(1)}, u32[]{:S(2)}, u32[]{:S(2)}) async-start(f32[32,8,128]{2,1,0:T(8,128)} %get-tuple-element.21), calls=%async_computation.1 | async-start | bytes 262144 | tf_op jit(solution)/shard_map/all_to_all | solution.py:289
  29.9 4.2 %shard_map.96 = bf16[16,32,256]{2,1,0:T(8,128)(2,1)} custom-call(bf16[16,144,128]{2,1,0:T(8,128)(2,1)S(1)} %all-to-all-done.recv_ref, f32[4,4,144,128]{3,2,1,0:T(8,128)S(1)} %get-tuple-element.22.win_ref, bf16[2,256,512]{2,1,0:T(8,128)(2,1)S(1)} %copy-done.2, bf16[2,512,256]{2,1,0:T(8,128)(2,1)S(1)} %copy-done.1), custom_call_target="tpu_custom_call" | custom-call | flops 4294967296 | bytes 1048576 | tf_op jit(solution)/shard_map/pallas_call | solution.py:310
  34.1 3.7 %all-to-all-done.1.refs_0_ = f32[32,8,128]{2,1,0:T(8,128)S(1)} async-done(((f32[32,8,128]{2,1,0:T(8,128)}), f32[32,8,128]{2,1,0:T(8,128)S(1)}, u32[]{:S(2)}, u32[]{:S(2)}) %all-to-all-start.1) | async-done | bytes 131104 | tf_op jit(solution)/shard_map/all_to_all | solution.py:289
  37.8 0.8 %shard_map.97 = (f32[64,256]{1,0:T(8,128)}, f32[64,256]{1,0:T(8,128)S(1)}) custom-call(f32[32,8,128]{2,1,0:T(8,128)S(1)} %all-to-all-done.1.refs_0_, f32[72,64]{1,0:T(8,128)S(1)} %copy-done, f32[72,64]{1,0:T(8,128)S(1)} %collective-permute-done.refs_2_), custom_call_target="tpu_custom_call" | custom-call | flops 4194304 | bytes 1048576 | tf_op jit(solution)/shard_map/pallas_call | solution.py:317
  38.6 1.9 %collective-permute-start.2 = (f32[64,256]{1,0:T(8,128)S(1)}, f32[64,256]{1,0:T(8,128)S(1)}, u32[]{:S(2)}, u32[]{:S(2)}) collective-permute-start(f32[64,256]{1,0:T(8,128)S(1)} %get-tuple-element.27), channel_id=1, source_target_pairs={{0,1},{1,2},{2,3},{3,4},{4,5},{5,6},{6,7},{7,0},{8,9},{9,10},{10,1... | collective-permute-start | bytes 196616 | tf_op jit(solution)/shard_map/ppermute | solution.py:264
  40.5 0.1 collective-permute-start.1
  40.6 3.5 %all-to-all-start.2 = ((bf16[16,32,256]{2,1,0:T(8,128)(2,1)}), bf16[16,32,256]{2,1,0:T(8,128)(2,1)S(1)}, u32[]{:S(2)}, u32[]{:S(2)}) async-start(bf16[16,32,256]{2,1,0:T(8,128)(2,1)} %shard_map.96), calls=%async_computation.2 | async-start | bytes 524288 | tf_op jit(solution)/shard_map/all_to_all | solution.py:289
  44.1 0.6 collective-permute-done.1
  44.8 6.5 %collective-permute-start.4 = (f32[64,256]{1,0:T(8,128)S(1)}, f32[64,256]{1,0:T(8,128)S(1)}, u32[]{:S(2)}, u32[]{:S(2)}) collective-permute-start(f32[64,256]{1,0:T(8,128)S(1)} %get-tuple-element.34), channel_id=1, source_target_pairs={{0,3},{1,4},{2,5},{3,6},{4,7},{5,0},{6,1},{7,2},{8,11},{9,12},{10,... | collective-permute-start | bytes 196616 | tf_op jit(solution)/shard_map/ppermute | solution.py:264
  51.3 0.0 collective-permute-start.3
  51.3 0.8 %all-to-all-done.2 = bf16[16,32,256]{2,1,0:T(8,128)(2,1)S(1)} async-done(((bf16[16,32,256]{2,1,0:T(8,128)(2,1)}), bf16[16,32,256]{2,1,0:T(8,128)(2,1)S(1)}, u32[]{:S(2)}, u32[]{:S(2)}) %all-to-all-start.2) | async-done | bytes 262176 | tf_op jit(solution)/shard_map/all_to_all | solution.py:289
  52.1 0.8 %reshape.13 = bf16[64,2048]{1,0:T(8,128)(2,1)} reshape(bf16[16,32,256]{2,1,0:T(8,128)(2,1)S(1)} %all-to-all-done.2) | data formatting | bytes 524288 | tf_op jit(solution)/shard_map/reshape | solution.py:324
  53.0 2.4 %collective-permute-done.4 = f32[64,256]{1,0:T(8,128)S(1)} collective-permute-done((f32[64,256]{1,0:T(8,128)S(1)}, f32[64,256]{1,0:T(8,128)S(1)}, u32[]{:S(2)}, u32[]{:S(2)}) %collective-permute-start.4) | collective-permute-done | bytes 65568 | tf_op jit(solution)/shard_map/ppermute | solution.py:264
  55.4 5.4 %collective-permute-done.3 = f32[64,256]{1,0:T(8,128)S(1)} collective-permute-done((f32[64,256]{1,0:T(8,128)S(1)}, f32[64,256]{1,0:T(8,128)S(1)}, u32[]{:S(2)}, u32[]{:S(2)}) %collective-permute-start.3) | collective-permute-done | bytes 65568 | tf_op jit(solution)/shard_map/ppermute | solution.py:264
  60.8 0.6 %add_add_fusion = f32[64,256]{1,0:T(8,128)} fusion(f32[64,256]{1,0:T(8,128)S(1)} %collective-permute-done.4, f32[64,256]{1,0:T(8,128)S(1)} %get-tuple-element.33, f32[64,256]{1,0:T(8,128)S(1)} %collective-permute-done.3), kind=kLoop, calls=%fused_computation | loop fusion | flops 32768 | bytes 262144 | tf_op jit(solution)/shard_map/add | solution.py:274
  (5 shorter events, 0.0 us)
Async XLA Ops:
  0.6 20.0 %copy-start.1 = (bf16[2,512,256]{2,1,0:T(8,128)(2,1)S(1)}, bf16[2,512,256]{2,1,0:T(8,128)(2,1)}, u32[]{:S(2)}) copy-start(bf16[2,512,256]{2,1,0:T(8,128)(2,1)} %constant.5.clone.inv_ref) | copy-start | bytes 1572868
  0.6 19.9 %copy-start.2 = (bf16[2,256,512]{2,1,0:T(8,128)(2,1)S(1)}, bf16[2,256,512]{2,1,0:T(8,128)(2,1)}, u32[]{:S(2)}) copy-start(bf16[2,256,512]{2,1,0:T(8,128)(2,1)} %constant.4.clone.fwd_ref) | copy-start | bytes 1572868
  3.1 5.5 %copy-start = (f32[72,64]{1,0:T(8,128)S(1)}, f32[72,64]{1,0:T(8,128)}, u32[]{:S(2)}) copy-start(f32[72,64]{1,0:T(8,128)} %get-tuple-element.19.refs_1_) | copy-start | bytes 55300
  3.1 17.5 %all-to-all-start = ((bf16[16,144,128]{2,1,0:T(8,128)(2,1)}), bf16[16,144,128]{2,1,0:T(8,128)(2,1)S(1)}, u32[]{:S(2)}, u32[]{:S(2)}) async-start(bf16[16,144,128]{2,1,0:T(8,128)(2,1)} %get-tuple-element.18), calls=%async_computation | async-start | bytes 1179648 | tf_op jit(solution)/shard_map/all_to_all | solution.py:289
  8.6 11.4 %collective-permute-start = (f32[72,64]{1,0:T(8,128)S(1)}, f32[72,64]{1,0:T(8,128)S(1)}, u32[]{:S(2)}, u32[]{:S(2)}) collective-permute-start(f32[72,64]{1,0:T(8,128)S(1)} %copy-done), channel_id=1, source_target_pairs={{0,8},{8,0},{1,9},{9,1},{2,10},{10,2},{3,11},{11,3},{4,12},{12,4},... | collective-permute-start | bytes 55304 | tf_op jit(solution)/shard_map/ppermute | solution.py:300
  24.9 12.9 %all-to-all-start.1 = ((f32[32,8,128]{2,1,0:T(8,128)}), f32[32,8,128]{2,1,0:T(8,128)S(1)}, u32[]{:S(2)}, u32[]{:S(2)}) async-start(f32[32,8,128]{2,1,0:T(8,128)} %get-tuple-element.21), calls=%async_computation.1 | async-start | bytes 262144 | tf_op jit(solution)/shard_map/all_to_all | solution.py:289
  38.6 5.6 %collective-permute-start.2 = (f32[64,256]{1,0:T(8,128)S(1)}, f32[64,256]{1,0:T(8,128)S(1)}, u32[]{:S(2)}, u32[]{:S(2)}) collective-permute-start(f32[64,256]{1,0:T(8,128)S(1)} %get-tuple-element.27), channel_id=1, source_target_pairs={{0,1},{1,2},{2,3},{3,4},{4,5},{5,6},{6,7},{7,0},{8,9},{9,10},{10,1... | collective-permute-start | bytes 196616 | tf_op jit(solution)/shard_map/ppermute | solution.py:264
  40.5 4.3 %collective-permute-start.1 = (f32[64,256]{1,0:T(8,128)S(1)}, f32[64,256]{1,0:T(8,128)S(1)}, u32[]{:S(2)}, u32[]{:S(2)}) collective-permute-start(f32[64,256]{1,0:T(8,128)S(1)} %get-tuple-element.27), channel_id=1, source_target_pairs={{0,7},{1,0},{2,1},{3,2},{4,3},{5,4},{6,5},{7,6},{8,15},{9,8},{10,9... | collective-permute-start | bytes 196616 | tf_op jit(solution)/shard_map/ppermute | solution.py:264
  40.6 11.6 %all-to-all-start.2 = ((bf16[16,32,256]{2,1,0:T(8,128)(2,1)}), bf16[16,32,256]{2,1,0:T(8,128)(2,1)S(1)}, u32[]{:S(2)}, u32[]{:S(2)}) async-start(bf16[16,32,256]{2,1,0:T(8,128)(2,1)} %shard_map.96), calls=%async_computation.2 | async-start | bytes 524288 | tf_op jit(solution)/shard_map/all_to_all | solution.py:289
  44.8 10.6 %collective-permute-start.4 = (f32[64,256]{1,0:T(8,128)S(1)}, f32[64,256]{1,0:T(8,128)S(1)}, u32[]{:S(2)}, u32[]{:S(2)}) collective-permute-start(f32[64,256]{1,0:T(8,128)S(1)} %get-tuple-element.34), channel_id=1, source_target_pairs={{0,3},{1,4},{2,5},{3,6},{4,7},{5,0},{6,1},{7,2},{8,11},{9,12},{10,... | collective-permute-start | bytes 196616 | tf_op jit(solution)/shard_map/ppermute | solution.py:264
  51.3 9.5 %collective-permute-start.3 = (f32[64,256]{1,0:T(8,128)S(1)}, f32[64,256]{1,0:T(8,128)S(1)}, u32[]{:S(2)}, u32[]{:S(2)}) collective-permute-start(f32[64,256]{1,0:T(8,128)S(1)} %get-tuple-element.33), channel_id=1, source_target_pairs={{0,5},{1,6},{2,7},{3,0},{4,1},{5,2},{6,3},{7,4},{8,13},{9,14},{10,... | collective-permute-start | bytes 196616 | tf_op jit(solution)/shard_map/ppermute | solution.py:264

commit v3 on v2

--- a/solution.py
+++ b/solution.py
@@ -259,19 +259,23 @@
     )
 
 
-def shifted(values, axis, distance):
-    size = lax.axis_size(axis)
-    return lax.ppermute(values, axis, [(i, (i + distance) % size) for i in range(size)])
+def swapped(values, axis, mask):
+    return lax.ppermute(values, axis, [(i, i ^ mask) for i in range(lax.axis_size(axis))])
+
+
+def paired(values, axis, partner):
+    return lax.ppermute(values, axis, list(enumerate(partner)))
+
+
+FAR = (6, 7, 4, 5, 2, 3, 0, 1)
 
 
 def summed(values, axis, beside):
-    below = shifted(values, axis, 1)
-    above = shifted(values, axis, -1)
-    two = values + above
-    three = two + below
-    far = (shifted(three, axis, -3), shifted(two, axis, 3))
+    near = [swapped(values, axis, mask) for mask in (1,3,2)]
+    values = values + near[0]+near[1]+near[2]
+    far = paired(values, axis, FAR)
     far, beside = lax.optimization_barrier((far, beside))
-    return three + far[0] + far[1], beside
+    return values + far, beside
 
 
 def shards(inputs, cotangent, features, projection, decay_rates):

time: 62 us -> 57.7 us (0.931)
  waiting for transfers between devices: 22.1 us -> 15.8 us
  starting transfers between devices: 25.4 us -> 27.4 us
    ppermute x4, waiting for transfers between devices: 8.42 us -> 1.08 us  [the longest x1 0.73 us: paired(): return lax.ppermute(values, axis, list(enumerate(partner)))]
    ppermute x4, starting transfers between devices: 8.56 us -> 10.6 us  [the longest x1 5.84 us: paired(): return lax.ppermute(values, axis, list(enumerate(partner)))]
    all_to_all x3, waiting for transfers between devices: 5.15 us -> 6.11 us  [exchanged(): return lax.all_to_all(values, axes, 0, 0, tiled=True)]
  transfers between devices with their start and end apart: 8 -> 8, of which waited for: 7 -> 6; matrix products, arithmetic and copies ran while one was open for 1% -> 1% of each run, Pallas kernels for 7% -> 7%
where the time goes in v3:
time: 57.7 us; the launch traced here: 57 us
  starting transfers between devices  27.4 us (47%)
  waiting for transfers between devices  15.8 us (27%)
  Pallas kernels  11.6 us (20%)
  local copies, waits for them, and re-layouts  0.85 us (1%)
  between operations  0.72 us (1%)
  other arithmetic  0.66 us (1%)
    all_to_all x3, starting transfers between devices, exchanged(): return lax.all_to_all(values, axes, 0, 0, tiled=True)  14 us
    ppermute x1, waiting for transfers between devices, shards(): other = lax.ppermute(both, 'x_hi', [(0, 1), (1, 0)])  8.56 us
    all_to_all x3, waiting for transfers between devices, exchanged(): return lax.all_to_all(values, axes, 0, 0, tiled=True)  6.11 us
    ppermute x1, starting transfers between devices, paired(): return lax.ppermute(values, axis, list(enumerate(partner)))  5.84 us
    ppermute x3, starting transfers between devices, swapped(): lax.ppermute(values, axis, [(i, i ^ mask) for i in range(lax.axis_size(ax...  4.73 us
    pallas_call x1, Pallas kernels, shards(): call(taps_kernel, (shape((per, 4, blocks + lags, LANES), F32), shape((2 *...  4.28 us
    pallas_call x1, Pallas kernels, shards(): call(inputs_kernel, shape((groups, per * subs, SUB), BF16), [(groups * 16...  4.23 us
    ppermute x1, starting transfers between devices, shards(): other = lax.ppermute(both, 'x_hi', [(0, 1), (1, 0)])  2.82 us
  transfers between devices with their start and end apart: 8, of which 6 were waited for; matrix products, arithmetic and copies ran while one was open for 1% of the time, Pallas kernels for 7%

profile of v3, /device:TPU:32, one launch (start us, length us, event | category | flops | bytes accessed | tf_op | source)
XLA Modules:
  0.0 57.0 jit_solution(4850194969278285974)
XLA Ops:
  0.6 0.0 copy-start.1
  0.6 0.0 copy-start.2
  0.7 2.4 %shard_map.94 = (bf16[16,144,128]{2,1,0:T(8,128)(2,1)}, f32[72,64]{1,0:T(8,128)}) custom-call(f32[64,256]{1,0:T(8,128)} %refs_0_.1, f32[64,64]{1,0:T(8,128)} %refs_1_.1, f32[1,64]{1,0:T(1,128)} %bitcast.1, bf16[64,2048]{1,0:T(8,128)(2,1)} %refs_3_.1, bf16[64,2048]{1,0:T(8,128)(2,1)} %refs_4_.1), custom_call_target="tpu_custom_call" | custom-call | flops 4194304 | bytes 1048576 | tf_op jit(solution)/shard_map/pallas_call | solution.py:296
  3.0 0.0 copy-start
  3.1 5.5 %all-to-all-start = ((bf16[16,144,128]{2,1,0:T(8,128)(2,1)}), bf16[16,144,128]{2,1,0:T(8,128)(2,1)S(1)}, u32[]{:S(2)}, u32[]{:S(2)}) async-start(bf16[16,144,128]{2,1,0:T(8,128)(2,1)} %get-tuple-element.17), calls=%async_computation | async-start | bytes 1179648 | tf_op jit(solution)/shard_map/all_to_all | solution.py:293
  8.6 2.8 %collective-permute-start = (f32[72,64]{1,0:T(8,128)S(1)}, f32[72,64]{1,0:T(8,128)S(1)}, u32[]{:S(2)}, u32[]{:S(2)}) collective-permute-start(f32[72,64]{1,0:T(8,128)S(1)} %copy-done), channel_id=1, source_target_pairs={{0,8},{8,0},{1,9},{9,1},{2,10},{10,2},{3,11},{11,3},{4,12},{12,4},... | collective-permute-start | bytes 55304 | tf_op jit(solution)/shard_map/ppermute | solution.py:304
  11.4 8.6 %collective-permute-done.refs_2_ = f32[72,64]{1,0:T(8,128)S(1)} collective-permute-done((f32[72,64]{1,0:T(8,128)S(1)}, f32[72,64]{1,0:T(8,128)S(1)}, u32[]{:S(2)}, u32[]{:S(2)}) %collective-permute-start) | collective-permute-done | bytes 18464 | tf_op jit(solution)/shard_map/ppermute | solution.py:304
  20.0 0.6 %all-to-all-done.recv_ref = bf16[16,144,128]{2,1,0:T(8,128)(2,1)S(1)} async-done(((bf16[16,144,128]{2,1,0:T(8,128)(2,1)}), bf16[16,144,128]{2,1,0:T(8,128)(2,1)S(1)}, u32[]{:S(2)}, u32[]{:S(2)}) %all-to-all-start) | async-done | bytes 589856 | tf_op jit(solution)/shard_map/all_to_all | solution.py:293
  20.6 4.3 %shard_map.95 = (f32[4,4,144,128]{3,2,1,0:T(8,128)S(1)}, f32[32,8,128]{2,1,0:T(8,128)}) custom-call(bf16[16,144,128]{2,1,0:T(8,128)(2,1)S(1)} %all-to-all-done.recv_ref, bf16[2,256,512]{2,1,0:T(8,128)(2,1)S(1)} %copy-done.2, bf16[2,512,256]{2,1,0:T(8,128)(2,1)S(1)} %copy-done.1), custom_call_target="tpu_custom_call" | custom-call | flops 4294967296 | bytes 1048576 | tf_op jit(solution)/shard_map/pallas_call | solution.py:307
  24.9 5.0 %all-to-all-start.1 = ((f32[32,8,128]{2,1,0:T(8,128)}), f32[32,8,128]{2,1,0:T(8,128)S(1)}, u32[]{:S(2)}, u32[]{:S(2)}) async-start(f32[32,8,128]{2,1,0:T(8,128)} %get-tuple-element.20), calls=%async_computation.1 | async-start | bytes 262144 | tf_op jit(solution)/shard_map/all_to_all | solution.py:293
  29.9 4.2 %shard_map.96 = bf16[16,32,256]{2,1,0:T(8,128)(2,1)} custom-call(bf16[16,144,128]{2,1,0:T(8,128)(2,1)S(1)} %all-to-all-done.recv_ref, f32[4,4,144,128]{3,2,1,0:T(8,128)S(1)} %get-tuple-element.21.win_ref, bf16[2,256,512]{2,1,0:T(8,128)(2,1)S(1)} %copy-done.2, bf16[2,512,256]{2,1,0:T(8,128)(2,1)S(1)} %copy-done.1), custom_call_target="tpu_custom_call" | custom-call | flops 4294967296 | bytes 1048576 | tf_op jit(solution)/shard_map/pallas_call | solution.py:314
  34.1 3.7 %all-to-all-done.1.refs_0_ = f32[32,8,128]{2,1,0:T(8,128)S(1)} async-done(((f32[32,8,128]{2,1,0:T(8,128)}), f32[32,8,128]{2,1,0:T(8,128)S(1)}, u32[]{:S(2)}, u32[]{:S(2)}) %all-to-all-start.1) | async-done | bytes 131104 | tf_op jit(solution)/shard_map/all_to_all | solution.py:293
  37.8 0.8 %shard_map.97 = (f32[64,256]{1,0:T(8,128)}, f32[64,256]{1,0:T(8,128)S(1)}) custom-call(f32[32,8,128]{2,1,0:T(8,128)S(1)} %all-to-all-done.1.refs_0_, f32[72,64]{1,0:T(8,128)S(1)} %copy-done, f32[72,64]{1,0:T(8,128)S(1)} %collective-permute-done.refs_2_), custom_call_target="tpu_custom_call" | custom-call | flops 4194304 | bytes 1048576 | tf_op jit(solution)/shard_map/pallas_call | solution.py:321
  38.5 3.3 %collective-permute-start.3 = (f32[64,256]{1,0:T(8,128)S(1)}, f32[64,256]{1,0:T(8,128)S(1)}, u32[]{:S(2)}, u32[]{:S(2)}) collective-permute-start(f32[64,256]{1,0:T(8,128)S(1)} %get-tuple-element.26), channel_id=1, source_target_pairs={{0,2},{1,3},{2,0},{3,1},{4,6},{5,7},{6,4},{7,5},{8,10},{9,11},{10,... | collective-permute-start | bytes 196616 | tf_op jit(solution)/shard_map/ppermute | solution.py:263
  41.8 0.0 collective-permute-start.2
  41.8 1.5 %collective-permute-start.1 = (f32[64,256]{1,0:T(8,128)S(1)}, f32[64,256]{1,0:T(8,128)S(1)}, u32[]{:S(2)}, u32[]{:S(2)}) collective-permute-start(f32[64,256]{1,0:T(8,128)S(1)} %get-tuple-element.26), channel_id=1, source_target_pairs={{0,1},{1,0},{2,3},{3,2},{4,5},{5,4},{6,7},{7,6},{8,9},{9,8},{10,11... | collective-permute-start | bytes 196616 | tf_op jit(solution)/shard_map/ppermute | solution.py:263
  43.3 3.5 %all-to-all-start.2 = ((bf16[16,32,256]{2,1,0:T(8,128)(2,1)}), bf16[16,32,256]{2,1,0:T(8,128)(2,1)S(1)}, u32[]{:S(2)}, u32[]{:S(2)}) async-start(bf16[16,32,256]{2,1,0:T(8,128)(2,1)} %shard_map.96), calls=%async_computation.2 | async-start | bytes 524288 | tf_op jit(solution)/shard_map/all_to_all | solution.py:293
  46.8 0.0 collective-permute-done.3
  46.8 0.3 collective-permute-done.2
  47.2 5.8 %collective-permute-start.4 = (f32[64,256]{1,0:T(8,128)S(1)}, f32[64,256]{1,0:T(8,128)S(1)}, u32[]{:S(2)}, u32[]{:S(2)}) collective-permute-start(f32[64,256]{1,0:T(8,128)S(1)} %add_add_fusion), channel_id=1, source_target_pairs={{0,6},{1,7},{2,4},{3,5},{4,2},{5,3},{6,0},{7,1},{8,14},{9,15},{10,... | collective-permute-start | bytes 196616 | tf_op jit(solution)/shard_map/ppermute | solution.py:267
  53.0 1.8 %all-to-all-done.2 = bf16[16,32,256]{2,1,0:T(8,128)(2,1)S(1)} async-done(((bf16[16,32,256]{2,1,0:T(8,128)(2,1)}), bf16[16,32,256]{2,1,0:T(8,128)(2,1)S(1)}, u32[]{:S(2)}, u32[]{:S(2)}) %all-to-all-start.2) | async-done | bytes 262176 | tf_op jit(solution)/shard_map/all_to_all | solution.py:293
  54.8 0.8 %reshape.13 = bf16[64,2048]{1,0:T(8,128)(2,1)} reshape(bf16[16,32,256]{2,1,0:T(8,128)(2,1)S(1)} %all-to-all-done.2) | data formatting | bytes 524288 | tf_op jit(solution)/shard_map/reshape | solution.py:328
  55.7 0.7 %collective-permute-done.4 = f32[64,256]{1,0:T(8,128)S(1)} collective-permute-done((f32[64,256]{1,0:T(8,128)S(1)}, f32[64,256]{1,0:T(8,128)S(1)}, u32[]{:S(2)}, u32[]{:S(2)}) %collective-permute-start.4) | collective-permute-done | bytes 65568 | tf_op jit(solution)/shard_map/ppermute | solution.py:267
  56.4 0.6 %add.15 = f32[64,256]{1,0:T(8,128)} add(f32[64,256]{1,0:T(8,128)S(1)} %add_add_fusion, f32[64,256]{1,0:T(8,128)S(1)} %collective-permute-done.4) | non-fusion elementwise | flops 16384 | bytes 196608 | tf_op jit(solution)/shard_map/add | solution.py:278
  (5 shorter events, 0.0 us)
Async XLA Ops:
  0.6 19.9 %copy-start.1 = (bf16[2,512,256]{2,1,0:T(8,128)(2,1)S(1)}, bf16[2,512,256]{2,1,0:T(8,128)(2,1)}, u32[]{:S(2)}) copy-start(bf16[2,512,256]{2,1,0:T(8,128)(2,1)} %constant.5.clone.inv_ref) | copy-start | bytes 1572868
  0.6 19.9 %copy-start.2 = (bf16[2,256,512]{2,1,0:T(8,128)(2,1)S(1)}, bf16[2,256,512]{2,1,0:T(8,128)(2,1)}, u32[]{:S(2)}) copy-start(bf16[2,256,512]{2,1,0:T(8,128)(2,1)} %constant.4.clone.fwd_ref) | copy-start | bytes 1572868
  3.0 5.5 %copy-start = (f32[72,64]{1,0:T(8,128)S(1)}, f32[72,64]{1,0:T(8,128)}, u32[]{:S(2)}) copy-start(f32[72,64]{1,0:T(8,128)} %get-tuple-element.18.refs_1_) | copy-start | bytes 55300
  3.1 17.5 %all-to-all-start = ((bf16[16,144,128]{2,1,0:T(8,128)(2,1)}), bf16[16,144,128]{2,1,0:T(8,128)(2,1)S(1)}, u32[]{:S(2)}, u32[]{:S(2)}) async-start(bf16[16,144,128]{2,1,0:T(8,128)(2,1)} %get-tuple-element.17), calls=%async_computation | async-start | bytes 1179648 | tf_op jit(solution)/shard_map/all_to_all | solution.py:293
  8.6 11.4 %collective-permute-start = (f32[72,64]{1,0:T(8,128)S(1)}, f32[72,64]{1,0:T(8,128)S(1)}, u32[]{:S(2)}, u32[]{:S(2)}) collective-permute-start(f32[72,64]{1,0:T(8,128)S(1)} %copy-done), channel_id=1, source_target_pairs={{0,8},{8,0},{1,9},{9,1},{2,10},{10,2},{3,11},{11,3},{4,12},{12,4},... | collective-permute-start | bytes 55304 | tf_op jit(solution)/shard_map/ppermute | solution.py:304
  24.9 12.9 %all-to-all-start.1 = ((f32[32,8,128]{2,1,0:T(8,128)}), f32[32,8,128]{2,1,0:T(8,128)S(1)}, u32[]{:S(2)}, u32[]{:S(2)}) async-start(f32[32,8,128]{2,1,0:T(8,128)} %get-tuple-element.20), calls=%async_computation.1 | async-start | bytes 262144 | tf_op jit(solution)/shard_map/all_to_all | solution.py:293
  38.5 8.3 %collective-permute-start.3 = (f32[64,256]{1,0:T(8,128)S(1)}, f32[64,256]{1,0:T(8,128)S(1)}, u32[]{:S(2)}, u32[]{:S(2)}) collective-permute-start(f32[64,256]{1,0:T(8,128)S(1)} %get-tuple-element.26), channel_id=1, source_target_pairs={{0,2},{1,3},{2,0},{3,1},{4,6},{5,7},{6,4},{7,5},{8,10},{9,11},{10,... | collective-permute-start | bytes 196616 | tf_op jit(solution)/shard_map/ppermute | solution.py:263
  41.8 5.4 %collective-permute-start.2 = (f32[64,256]{1,0:T(8,128)S(1)}, f32[64,256]{1,0:T(8,128)S(1)}, u32[]{:S(2)}, u32[]{:S(2)}) collective-permute-start(f32[64,256]{1,0:T(8,128)S(1)} %get-tuple-element.26), channel_id=1, source_target_pairs={{0,3},{1,2},{2,1},{3,0},{4,7},{5,6},{6,5},{7,4},{8,11},{9,10},{10,... | collective-permute-start | bytes 196616 | tf_op jit(solution)/shard_map/ppermute | solution.py:263
  41.8 5.4 %collective-permute-start.1 = (f32[64,256]{1,0:T(8,128)S(1)}, f32[64,256]{1,0:T(8,128)S(1)}, u32[]{:S(2)}, u32[]{:S(2)}) collective-permute-start(f32[64,256]{1,0:T(8,128)S(1)} %get-tuple-element.26), channel_id=1, source_target_pairs={{0,1},{1,0},{2,3},{3,2},{4,5},{5,4},{6,7},{7,6},{8,9},{9,8},{10,11... | collective-permute-start | bytes 196616 | tf_op jit(solution)/shard_map/ppermute | solution.py:263
  43.3 11.6 %all-to-all-start.2 = ((bf16[16,32,256]{2,1,0:T(8,128)(2,1)}), bf16[16,32,256]{2,1,0:T(8,128)(2,1)S(1)}, u32[]{:S(2)}, u32[]{:S(2)}) async-start(bf16[16,32,256]{2,1,0:T(8,128)(2,1)} %shard_map.96), calls=%async_computation.2 | async-start | bytes 524288 | tf_op jit(solution)/shard_map/all_to_all | solution.py:293
  47.2 9.2 %collective-permute-start.4 = (f32[64,256]{1,0:T(8,128)S(1)}, f32[64,256]{1,0:T(8,128)S(1)}, u32[]{:S(2)}, u32[]{:S(2)}) collective-permute-start(f32[64,256]{1,0:T(8,128)S(1)} %add_add_fusion), channel_id=1, source_target_pairs={{0,6},{1,7},{2,4},{3,5},{4,2},{5,3},{6,0},{7,1},{8,14},{9,15},{10,... | collective-permute-start | bytes 196616 | tf_op jit(solution)/shard_map/ppermute | solution.py:267

commit v4 on v3

--- a/solution.py
+++ b/solution.py
@@ -116,7 +116,17 @@
                     store(chan, tile, (first + src) * subs, result[row : row + subs, tile * LANES : (tile + 1) * LANES])
 
 
-def taps_kernel(recv_ref, fwd_ref, inv_ref, win_ref, grad_ref, cot_spec, in_spec, sums, spec):
+def products(real, imag):
+    return real - imag, real, imag
+
+
+def window_of(win_ref, mixed, index, which, row, rows):
+    if which == 0:
+        return win_ref[index, 0, row : row + rows, :]
+    return mixed[index, which - 1, row : row + rows, :]
+
+
+def taps_kernel(recv_ref, fwd_ref, inv_ref, win_ref, grad_ref, cot_spec, in_spec, mixed, sums, spec):
     groups = recv_ref.shape[0]
     per, subs, lags = 4, 8, 16
     blocks = groups * subs
@@ -125,46 +135,59 @@
         cot_spec[chan, tile, row : row + subs, :] = value
 
     def store_in(chan, tile, row, value):
-        in_spec[chan, tile, row : row + subs, :] = value
+        in_spec[(chan * 2 + tile % 2) * 3 + 1 + tile // 2, row : row + subs, :] = value
 
     block_spectra(recv_ref, 0, fwd_ref, store_cot)
     cot_spec[:, :, blocks:, :] = jnp.zeros((per, 4, subs, LANES), F32)
     block_spectra(recv_ref, 64, fwd_ref, store_in)
-    win_ref[:, :, blocks:, :] = jnp.zeros((per, 4, lags, LANES), F32)
+    for ref in (win_ref, mixed):
+        ref[:, :, blocks:, :] = jnp.zeros((2 * per, 2, lags, LANES), F32)
     for chan in range(per):
         now = [cot_spec[chan, tile, 0:blocks, :] for tile in range(4)]
         nxt = [cot_spec[chan, tile, 1 : blocks + 1, :] for tile in range(4)]
-        win_ref[chan, 0, 0:blocks, :] = now[0] + nxt[2]
-        win_ref[chan, 1, 0:blocks, :] = now[1] - nxt[3]
-        win_ref[chan, 2, 0:blocks, :] = now[2] - nxt[0]
-        win_ref[chan, 3, 0:blocks, :] = now[3] + nxt[1]
+        parts = ((now[0] + nxt[2], now[2] - nxt[0]), (now[1] - nxt[3], now[3] + nxt[1]))
+        for half, (real, imag) in enumerate(parts):
+            base = chan * 2 + half
+            win_ref[base, 0, 0:blocks, :] = real
+            win_ref[base, 1, 0:blocks, :] = imag
+            mixed[base, 0, 0:blocks, :] = imag - real
+            mixed[base, 1, 0:blocks, :] = real + imag
+
+    for part in range(2 * per):
+        in_spec[3 * part] = in_spec[3 * part + 1] - in_spec[3 * part + 2]
 
     def one(index, carry):
-        chan = index // 2
-        half = index % 2
-        acc_re = [None] * lags
-        acc_im = [None] * lags
-        for src in range(groups):
-            left_re = in_spec[chan, half, src * subs : (src + 1) * subs, :]
-            left_im = in_spec[chan, 2 + half, src * subs : (src + 1) * subs, :]
+        for which in range(3):
+            acc = [None] * lags
+            left = None
+            for src in range(groups + 1):
+                before = left
+                if src < groups:
+                    left = in_spec[3 * index + which, src * subs : (src + 1) * subs, :]
+                for lag in range(subs):
+                    row = src * subs + lag
+                    window = window_of(win_ref, mixed, index, which, row, subs)
+                    if src < groups:
+                        acc[lag] = left * window if src == 0 else acc[lag] + left * window
+                    if src > 0:
+                        far = lag + subs
+                        acc[far] = before * window if src == 1 else acc[far] + before * window
             for lag in range(lags):
-                row = src * subs + lag
-                win_re = win_ref[chan, half, row : row + subs, :]
-                win_im = win_ref[chan, 2 + half, row : row + subs, :]
-                term_re = left_re * win_re + left_im * win_im
-                term_im = left_re * win_im - left_im * win_re
-                acc_re[lag] = term_re if src == 0 else acc_re[lag] + term_re
-                acc_im[lag] = term_im if src == 0 else acc_im[lag] + term_im
-        for part, acc in enumerate((acc_re, acc_im)):
-            for lag in range(lags):
-                sums[part, lag * subs : (lag + 1) * subs, :] = acc[lag]
-            total = sums[part, pl.ds(0, lags, stride=subs), :]
-            for sub in range(1, subs):
-                total = total + sums[part, pl.ds(sub, lags, stride=subs), :]
-            spec[2 * part + half, pl.ds(chan, lags, stride=per), :] = total
+                sums[3 * index + which, lag * subs : (lag + 1) * subs, :] = acc[lag]
         return carry
 
     lax.fori_loop(0, 2 * per, one, 0)
+    for chan in range(per):
+        for half in range(2):
+            totals = []
+            for which in range(3):
+                index = (chan * 2 + half) * 3 + which
+                total = sums[index, pl.ds(0, lags, stride=subs), :]
+                for sub in range(1, subs):
+                    total = total + sums[index, pl.ds(sub, lags, stride=subs), :]
+                totals.append(total)
+            spec[half, pl.ds(chan, lags, stride=per), :] = totals[0] + totals[2]
+            spec[2 + half, pl.ds(chan, lags, stride=per), :] = totals[0] + totals[1]
     left = jnp.concatenate([spec[tile] for tile in range(4)], axis=1)
     result = dot_terms(left, inv_ref)
     for lag in range(lags):
@@ -174,10 +197,9 @@
             grad_ref[2 * lag + copy, per : 2 * per, :] = result[own, LANES:]
 
 
-def inputs_kernel(recv_ref, win_ref, fwd_ref, inv_ref, grad_ref, frows, fspec, spec):
+def inputs_kernel(recv_ref, win_ref, fwd_ref, inv_ref, grad_ref, frows, fspec, mixed, spec):
     groups = recv_ref.shape[0]
     per, subs, lags = 4, 8, 16
-    blocks = groups * subs
     frows[...] = recv_ref[:, 128:144, :].astype(F32).reshape(groups * 16, LANES)
     terms = []
     for term in range(2):
@@ -187,59 +209,94 @@
             chans.append(jnp.concatenate(halves, axis=1))
         terms.append(jnp.concatenate(chans, axis=0).astype(BF16))
     result = dot(terms[0], fwd_ref[0]) + dot(terms[0], fwd_ref[1]) + dot(terms[1], fwd_ref[0])
-    for tile in range(4):
-        for chan in range(per):
-            fspec[chan, tile] = result[chan * lags : (chan + 1) * lags, tile * LANES : (tile + 1) * LANES]
+    for chan in range(per):
+        rows = result[chan * lags : (chan + 1) * lags]
+        for half in range(2):
+            real = rows[:, half * LANES : (half + 1) * LANES]
+            imag = rows[:, (2 + half) * LANES : (3 + half) * LANES]
+            for which, value in enumerate(products(real, imag)):
+                fspec[(chan * 2 + half) * 3 + which] = value
+
+    for part in range(2 * per):
+        mixed[part, 0] = win_ref[part, 1] - win_ref[part, 0]
+        mixed[part, 1] = win_ref[part, 0] + win_ref[part, 1]
 
     def one(index, carry):
-        chan = index // 2
-        half = index % 2
-        filt_re = [jnp.broadcast_to(fspec[chan, half, lag : lag + 1, :], (subs, LANES)) for lag in range(lags)]
-        filt_im = [jnp.broadcast_to(fspec[chan, 2 + half, lag : lag + 1, :], (subs, LANES)) for lag in range(lags)]
-        for src in range(groups):
-            acc_re = None
-            acc_im = None
-            for lag in range(lags):
-                row = src * subs + lag
-                win_re = win_ref[chan, half, row : row + subs, :]
-                win_im = win_ref[chan, 2 + half, row : row + subs, :]
-                term_re = filt_re[lag] * win_re + filt_im[lag] * win_im
-                term_im = filt_re[lag] * win_im - filt_im[lag] * win_re
-                acc_re = term_re if lag == 0 else acc_re + term_re
-                acc_im = term_im if lag == 0 else acc_im + term_im
-            spec[chan, half, src * subs : (src + 1) * subs, :] = acc_re
-            spec[chan, 2 + half, src * subs : (src + 1) * subs, :] = acc_im
+        for which in range(3):
+            own = 3 * index + which
+            filt = [jnp.broadcast_to(fspec[own, lag : lag + 1, :], (subs, LANES)) for lag in range(lags)]
+            low = None
+            for src in range(groups + 1):
+                before = low
+                near = [None, None]
+                far = [None, None]
+                for lag in range(subs):
+                    row = src * subs + lag
+                    window = window_of(win_ref, mixed, index, which, row, subs)
+                    way = lag % 2
+                    if src < groups:
+                        term = filt[lag] * window
+                        near[way] = term if near[way] is None else near[way] + term
+                    if src > 0:
+                        term = filt[lag + subs] * window
+                        far[way] = term if far[way] is None else far[way] + term
+                if src < groups:
+                    low = near[0] + near[1]
+                if src > 0:
+                    spec[own, (src - 1) * subs : src * subs, :] = before + (far[0] + far[1])
         return carry
 
     lax.fori_loop(0, 2 * per, one, 0)
     for first in range(0, per, 2):
         pair = []
         for chan in (first, first + 1):
-            left = jnp.concatenate([spec[chan, tile] for tile in range(4)], axis=1)
-            pair.append(dot_terms(left, inv_ref).reshape(groups, subs, SUB))
+            base = chan * 6
+            tiles = [spec[base + 3 * half] + spec[base + 3 * half + 2] for half in range(2)]
+            tiles += [spec[base + 3 * half] + spec[base + 3 * half + 1] for half in range(2)]
+            pair.append(dot_terms(jnp.concatenate(tiles, axis=1), inv_ref).reshape(groups, subs, SUB))
         both = jnp.concatenate(pair, axis=1)
         grad_ref[:, first * subs : (first + 2) * subs, :] = both.astype(BF16)
 
 
-def features_kernel(taps, grad_ref, mine_ref, other_ref, out_ref, part_ref, held):
+def features_kernel(taps, grad_ref, mine_ref, other_ref, part_ref, held):
     groups = grad_ref.shape[0] // 2
     per = grad_ref.shape[1] // 2
-    channels, tap_rows = out_ref.shape
+    tap_rows = part_ref.shape[1]
     order = mine_ref.shape[0] - 8
     me = lax.axis_index("x_hi")
-    for group in range(groups):
-        own = slice(group * per, (group + 1) * per)
-        for ref, source in ((out_ref, 2 * group + me), (held, 2 * group + 1 - me)):
-            ref[own, 0:LANES] = grad_ref[source, 0:per, :]
-            ref[own, LANES:] = grad_ref[source, per : 2 * per, :]
     total = None
-    for both, grads in ((mine_ref, out_ref), (other_ref, held)):
+    for which, both in enumerate((mine_ref, other_ref)):
+        for group in range(groups):
+            own = slice(group * per, (group + 1) * per)
+            source = 2 * group + (1 - me if which else me)
+            held[which, own, 0:LANES] = grad_ref[source, 0:per, :]
+            held[which, own, LANES:] = grad_ref[source, per : 2 * per, :]
         decay = decay_of(both[order : order + 1, :], tap_rows, taps)
         left_high, left_low = two_terms(both[0:order, :])
-        high, low = two_terms(decay * grads[...])
+        high, low = two_terms(decay * held[which])
         term = dot(left_high, high) + dot(left_high, low) + dot(left_low, high)
         total = term if total is None else total + term
     part_ref[...] = total
+
+
+def finish_kernel(recv_ref, grad_ref, near_ref, far_ref, x_ref, filter_ref, feature_ref, rows):
+    groups, span = recv_ref.shape[:2]
+    per = grad_ref.shape[1] // 2
+    channels = x_ref.shape[0]
+    subs = x_ref.shape[1] // SUB
+    me = lax.axis_index("x_hi")
+    feature_ref[...] = near_ref[...] + far_ref[...]
+    for group in range(groups):
+        own = slice(group * per, (group + 1) * per)
+        filter_ref[own, 0:LANES] = grad_ref[2 * group + me, 0:per, :]
+        filter_ref[own, LANES:] = grad_ref[2 * group + me, per : 2 * per, :]
+        block = recv_ref[group].astype(F32)
+        for half in range(2):
+            rows[half, group * span : (group + 1) * span, :] = block[:, half * LANES : (half + 1) * LANES]
+    for sub in range(subs):
+        for half in range(2):
+            start = sub * SUB + half * LANES
+            x_ref[:, start : start + LANES] = rows[half, pl.ds(sub, channels, stride=subs), :].astype(BF16)
 
 
 def call(kernel, out, scratch, flops, fetched=(), limit=VMEM_LIMIT):
@@ -270,12 +327,10 @@
 FAR = (6, 7, 4, 5, 2, 3, 0, 1)
 
 
-def summed(values, axis, beside):
-    near = [swapped(values, axis, mask) for mask in (1,3,2)]
-    values = values + near[0]+near[1]+near[2]
-    far = paired(values, axis, FAR)
-    far, beside = lax.optimization_barrier((far, beside))
-    return values + far, beside
+def halves_of_sum(values, axis):
+    near = [swapped(values, axis, mask) for mask in (1, 3, 2)]
+    values = values + near[0] + near[1] + near[2]
+    return values, paired(values, axis, FAR)
 
 
 def shards(inputs, cotangent, features, projection, decay_rates):
@@ -304,30 +359,35 @@
     other = lax.ppermute(both, "x_hi", [(0, 1), (1, 0)])
     received, other = lax.optimization_barrier((exchanged(payload, "ctx"), other))
     blocks = groups * subs
+    mixed = (2 * per, 2, blocks + lags, LANES)
     windows, tap_grads = call(
         taps_kernel,
-        (shape((per, 4, blocks + lags, LANES), F32), shape((2 * groups, 2 * per, LANES), F32)),
-        [(per, 4, blocks + subs, LANES), (per, 4, blocks, LANES), (2, lags * subs, LANES), (4, per * lags, LANES)],
+        (shape((2 * per, 2, blocks + lags, LANES), F32), shape((2 * groups, 2 * per, LANES), F32)),
+        [(per, 4, blocks + subs, LANES), (6 * per, blocks, LANES), mixed, (6 * per, lags * subs, LANES), (4, per * lags, LANES)],
         1 << 32,
     )(received, forward, backward)
     tap_grads = exchanged(tap_grads, ("ctx", "x_hi"))
     x_parts = call(
         inputs_kernel,
         shape((groups, per * subs, SUB), BF16),
-        [(groups * 16, LANES), (per, 4, lags, LANES), (per, 4, blocks, LANES)],
+        [(groups * 16, LANES), (6 * per, lags, LANES), mixed, (6 * per, blocks, LANES)],
         1 << 32,
     )(received, windows, forward, backward)
     tap_grads, x_parts = lax.optimization_barrier((tap_grads, x_parts))
-    filter_grad, part = call(
+    part = call(
         lambda *refs: features_kernel(taps, *refs),
-        (shape((channels, tap_rows), F32), shape((order, tap_rows), F32)),
-        [(channels, tap_rows)],
+        shape((order, tap_rows), F32),
+        [(2, channels, tap_rows)],
         1 << 22,
     )(tap_grads, both, other)
     part, x_parts = lax.optimization_barrier((part, x_parts))
-    x_grad = exchanged(x_parts, "ctx").reshape(channels, block_len)
-    feature_grad, x_grad = summed(part, "z", x_grad)
-    return (x_grad, filter_grad, feature_grad)
+    near, far = halves_of_sum(part, "z")
+    return call(
+        finish_kernel,
+        (shape((channels, block_len), BF16), shape((channels, tap_rows), F32), shape((order, tap_rows), F32)),
+        [(2, channels * subs, LANES)],
+        1 << 22,
+    )(exchanged(x_parts, "ctx"), tap_grads, near, far)
 
 
 def solution(mesh):

time: 57.7 us -> 56.8 us (0.984)
  waiting for transfers between devices: 15.8 us -> 17.4 us
  Pallas kernels: 11.6 us -> 10.5 us
  local copies, waits for them, and re-layouts: 0.85 us -> 0.02 us
  other arithmetic: 0.66 us -> 0.02 us
    ppermute x1, waiting for transfers between devices: 0.73 us -> 3.35 us  [paired(): return lax.ppermute(values, axis, list(enumerate(partner)))]
    pallas_call x1, Pallas kernels: 4.23 us -> 3.22 us  [shards(): call(inputs_kernel, shape((groups, per * subs, SUB), BF16), [(groups * 16...]
    reshape x1 -> x0, local copies, waits for them, and re-layouts: 0.83 us -> none  [shards(): x_grad = exchanged(x_parts, 'ctx').reshape(channels, block_len)]
    all_to_all x3, waiting for transfers between devices: 6.11 us -> 5.32 us  [exchanged(): return lax.all_to_all(values, axes, 0, 0, tiled=True)]
    add x2 -> x1, other arithmetic: 0.66 us -> 0.02 us  [halves_of_sum(): values = values + near[0] + near[1] + near[2]]
    pallas_call x2 -> x3, Pallas kernels: 5.03 us -> 4.94 us  [the longest x1 3.79 us: shards(): call(taps_kernel, (shape((2 * per, 2, blocks + lags, LANES), F32), shape(...]
  transfers between devices with their start and end apart: 8 -> 8, of which waited for: 6 -> 5; matrix products, arithmetic and copies ran while one was open for 1% -> 0% of each run, Pallas kernels for 7% -> 6%
where the time goes in v4:
time: 56.8 us; the launch traced here: 56.4 us
  starting transfers between devices  27.7 us (49%)
  waiting for transfers between devices  17.4 us (31%)
  Pallas kernels  10.5 us (18%)
  between operations  0.72 us (1%)
    all_to_all x3, starting transfers between devices, exchanged(): return lax.all_to_all(values, axes, 0, 0, tiled=True)  14 us
    ppermute x1, waiting for transfers between devices, shards(): other = lax.ppermute(both, 'x_hi', [(0, 1), (1, 0)])  8.56 us
    ppermute x1, starting transfers between devices, paired(): return lax.ppermute(values, axis, list(enumerate(partner)))  5.88 us
    all_to_all x3, waiting for transfers between devices, exchanged(): return lax.all_to_all(values, axes, 0, 0, tiled=True)  5.32 us
    ppermute x3, starting transfers between devices, swapped(): lax.ppermute(values, axis, [(i, i ^ mask) for i in range(lax.axis_size(ax...  4.92 us
    pallas_call x1, Pallas kernels, shards(): call(taps_kernel, (shape((2 * per, 2, blocks + lags, LANES), F32), shape(...  3.79 us
    ppermute x1, waiting for transfers between devices, paired(): return lax.ppermute(values, axis, list(enumerate(partner)))  3.35 us
    pallas_call x1, Pallas kernels, shards(): call(inputs_kernel, shape((groups, per * subs, SUB), BF16), [(groups * 16...  3.22 us
  transfers between devices with their start and end apart: 8, of which 5 were waited for; matrix products, arithmetic and copies ran while one was open for 0% of the time, Pallas kernels for 6%

profile of v4, /device:TPU:32, one launch (start us, length us, event | category | flops | bytes accessed | tf_op | source)
XLA Modules:
  0.0 56.4 jit_solution(12486218736625203029)
XLA Ops:
  0.6 0.0 copy-start.1
  0.6 0.0 copy-start.2
  0.7 2.4 %shard_map.94 = (bf16[16,144,128]{2,1,0:T(8,128)(2,1)}, f32[72,64]{1,0:T(8,128)}) custom-call(f32[64,256]{1,0:T(8,128)} %refs_0_.1, f32[64,64]{1,0:T(8,128)} %refs_1_.1, f32[1,64]{1,0:T(1,128)} %bitcast.1, bf16[64,2048]{1,0:T(8,128)(2,1)} %refs_3_.1, bf16[64,2048]{1,0:T(8,128)(2,1)} %refs_4_.1), custom_call_target="tpu_custom_call" | custom-call | flops 4194304 | bytes 1048576 | tf_op jit(solution)/shard_map/pallas_call | solution.py:351
  3.0 0.0 copy-start
  3.1 5.5 %all-to-all-start = ((bf16[16,144,128]{2,1,0:T(8,128)(2,1)}), bf16[16,144,128]{2,1,0:T(8,128)(2,1)S(1)}, u32[]{:S(2)}, u32[]{:S(2)}) async-start(bf16[16,144,128]{2,1,0:T(8,128)(2,1)} %get-tuple-element.13), calls=%async_computation | async-start | bytes 1179648 | tf_op jit(solution)/shard_map/all_to_all | solution.py:348
  8.6 2.8 %collective-permute-start = (f32[72,64]{1,0:T(8,128)S(1)}, f32[72,64]{1,0:T(8,128)S(1)}, u32[]{:S(2)}, u32[]{:S(2)}) collective-permute-start(f32[72,64]{1,0:T(8,128)S(1)} %copy-done), channel_id=1, source_target_pairs={{0,8},{8,0},{1,9},{9,1},{2,10},{10,2},{3,11},{11,3},{4,12},{12,4},... | collective-permute-start | bytes 55304 | tf_op jit(solution)/shard_map/ppermute | solution.py:359
  11.4 8.6 %collective-permute-done.refs_2_ = f32[72,64]{1,0:T(8,128)S(1)} collective-permute-done((f32[72,64]{1,0:T(8,128)S(1)}, f32[72,64]{1,0:T(8,128)S(1)}, u32[]{:S(2)}, u32[]{:S(2)}) %collective-permute-start) | collective-permute-done | bytes 18464 | tf_op jit(solution)/shard_map/ppermute | solution.py:359
  20.0 0.6 %all-to-all-done.recv_ref = bf16[16,144,128]{2,1,0:T(8,128)(2,1)S(1)} async-done(((bf16[16,144,128]{2,1,0:T(8,128)(2,1)}), bf16[16,144,128]{2,1,0:T(8,128)(2,1)S(1)}, u32[]{:S(2)}, u32[]{:S(2)}) %all-to-all-start) | async-done | bytes 589856 | tf_op jit(solution)/shard_map/all_to_all | solution.py:348
  20.6 3.8 %shard_map.95 = (f32[8,2,144,128]{3,2,1,0:T(8,128)S(1)}, f32[32,8,128]{2,1,0:T(8,128)}) custom-call(bf16[16,144,128]{2,1,0:T(8,128)(2,1)S(1)} %all-to-all-done.recv_ref, bf16[2,256,512]{2,1,0:T(8,128)(2,1)S(1)} %copy-done.2, bf16[2,512,256]{2,1,0:T(8,128)(2,1)S(1)} %copy-done.1), custom_call_target="tpu_custom_call" | custom-call | flops 4294967296 | bytes 1048576 | tf_op jit(solution)/shard_map/pallas_call | solution.py:363
  24.4 5.0 %all-to-all-start.1 = ((f32[32,8,128]{2,1,0:T(8,128)}), f32[32,8,128]{2,1,0:T(8,128)S(1)}, u32[]{:S(2)}, u32[]{:S(2)}) async-start(f32[32,8,128]{2,1,0:T(8,128)} %get-tuple-element.16), calls=%async_computation.1 | async-start | bytes 262144 | tf_op jit(solution)/shard_map/all_to_all | solution.py:348
  29.4 3.2 %shard_map.96 = bf16[16,32,256]{2,1,0:T(8,128)(2,1)} custom-call(bf16[16,144,128]{2,1,0:T(8,128)(2,1)S(1)} %all-to-all-done.recv_ref, f32[8,2,144,128]{3,2,1,0:T(8,128)S(1)} %get-tuple-element.17.win_ref, bf16[2,256,512]{2,1,0:T(8,128)(2,1)S(1)} %copy-done.2, bf16[2,512,256]{2,1,0:T(8,128)(2,1)S(1)} %copy-done.1), custom_call_target="tpu_custom_call" | custom-call | flops 4294967296 | bytes 1048576 | tf_op jit(solution)/shard_map/pallas_call | solution.py:370
  32.6 4.7 %all-to-all-done.1.refs_0_.grad_ref = f32[32,8,128]{2,1,0:T(8,128)S(1)} async-done(((f32[32,8,128]{2,1,0:T(8,128)}), f32[32,8,128]{2,1,0:T(8,128)S(1)}, u32[]{:S(2)}, u32[]{:S(2)}) %all-to-all-start.1) | async-done | bytes 131104 | tf_op jit(solution)/shard_map/all_to_all | solution.py:348
  37.3 0.3 shard_map.97
  37.6 3.4 %collective-permute-start.3 = (f32[64,256]{1,0:T(8,128)S(1)}, f32[64,256]{1,0:T(8,128)S(1)}, u32[]{:S(2)}, u32[]{:S(2)}) collective-permute-start(f32[64,256]{1,0:T(8,128)S(1)} %shard_map.97), channel_id=1, source_target_pairs={{0,2},{1,3},{2,0},{3,1},{4,6},{5,7},{6,4},{7,5},{8,10},{9,11},{10,... | collective-permute-start | bytes 196616 | tf_op jit(solution)/shard_map/ppermute | solution.py:320
  41.0 0.0 collective-permute-start.2
  41.0 1.6 %collective-permute-start.1 = (f32[64,256]{1,0:T(8,128)S(1)}, f32[64,256]{1,0:T(8,128)S(1)}, u32[]{:S(2)}, u32[]{:S(2)}) collective-permute-start(f32[64,256]{1,0:T(8,128)S(1)} %shard_map.97), channel_id=1, source_target_pairs={{0,1},{1,0},{2,3},{3,2},{4,5},{5,4},{6,7},{7,6},{8,9},{9,8},{10,11... | collective-permute-start | bytes 196616 | tf_op jit(solution)/shard_map/ppermute | solution.py:320
  42.5 3.5 %all-to-all-start.2 = ((bf16[16,32,256]{2,1,0:T(8,128)(2,1)}), bf16[16,32,256]{2,1,0:T(8,128)(2,1)S(1)}, u32[]{:S(2)}, u32[]{:S(2)}) async-start(bf16[16,32,256]{2,1,0:T(8,128)(2,1)} %shard_map.96), calls=%async_computation.2 | async-start | bytes 524288 | tf_op jit(solution)/shard_map/all_to_all | solution.py:348
  46.1 0.0 collective-permute-done.3
  46.1 0.2 collective-permute-done.2
  46.3 0.0 collective-permute-done.1
  46.3 5.9 %collective-permute-start.4 = (f32[64,256]{1,0:T(8,128)S(1)}, f32[64,256]{1,0:T(8,128)S(1)}, u32[]{:S(2)}, u32[]{:S(2)}) collective-permute-start(f32[64,256]{1,0:T(8,128)S(1)} %add_add_fusion.near_ref), channel_id=1, source_target_pairs={{0,6},{1,7},{2,4},{3,5},{4,2},{5,3},{6,0},{7,1},{8,14},{9,15},{10,... | collective-permute-start | bytes 196616 | tf_op jit(solution)/shard_map/ppermute | solution.py:324
  52.2 3.3 %collective-permute-done.4.far_ref = f32[64,256]{1,0:T(8,128)S(1)} collective-permute-done((f32[64,256]{1,0:T(8,128)S(1)}, f32[64,256]{1,0:T(8,128)S(1)}, u32[]{:S(2)}, u32[]{:S(2)}) %collective-permute-start.4) | collective-permute-done | bytes 65568 | tf_op jit(solution)/shard_map/ppermute | solution.py:324
  55.5 0.0 all-to-all-done.2.recv_ref
  55.5 0.9 %shard_map.98 = (bf16[64,2048]{1,0:T(8,128)(2,1)}, f32[64,256]{1,0:T(8,128)}, f32[64,256]{1,0:T(8,128)}) custom-call(bf16[16,32,256]{2,1,0:T(8,128)(2,1)S(1)} %all-to-all-done.2.recv_ref, f32[32,8,128]{2,1,0:T(8,128)S(1)} %all-to-all-done.1.refs_0_.grad_ref, f32[64,256]{1,0:T(8,128)S(1)} %add_add_fusion.near_ref, f32[64,256]{1,0:T(8,128)S(1)} %collective-permute-done.4.far_ref), custom_call_target="tpu_custom_call" | custom-call | flops 4194304 | bytes 1048576 | tf_op jit(solution)/shard_map/pallas_call | solution.py:385
  (4 shorter events, 0.0 us)
Async XLA Ops:
  0.6 20.0 %copy-start.1 = (bf16[2,512,256]{2,1,0:T(8,128)(2,1)S(1)}, bf16[2,512,256]{2,1,0:T(8,128)(2,1)}, u32[]{:S(2)}) copy-start(bf16[2,512,256]{2,1,0:T(8,128)(2,1)} %constant.5.clone.inv_ref) | copy-start | bytes 1572868
  0.6 19.9 %copy-start.2 = (bf16[2,256,512]{2,1,0:T(8,128)(2,1)S(1)}, bf16[2,256,512]{2,1,0:T(8,128)(2,1)}, u32[]{:S(2)}) copy-start(bf16[2,256,512]{2,1,0:T(8,128)(2,1)} %constant.4.clone.fwd_ref) | copy-start | bytes 1572868
  3.0 5.5 %copy-start = (f32[72,64]{1,0:T(8,128)S(1)}, f32[72,64]{1,0:T(8,128)}, u32[]{:S(2)}) copy-start(f32[72,64]{1,0:T(8,128)} %get-tuple-element.14.refs_1_) | copy-start | bytes 55300
  3.1 17.5 %all-to-all-start = ((bf16[16,144,128]{2,1,0:T(8,128)(2,1)}), bf16[16,144,128]{2,1,0:T(8,128)(2,1)S(1)}, u32[]{:S(2)}, u32[]{:S(2)}) async-start(bf16[16,144,128]{2,1,0:T(8,128)(2,1)} %get-tuple-element.13), calls=%async_computation | async-start | bytes 1179648 | tf_op jit(solution)/shard_map/all_to_all | solution.py:348
  8.6 11.4 %collective-permute-start = (f32[72,64]{1,0:T(8,128)S(1)}, f32[72,64]{1,0:T(8,128)S(1)}, u32[]{:S(2)}, u32[]{:S(2)}) collective-permute-start(f32[72,64]{1,0:T(8,128)S(1)} %copy-done), channel_id=1, source_target_pairs={{0,8},{8,0},{1,9},{9,1},{2,10},{10,2},{3,11},{11,3},{4,12},{12,4},... | collective-permute-start | bytes 55304 | tf_op jit(solution)/shard_map/ppermute | solution.py:359
  24.4 12.9 %all-to-all-start.1 = ((f32[32,8,128]{2,1,0:T(8,128)}), f32[32,8,128]{2,1,0:T(8,128)S(1)}, u32[]{:S(2)}, u32[]{:S(2)}) async-start(f32[32,8,128]{2,1,0:T(8,128)} %get-tuple-element.16), calls=%async_computation.1 | async-start | bytes 262144 | tf_op jit(solution)/shard_map/all_to_all | solution.py:348
  37.6 8.5 %collective-permute-start.3 = (f32[64,256]{1,0:T(8,128)S(1)}, f32[64,256]{1,0:T(8,128)S(1)}, u32[]{:S(2)}, u32[]{:S(2)}) collective-permute-start(f32[64,256]{1,0:T(8,128)S(1)} %shard_map.97), channel_id=1, source_target_pairs={{0,2},{1,3},{2,0},{3,1},{4,6},{5,7},{6,4},{7,5},{8,10},{9,11},{10,... | collective-permute-start | bytes 196616 | tf_op jit(solution)/shard_map/ppermute | solution.py:320
  41.0 5.3 %collective-permute-start.2 = (f32[64,256]{1,0:T(8,128)S(1)}, f32[64,256]{1,0:T(8,128)S(1)}, u32[]{:S(2)}, u32[]{:S(2)}) collective-permute-start(f32[64,256]{1,0:T(8,128)S(1)} %shard_map.97), channel_id=1, source_target_pairs={{0,3},{1,2},{2,1},{3,0},{4,7},{5,6},{6,5},{7,4},{8,11},{9,10},{10,... | collective-permute-start | bytes 196616 | tf_op jit(solution)/shard_map/ppermute | solution.py:320
  41.0 5.3 %collective-permute-start.1 = (f32[64,256]{1,0:T(8,128)S(1)}, f32[64,256]{1,0:T(8,128)S(1)}, u32[]{:S(2)}, u32[]{:S(2)}) collective-permute-start(f32[64,256]{1,0:T(8,128)S(1)} %shard_map.97), channel_id=1, source_target_pairs={{0,1},{1,0},{2,3},{3,2},{4,5},{5,4},{6,7},{7,6},{8,9},{9,8},{10,11... | collective-permute-start | bytes 196616 | tf_op jit(solution)/shard_map/ppermute | solution.py:320
  42.5 13.0 %all-to-all-start.2 = ((bf16[16,32,256]{2,1,0:T(8,128)(2,1)}), bf16[16,32,256]{2,1,0:T(8,128)(2,1)S(1)}, u32[]{:S(2)}, u32[]{:S(2)}) async-start(bf16[16,32,256]{2,1,0:T(8,128)(2,1)} %shard_map.96), calls=%async_computation.2 | async-start | bytes 524288 | tf_op jit(solution)/shard_map/all_to_all | solution.py:348
  46.3 9.2 %collective-permute-start.4 = (f32[64,256]{1,0:T(8,128)S(1)}, f32[64,256]{1,0:T(8,128)S(1)}, u32[]{:S(2)}, u32[]{:S(2)}) collective-permute-start(f32[64,256]{1,0:T(8,128)S(1)} %add_add_fusion.near_ref), channel_id=1, source_target_pairs={{0,6},{1,7},{2,4},{3,5},{4,2},{5,3},{6,0},{7,1},{8,14},{9,15},{10,... | collective-permute-start | bytes 196616 | tf_op jit(solution)/shard_map/ppermute | solution.py:324

commit v5 on v4

--- a/solution.py
+++ b/solution.py
@@ -328,7 +328,7 @@
 
 
 def halves_of_sum(values, axis):
-    near = [swapped(values, axis, mask) for mask in (1, 3, 2)]
+    near = [swapped(values, axis, mask) for mask in (1, 2, 3)]
     values = values + near[0] + near[1] + near[2]
     return values, paired(values, axis, FAR)
 

time: 56.8 us -> 56.4 us (level)
  starting transfers between devices: 27.7 us -> 26.5 us
  waiting for transfers between devices: 17.4 us -> 18.1 us
    ppermute x3, waiting for transfers between devices: 0.21 us -> 1.31 us  [swapped(): lax.ppermute(values, axis, [(i, i ^ mask) for i in range(lax.axis_size(ax...]
    ppermute x1, starting transfers between devices: 5.88 us -> 4.81 us  [paired(): return lax.ppermute(values, axis, list(enumerate(partner)))]
where the time goes in v5:
time: 56.4 us; the launch traced here: 55.9 us
  starting transfers between devices  26.5 us (47%)
  waiting for transfers between devices  18.1 us (32%)
  Pallas kernels  10.5 us (19%)
  between operations  0.73 us (1%)
    all_to_all x3, starting transfers between devices, exchanged(): return lax.all_to_all(values, axes, 0, 0, tiled=True)  14 us
    ppermute x1, waiting for transfers between devices, shards(): other = lax.ppermute(both, 'x_hi', [(0, 1), (1, 0)])  8.56 us
    all_to_all x3, waiting for transfers between devices, exchanged(): return lax.all_to_all(values, axes, 0, 0, tiled=True)  5.32 us
    ppermute x3, starting transfers between devices, swapped(): lax.ppermute(values, axis, [(i, i ^ mask) for i in range(lax.axis_size(ax...  4.83 us
    ppermute x1, starting transfers between devices, paired(): return lax.ppermute(values, axis, list(enumerate(partner)))  4.81 us
    pallas_call x1, Pallas kernels, shards(): call(taps_kernel, (shape((2 * per, 2, blocks + lags, LANES), F32), shape(...  3.79 us
    pallas_call x1, Pallas kernels, shards(): call(inputs_kernel, shape((groups, per * subs, SUB), BF16), [(groups * 16...  3.22 us
    ppermute x1, waiting for transfers between devices, paired(): return lax.ppermute(values, axis, list(enumerate(partner)))  2.91 us
  transfers between devices with their start and end apart: 8, of which 5 were waited for; matrix products, arithmetic and copies ran while one was open for 0% of the time, Pallas kernels for 6%

profile of v5, /device:TPU:32, one launch (start us, length us, event | category | flops | bytes accessed | tf_op | source)
XLA Modules:
  0.0 55.9 jit_solution(17490376480132765932)
XLA Ops:
  0.6 0.0 copy-start.1
  0.6 0.0 copy-start.2
  0.7 2.4 %shard_map.94 = (bf16[16,144,128]{2,1,0:T(8,128)(2,1)}, f32[72,64]{1,0:T(8,128)}) custom-call(f32[64,256]{1,0:T(8,128)} %refs_0_.1, f32[64,64]{1,0:T(8,128)} %refs_1_.1, f32[1,64]{1,0:T(1,128)} %bitcast.1, bf16[64,2048]{1,0:T(8,128)(2,1)} %refs_3_.1, bf16[64,2048]{1,0:T(8,128)(2,1)} %refs_4_.1), custom_call_target="tpu_custom_call" | custom-call | flops 4194304 | bytes 1048576 | tf_op jit(solution)/shard_map/pallas_call | solution.py:351
  3.0 0.0 copy-start
  3.1 5.5 %all-to-all-start = ((bf16[16,144,128]{2,1,0:T(8,128)(2,1)}), bf16[16,144,128]{2,1,0:T(8,128)(2,1)S(1)}, u32[]{:S(2)}, u32[]{:S(2)}) async-start(bf16[16,144,128]{2,1,0:T(8,128)(2,1)} %get-tuple-element.13), calls=%async_computation | async-start | bytes 1179648 | tf_op jit(solution)/shard_map/all_to_all | solution.py:348
  8.6 2.8 %collective-permute-start = (f32[72,64]{1,0:T(8,128)S(1)}, f32[72,64]{1,0:T(8,128)S(1)}, u32[]{:S(2)}, u32[]{:S(2)}) collective-permute-start(f32[72,64]{1,0:T(8,128)S(1)} %copy-done), channel_id=1, source_target_pairs={{0,8},{8,0},{1,9},{9,1},{2,10},{10,2},{3,11},{11,3},{4,12},{12,4},... | collective-permute-start | bytes 55304 | tf_op jit(solution)/shard_map/ppermute | solution.py:359
  11.4 8.6 %collective-permute-done.refs_2_ = f32[72,64]{1,0:T(8,128)S(1)} collective-permute-done((f32[72,64]{1,0:T(8,128)S(1)}, f32[72,64]{1,0:T(8,128)S(1)}, u32[]{:S(2)}, u32[]{:S(2)}) %collective-permute-start) | collective-permute-done | bytes 18464 | tf_op jit(solution)/shard_map/ppermute | solution.py:359
  20.0 0.6 %all-to-all-done.recv_ref = bf16[16,144,128]{2,1,0:T(8,128)(2,1)S(1)} async-done(((bf16[16,144,128]{2,1,0:T(8,128)(2,1)}), bf16[16,144,128]{2,1,0:T(8,128)(2,1)S(1)}, u32[]{:S(2)}, u32[]{:S(2)}) %all-to-all-start) | async-done | bytes 589856 | tf_op jit(solution)/shard_map/all_to_all | solution.py:348
  20.6 3.8 %shard_map.95 = (f32[8,2,144,128]{3,2,1,0:T(8,128)S(1)}, f32[32,8,128]{2,1,0:T(8,128)}) custom-call(bf16[16,144,128]{2,1,0:T(8,128)(2,1)S(1)} %all-to-all-done.recv_ref, bf16[2,256,512]{2,1,0:T(8,128)(2,1)S(1)} %copy-done.2, bf16[2,512,256]{2,1,0:T(8,128)(2,1)S(1)} %copy-done.1), custom_call_target="tpu_custom_call" | custom-call | flops 4294967296 | bytes 1048576 | tf_op jit(solution)/shard_map/pallas_call | solution.py:363
  24.4 5.0 %all-to-all-start.1 = ((f32[32,8,128]{2,1,0:T(8,128)}), f32[32,8,128]{2,1,0:T(8,128)S(1)}, u32[]{:S(2)}, u32[]{:S(2)}) async-start(f32[32,8,128]{2,1,0:T(8,128)} %get-tuple-element.16), calls=%async_computation.1 | async-start | bytes 262144 | tf_op jit(solution)/shard_map/all_to_all | solution.py:348
  29.4 3.2 %shard_map.96 = bf16[16,32,256]{2,1,0:T(8,128)(2,1)} custom-call(bf16[16,144,128]{2,1,0:T(8,128)(2,1)S(1)} %all-to-all-done.recv_ref, f32[8,2,144,128]{3,2,1,0:T(8,128)S(1)} %get-tuple-element.17.win_ref, bf16[2,256,512]{2,1,0:T(8,128)(2,1)S(1)} %copy-done.2, bf16[2,512,256]{2,1,0:T(8,128)(2,1)S(1)} %copy-done.1), custom_call_target="tpu_custom_call" | custom-call | flops 4294967296 | bytes 1048576 | tf_op jit(solution)/shard_map/pallas_call | solution.py:370
  32.6 4.7 %all-to-all-done.1.refs_0_.grad_ref = f32[32,8,128]{2,1,0:T(8,128)S(1)} async-done(((f32[32,8,128]{2,1,0:T(8,128)}), f32[32,8,128]{2,1,0:T(8,128)S(1)}, u32[]{:S(2)}, u32[]{:S(2)}) %all-to-all-start.1) | async-done | bytes 131104 | tf_op jit(solution)/shard_map/all_to_all | solution.py:348
  37.3 0.3 shard_map.97
  37.6 2.0 %collective-permute-start.3 = (f32[64,256]{1,0:T(8,128)S(1)}, f32[64,256]{1,0:T(8,128)S(1)}, u32[]{:S(2)}, u32[]{:S(2)}) collective-permute-start(f32[64,256]{1,0:T(8,128)S(1)} %shard_map.97), channel_id=1, source_target_pairs={{0,3},{1,2},{2,1},{3,0},{4,7},{5,6},{6,5},{7,4},{8,11},{9,10},{10,... | collective-permute-start | bytes 196616 | tf_op jit(solution)/shard_map/ppermute | solution.py:320
  39.6 1.5 %collective-permute-start.2 = (f32[64,256]{1,0:T(8,128)S(1)}, f32[64,256]{1,0:T(8,128)S(1)}, u32[]{:S(2)}, u32[]{:S(2)}) collective-permute-start(f32[64,256]{1,0:T(8,128)S(1)} %shard_map.97), channel_id=1, source_target_pairs={{0,2},{1,3},{2,0},{3,1},{4,6},{5,7},{6,4},{7,5},{8,10},{9,11},{10,... | collective-permute-start | bytes 196616 | tf_op jit(solution)/shard_map/ppermute | solution.py:320
  41.1 1.4 %collective-permute-start.1 = (f32[64,256]{1,0:T(8,128)S(1)}, f32[64,256]{1,0:T(8,128)S(1)}, u32[]{:S(2)}, u32[]{:S(2)}) collective-permute-start(f32[64,256]{1,0:T(8,128)S(1)} %shard_map.97), channel_id=1, source_target_pairs={{0,1},{1,0},{2,3},{3,2},{4,5},{5,4},{6,7},{7,6},{8,9},{9,8},{10,11... | collective-permute-start | bytes 196616 | tf_op jit(solution)/shard_map/ppermute | solution.py:320
  42.4 3.5 %all-to-all-start.2 = ((bf16[16,32,256]{2,1,0:T(8,128)(2,1)}), bf16[16,32,256]{2,1,0:T(8,128)(2,1)S(1)}, u32[]{:S(2)}, u32[]{:S(2)}) async-start(bf16[16,32,256]{2,1,0:T(8,128)(2,1)} %shard_map.96), calls=%async_computation.2 | async-start | bytes 524288 | tf_op jit(solution)/shard_map/all_to_all | solution.py:348
  46.0 0.0 collective-permute-done.3
  46.0 0.0 collective-permute-done.2
  46.0 1.3 %collective-permute-done.1 = f32[64,256]{1,0:T(8,128)S(1)} collective-permute-done((f32[64,256]{1,0:T(8,128)S(1)}, f32[64,256]{1,0:T(8,128)S(1)}, u32[]{:S(2)}, u32[]{:S(2)}) %collective-permute-start.1) | collective-permute-done | bytes 65568 | tf_op jit(solution)/shard_map/ppermute | solution.py:320
  47.3 4.8 %collective-permute-start.4 = (f32[64,256]{1,0:T(8,128)S(1)}, f32[64,256]{1,0:T(8,128)S(1)}, u32[]{:S(2)}, u32[]{:S(2)}) collective-permute-start(f32[64,256]{1,0:T(8,128)S(1)} %add_add_fusion.near_ref), channel_id=1, source_target_pairs={{0,6},{1,7},{2,4},{3,5},{4,2},{5,3},{6,0},{7,1},{8,14},{9,15},{10,... | collective-permute-start | bytes 196616 | tf_op jit(solution)/shard_map/ppermute | solution.py:324
  52.1 2.9 %collective-permute-done.4.far_ref = f32[64,256]{1,0:T(8,128)S(1)} collective-permute-done((f32[64,256]{1,0:T(8,128)S(1)}, f32[64,256]{1,0:T(8,128)S(1)}, u32[]{:S(2)}, u32[]{:S(2)}) %collective-permute-start.4) | collective-permute-done | bytes 65568 | tf_op jit(solution)/shard_map/ppermute | solution.py:324
  55.0 0.0 all-to-all-done.2.recv_ref
  55.0 0.9 %shard_map.98 = (bf16[64,2048]{1,0:T(8,128)(2,1)}, f32[64,256]{1,0:T(8,128)}, f32[64,256]{1,0:T(8,128)}) custom-call(bf16[16,32,256]{2,1,0:T(8,128)(2,1)S(1)} %all-to-all-done.2.recv_ref, f32[32,8,128]{2,1,0:T(8,128)S(1)} %all-to-all-done.1.refs_0_.grad_ref, f32[64,256]{1,0:T(8,128)S(1)} %add_add_fusion.near_ref, f32[64,256]{1,0:T(8,128)S(1)} %collective-permute-done.4.far_ref), custom_call_target="tpu_custom_call" | custom-call | flops 4194304 | bytes 1048576 | tf_op jit(solution)/shard_map/pallas_call | solution.py:385
  (4 shorter events, 0.0 us)
Async XLA Ops:
  0.6 20.0 %copy-start.1 = (bf16[2,512,256]{2,1,0:T(8,128)(2,1)S(1)}, bf16[2,512,256]{2,1,0:T(8,128)(2,1)}, u32[]{:S(2)}) copy-start(bf16[2,512,256]{2,1,0:T(8,128)(2,1)} %constant.5.clone.inv_ref) | copy-start | bytes 1572868
  0.6 19.9 %copy-start.2 = (bf16[2,256,512]{2,1,0:T(8,128)(2,1)S(1)}, bf16[2,256,512]{2,1,0:T(8,128)(2,1)}, u32[]{:S(2)}) copy-start(bf16[2,256,512]{2,1,0:T(8,128)(2,1)} %constant.4.clone.fwd_ref) | copy-start | bytes 1572868
  3.0 5.5 %copy-start = (f32[72,64]{1,0:T(8,128)S(1)}, f32[72,64]{1,0:T(8,128)}, u32[]{:S(2)}) copy-start(f32[72,64]{1,0:T(8,128)} %get-tuple-element.14.refs_1_) | copy-start | bytes 55300
  3.1 17.5 %all-to-all-start = ((bf16[16,144,128]{2,1,0:T(8,128)(2,1)}), bf16[16,144,128]{2,1,0:T(8,128)(2,1)S(1)}, u32[]{:S(2)}, u32[]{:S(2)}) async-start(bf16[16,144,128]{2,1,0:T(8,128)(2,1)} %get-tuple-element.13), calls=%async_computation | async-start | bytes 1179648 | tf_op jit(solution)/shard_map/all_to_all | solution.py:348
  8.6 11.4 %collective-permute-start = (f32[72,64]{1,0:T(8,128)S(1)}, f32[72,64]{1,0:T(8,128)S(1)}, u32[]{:S(2)}, u32[]{:S(2)}) collective-permute-start(f32[72,64]{1,0:T(8,128)S(1)} %copy-done), channel_id=1, source_target_pairs={{0,8},{8,0},{1,9},{9,1},{2,10},{10,2},{3,11},{11,3},{4,12},{12,4},... | collective-permute-start | bytes 55304 | tf_op jit(solution)/shard_map/ppermute | solution.py:359
  24.4 12.9 %all-to-all-start.1 = ((f32[32,8,128]{2,1,0:T(8,128)}), f32[32,8,128]{2,1,0:T(8,128)S(1)}, u32[]{:S(2)}, u32[]{:S(2)}) async-start(f32[32,8,128]{2,1,0:T(8,128)} %get-tuple-element.16), calls=%async_computation.1 | async-start | bytes 262144 | tf_op jit(solution)/shard_map/all_to_all | solution.py:348
  37.6 8.4 %collective-permute-start.3 = (f32[64,256]{1,0:T(8,128)S(1)}, f32[64,256]{1,0:T(8,128)S(1)}, u32[]{:S(2)}, u32[]{:S(2)}) collective-permute-start(f32[64,256]{1,0:T(8,128)S(1)} %shard_map.97), channel_id=1, source_target_pairs={{0,3},{1,2},{2,1},{3,0},{4,7},{5,6},{6,5},{7,4},{8,11},{9,10},{10,... | collective-permute-start | bytes 196616 | tf_op jit(solution)/shard_map/ppermute | solution.py:320
  39.6 6.4 %collective-permute-start.2 = (f32[64,256]{1,0:T(8,128)S(1)}, f32[64,256]{1,0:T(8,128)S(1)}, u32[]{:S(2)}, u32[]{:S(2)}) collective-permute-start(f32[64,256]{1,0:T(8,128)S(1)} %shard_map.97), channel_id=1, source_target_pairs={{0,2},{1,3},{2,0},{3,1},{4,6},{5,7},{6,4},{7,5},{8,10},{9,11},{10,... | collective-permute-start | bytes 196616 | tf_op jit(solution)/shard_map/ppermute | solution.py:320
  41.1 6.2 %collective-permute-start.1 = (f32[64,256]{1,0:T(8,128)S(1)}, f32[64,256]{1,0:T(8,128)S(1)}, u32[]{:S(2)}, u32[]{:S(2)}) collective-permute-start(f32[64,256]{1,0:T(8,128)S(1)} %shard_map.97), channel_id=1, source_target_pairs={{0,1},{1,0},{2,3},{3,2},{4,5},{5,4},{6,7},{7,6},{8,9},{9,8},{10,11... | collective-permute-start | bytes 196616 | tf_op jit(solution)/shard_map/ppermute | solution.py:320
  42.4 12.6 %all-to-all-start.2 = ((bf16[16,32,256]{2,1,0:T(8,128)(2,1)}), bf16[16,32,256]{2,1,0:T(8,128)(2,1)S(1)}, u32[]{:S(2)}, u32[]{:S(2)}) async-start(bf16[16,32,256]{2,1,0:T(8,128)(2,1)} %shard_map.96), calls=%async_computation.2 | async-start | bytes 524288 | tf_op jit(solution)/shard_map/all_to_all | solution.py:348
  47.3 7.7 %collective-permute-start.4 = (f32[64,256]{1,0:T(8,128)S(1)}, f32[64,256]{1,0:T(8,128)S(1)}, u32[]{:S(2)}, u32[]{:S(2)}) collective-permute-start(f32[64,256]{1,0:T(8,128)S(1)} %add_add_fusion.near_ref), channel_id=1, source_target_pairs={{0,6},{1,7},{2,4},{3,5},{4,2},{5,3},{6,0},{7,1},{8,14},{9,15},{10,... | collective-permute-start | bytes 196616 | tf_op jit(solution)/shard_map/ppermute | solution.py:324

commit v6 on v5

--- a/solution.py
+++ b/solution.py
@@ -356,8 +356,7 @@
         (features, projection, decay_rates.reshape(1, channels), cotangent, inputs),
         60 * 1024 * 1024,
     )(features, projection, decay_rates.reshape(1, channels), cotangent, inputs)
-    other = lax.ppermute(both, "x_hi", [(0, 1), (1, 0)])
-    received, other = lax.optimization_barrier((exchanged(payload, "ctx"), other))
+    received = exchanged(payload, "ctx")
     blocks = groups * subs
     mixed = (2 * per, 2, blocks + lags, LANES)
     windows, tap_grads = call(
@@ -366,6 +365,8 @@
         [(per, 4, blocks + subs, LANES), (6 * per, blocks, LANES), mixed, (6 * per, lags * subs, LANES), (4, per * lags, LANES)],
         1 << 32,
     )(received, forward, backward)
+    tap_grads, both = lax.optimization_barrier((tap_grads, both))
+    other = lax.ppermute(both, "x_hi", [(0, 1), (1, 0)])
     tap_grads = exchanged(tap_grads, ("ctx", "x_hi"))
     x_parts = call(
         inputs_kernel,
@@ -373,7 +374,7 @@
         [(groups * 16, LANES), (6 * per, lags, LANES), mixed, (6 * per, blocks, LANES)],
         1 << 32,
     )(received, windows, forward, backward)
-    tap_grads, x_parts = lax.optimization_barrier((tap_grads, x_parts))
+    tap_grads, x_parts, other = lax.optimization_barrier((tap_grads, x_parts, other))
     part = call(
         lambda *refs: features_kernel(taps, *refs),
         shape((order, tap_rows), F32),

time: 56.4 us -> 56.2 us (level)
  blocking collectives: 0 us -> 17.1 us
  waiting for transfers between devices: 18.1 us -> 5.87 us
  starting transfers between devices: 26.5 us -> 21.6 us
    all_to_all x0 -> x1, blocking collectives: none -> 17.1 us  [exchanged(): return lax.all_to_all(values, axes, 0, 0, tiled=True)]
    ppermute x1, waiting for transfers between devices: 8.56 us -> 0.01 us  [shards(): other = lax.ppermute(both, 'x_hi', [(0, 1), (1, 0)])]
    all_to_all x3 -> x2, starting transfers between devices: 14 us -> 8.62 us  [exchanged(): return lax.all_to_all(values, axes, 0, 0, tiled=True)]
    all_to_all x3 -> x2, waiting for transfers between devices: 5.32 us -> 1.5 us  [exchanged(): return lax.all_to_all(values, axes, 0, 0, tiled=True)]
  transfers between devices with their start and end apart: 8 -> 7, of which waited for: 5 -> 3; matrix products, arithmetic and copies ran while one was open for 0% -> 0% of each run, Pallas kernels for 6% -> 6%
where the time goes in v6:
time: 56.2 us; the launch traced here: 55.8 us
  starting transfers between devices  21.6 us (38%)
  blocking collectives  17.1 us (30%)
  Pallas kernels  10.5 us (19%)
  waiting for transfers between devices  5.87 us (10%)
  between operations  0.71 us (1%)
    all_to_all x1, blocking collectives, exchanged(): return lax.all_to_all(values, axes, 0, 0, tiled=True)  17.1 us
    all_to_all x2, starting transfers between devices, exchanged(): return lax.all_to_all(values, axes, 0, 0, tiled=True)  8.62 us
    ppermute x3, starting transfers between devices, swapped(): lax.ppermute(values, axis, [(i, i ^ mask) for i in range(lax.axis_size(ax...  4.83 us
    ppermute x1, starting transfers between devices, paired(): return lax.ppermute(values, axis, list(enumerate(partner)))  4.74 us
    pallas_call x1, Pallas kernels, shards(): call(taps_kernel, (shape((2 * per, 2, blocks + lags, LANES), F32), shape(...  3.75 us
    ppermute x1, starting transfers between devices, shards(): other = lax.ppermute(both, 'x_hi', [(0, 1), (1, 0)])  3.38 us
    pallas_call x1, Pallas kernels, shards(): call(inputs_kernel, shape((groups, per * subs, SUB), BF16), [(groups * 16...  3.25 us
    ppermute x1, waiting for transfers between devices, paired(): return lax.ppermute(values, axis, list(enumerate(partner)))  2.99 us
  transfers between devices with their start and end apart: 7, of which 3 were waited for; matrix products, arithmetic and copies ran while one was open for 0% of the time, Pallas kernels for 6%

profile of v6, /device:TPU:32, one launch (start us, length us, event | category | flops | bytes accessed | tf_op | source)
XLA Modules:
  0.0 55.8 jit_solution(16160465880532969261)
XLA Ops:
  0.6 0.0 copy-start.1
  0.6 0.0 copy-start.2
  0.7 2.4 %shard_map.94 = (bf16[16,144,128]{2,1,0:T(8,128)(2,1)}, f32[72,64]{1,0:T(8,128)}) custom-call(f32[64,256]{1,0:T(8,128)} %refs_0_.1, f32[64,64]{1,0:T(8,128)} %refs_1_.1, f32[1,64]{1,0:T(1,128)} %bitcast.1, bf16[64,2048]{1,0:T(8,128)(2,1)} %refs_3_.1, bf16[64,2048]{1,0:T(8,128)(2,1)} %refs_4_.1), custom_call_target="tpu_custom_call" | custom-call | flops 4194304 | bytes 1048576 | tf_op jit(solution)/shard_map/pallas_call | solution.py:351
  3.0 17.1 %all_to_all.15.recv_ref = bf16[16,144,128]{2,1,0:T(8,128)(2,1)S(1)} all-to-all(bf16[16,144,128]{2,1,0:T(8,128)(2,1)} %get-tuple-element.14), channel_id=1, replica_groups=mesh['ctx'=16,'x_hi'=2,'z'=8] {'ctx'}, dimensions={0} | all-to-all | bytes 1179648 | tf_op jit(solution)/shard_map/all_to_all | solution.py:348
  20.1 0.0 copy-done.1
  20.1 0.0 copy-done.2
  20.2 3.8 %shard_map.95 = (f32[8,2,144,128]{3,2,1,0:T(8,128)S(1)}, f32[32,8,128]{2,1,0:T(8,128)}) custom-call(bf16[16,144,128]{2,1,0:T(8,128)(2,1)S(1)} %all_to_all.15.recv_ref, bf16[2,256,512]{2,1,0:T(8,128)(2,1)S(1)} %copy-done.2, bf16[2,512,256]{2,1,0:T(8,128)(2,1)S(1)} %copy-done.1), custom_call_target="tpu_custom_call" | custom-call | flops 4294967296 | bytes 1048576 | tf_op jit(solution)/shard_map/pallas_call | solution.py:362
  23.9 5.1 %all-to-all-start.1 = ((f32[32,8,128]{2,1,0:T(8,128)}), f32[32,8,128]{2,1,0:T(8,128)S(1)}, u32[]{:S(2)}, u32[]{:S(2)}) async-start(f32[32,8,128]{2,1,0:T(8,128)} %get-tuple-element.17), calls=%async_computation.1 | async-start | bytes 262144 | tf_op jit(solution)/shard_map/all_to_all | solution.py:348
  29.0 3.4 %collective-permute-start = (f32[72,64]{1,0:T(8,128)S(1)}, f32[72,64]{1,0:T(8,128)S(1)}, u32[]{:S(2)}, u32[]{:S(2)}) collective-permute-start(f32[72,64]{1,0:T(8,128)S(1)} %copy-done), channel_id=1, source_target_pairs={{0,8},{8,0},{1,9},{9,1},{2,10},{10,2},{3,11},{11,3},{4,12},{12,4},... | collective-permute-start | bytes 55304 | tf_op jit(solution)/shard_map/ppermute | solution.py:369
  32.4 3.3 %shard_map.96 = bf16[16,32,256]{2,1,0:T(8,128)(2,1)} custom-call(bf16[16,144,128]{2,1,0:T(8,128)(2,1)S(1)} %all_to_all.15.recv_ref, f32[8,2,144,128]{3,2,1,0:T(8,128)S(1)} %get-tuple-element.18.win_ref, bf16[2,256,512]{2,1,0:T(8,128)(2,1)S(1)} %copy-done.2, bf16[2,512,256]{2,1,0:T(8,128)(2,1)S(1)} %copy-done.1), custom_call_target="tpu_custom_call" | custom-call | flops 4294967296 | bytes 1048576 | tf_op jit(solution)/shard_map/pallas_call | solution.py:371
  35.6 0.0 collective-permute-done.refs_2_
  35.7 1.5 %all-to-all-done.1.refs_0_.grad_ref = f32[32,8,128]{2,1,0:T(8,128)S(1)} async-done(((f32[32,8,128]{2,1,0:T(8,128)}), f32[32,8,128]{2,1,0:T(8,128)S(1)}, u32[]{:S(2)}, u32[]{:S(2)}) %all-to-all-start.1) | async-done | bytes 131104 | tf_op jit(solution)/shard_map/all_to_all | solution.py:348
  37.1 0.3 shard_map.97
  37.4 2.0 %collective-permute-start.3 = (f32[64,256]{1,0:T(8,128)S(1)}, f32[64,256]{1,0:T(8,128)S(1)}, u32[]{:S(2)}, u32[]{:S(2)}) collective-permute-start(f32[64,256]{1,0:T(8,128)S(1)} %shard_map.97), channel_id=1, source_target_pairs={{0,3},{1,2},{2,1},{3,0},{4,7},{5,6},{6,5},{7,4},{8,11},{9,10},{10,... | collective-permute-start | bytes 196616 | tf_op jit(solution)/shard_map/ppermute | solution.py:320
  39.5 1.5 %collective-permute-start.2 = (f32[64,256]{1,0:T(8,128)S(1)}, f32[64,256]{1,0:T(8,128)S(1)}, u32[]{:S(2)}, u32[]{:S(2)}) collective-permute-start(f32[64,256]{1,0:T(8,128)S(1)} %shard_map.97), channel_id=1, source_target_pairs={{0,2},{1,3},{2,0},{3,1},{4,6},{5,7},{6,4},{7,5},{8,10},{9,11},{10,... | collective-permute-start | bytes 196616 | tf_op jit(solution)/shard_map/ppermute | solution.py:320
  40.9 1.4 %collective-permute-start.1 = (f32[64,256]{1,0:T(8,128)S(1)}, f32[64,256]{1,0:T(8,128)S(1)}, u32[]{:S(2)}, u32[]{:S(2)}) collective-permute-start(f32[64,256]{1,0:T(8,128)S(1)} %shard_map.97), channel_id=1, source_target_pairs={{0,1},{1,0},{2,3},{3,2},{4,5},{5,4},{6,7},{7,6},{8,9},{9,8},{10,11... | collective-permute-start | bytes 196616 | tf_op jit(solution)/shard_map/ppermute | solution.py:320
  42.3 3.5 %all-to-all-start.2 = ((bf16[16,32,256]{2,1,0:T(8,128)(2,1)}), bf16[16,32,256]{2,1,0:T(8,128)(2,1)S(1)}, u32[]{:S(2)}, u32[]{:S(2)}) async-start(bf16[16,32,256]{2,1,0:T(8,128)(2,1)} %shard_map.96), calls=%async_computation.2 | async-start | bytes 524288 | tf_op jit(solution)/shard_map/all_to_all | solution.py:348
  45.8 0.0 collective-permute-done.3
  45.8 0.0 collective-permute-done.2
  45.8 1.4 %collective-permute-done.1 = f32[64,256]{1,0:T(8,128)S(1)} collective-permute-done((f32[64,256]{1,0:T(8,128)S(1)}, f32[64,256]{1,0:T(8,128)S(1)}, u32[]{:S(2)}, u32[]{:S(2)}) %collective-permute-start.1) | collective-permute-done | bytes 65568 | tf_op jit(solution)/shard_map/ppermute | solution.py:320
  47.2 4.7 %collective-permute-start.4 = (f32[64,256]{1,0:T(8,128)S(1)}, f32[64,256]{1,0:T(8,128)S(1)}, u32[]{:S(2)}, u32[]{:S(2)}) collective-permute-start(f32[64,256]{1,0:T(8,128)S(1)} %add_add_fusion.near_ref), channel_id=1, source_target_pairs={{0,6},{1,7},{2,4},{3,5},{4,2},{5,3},{6,0},{7,1},{8,14},{9,15},{10,... | collective-permute-start | bytes 196616 | tf_op jit(solution)/shard_map/ppermute | solution.py:324
  52.0 3.0 %collective-permute-done.4.far_ref = f32[64,256]{1,0:T(8,128)S(1)} collective-permute-done((f32[64,256]{1,0:T(8,128)S(1)}, f32[64,256]{1,0:T(8,128)S(1)}, u32[]{:S(2)}, u32[]{:S(2)}) %collective-permute-start.4) | collective-permute-done | bytes 65568 | tf_op jit(solution)/shard_map/ppermute | solution.py:324
  55.0 0.0 all-to-all-done.2.recv_ref
  55.0 0.9 %shard_map.98 = (bf16[64,2048]{1,0:T(8,128)(2,1)}, f32[64,256]{1,0:T(8,128)}, f32[64,256]{1,0:T(8,128)}) custom-call(bf16[16,32,256]{2,1,0:T(8,128)(2,1)S(1)} %all-to-all-done.2.recv_ref, f32[32,8,128]{2,1,0:T(8,128)S(1)} %all-to-all-done.1.refs_0_.grad_ref, f32[64,256]{1,0:T(8,128)S(1)} %add_add_fusion.near_ref, f32[64,256]{1,0:T(8,128)S(1)} %collective-permute-done.4.far_ref), custom_call_target="tpu_custom_call" | custom-call | flops 4194304 | bytes 1048576 | tf_op jit(solution)/shard_map/pallas_call | solution.py:386
  (3 shorter events, 0.0 us)
Async XLA Ops:
  0.6 19.5 %copy-start.1 = (bf16[2,512,256]{2,1,0:T(8,128)(2,1)S(1)}, bf16[2,512,256]{2,1,0:T(8,128)(2,1)}, u32[]{:S(2)}) copy-start(bf16[2,512,256]{2,1,0:T(8,128)(2,1)} %constant.5.clone.inv_ref) | copy-start | bytes 1572868
  0.6 19.5 %copy-start.2 = (bf16[2,256,512]{2,1,0:T(8,128)(2,1)S(1)}, bf16[2,256,512]{2,1,0:T(8,128)(2,1)}, u32[]{:S(2)}) copy-start(bf16[2,256,512]{2,1,0:T(8,128)(2,1)} %constant.4.clone.fwd_ref) | copy-start | bytes 1572868
  20.1 8.9 %copy-start = (f32[72,64]{1,0:T(8,128)S(1)}, f32[72,64]{1,0:T(8,128)}, u32[]{:S(2)}) copy-start(f32[72,64]{1,0:T(8,128)} %get-tuple-element.19.refs_1_) | copy-start | bytes 55300
  23.9 13.2 %all-to-all-start.1 = ((f32[32,8,128]{2,1,0:T(8,128)}), f32[32,8,128]{2,1,0:T(8,128)S(1)}, u32[]{:S(2)}, u32[]{:S(2)}) async-start(f32[32,8,128]{2,1,0:T(8,128)} %get-tuple-element.17), calls=%async_computation.1 | async-start | bytes 262144 | tf_op jit(solution)/shard_map/all_to_all | solution.py:348
  29.0 6.6 %collective-permute-start = (f32[72,64]{1,0:T(8,128)S(1)}, f32[72,64]{1,0:T(8,128)S(1)}, u32[]{:S(2)}, u32[]{:S(2)}) collective-permute-start(f32[72,64]{1,0:T(8,128)S(1)} %copy-done), channel_id=1, source_target_pairs={{0,8},{8,0},{1,9},{9,1},{2,10},{10,2},{3,11},{11,3},{4,12},{12,4},... | collective-permute-start | bytes 55304 | tf_op jit(solution)/shard_map/ppermute | solution.py:369
  37.4 8.4 %collective-permute-start.3 = (f32[64,256]{1,0:T(8,128)S(1)}, f32[64,256]{1,0:T(8,128)S(1)}, u32[]{:S(2)}, u32[]{:S(2)}) collective-permute-start(f32[64,256]{1,0:T(8,128)S(1)} %shard_map.97), channel_id=1, source_target_pairs={{0,3},{1,2},{2,1},{3,0},{4,7},{5,6},{6,5},{7,4},{8,11},{9,10},{10,... | collective-permute-start | bytes 196616 | tf_op jit(solution)/shard_map/ppermute | solution.py:320
  39.5 6.4 %collective-permute-start.2 = (f32[64,256]{1,0:T(8,128)S(1)}, f32[64,256]{1,0:T(8,128)S(1)}, u32[]{:S(2)}, u32[]{:S(2)}) collective-permute-start(f32[64,256]{1,0:T(8,128)S(1)} %shard_map.97), channel_id=1, source_target_pairs={{0,2},{1,3},{2,0},{3,1},{4,6},{5,7},{6,4},{7,5},{8,10},{9,11},{10,... | collective-permute-start | bytes 196616 | tf_op jit(solution)/shard_map/ppermute | solution.py:320
  40.9 6.3 %collective-permute-start.1 = (f32[64,256]{1,0:T(8,128)S(1)}, f32[64,256]{1,0:T(8,128)S(1)}, u32[]{:S(2)}, u32[]{:S(2)}) collective-permute-start(f32[64,256]{1,0:T(8,128)S(1)} %shard_map.97), channel_id=1, source_target_pairs={{0,1},{1,0},{2,3},{3,2},{4,5},{5,4},{6,7},{7,6},{8,9},{9,8},{10,11... | collective-permute-start | bytes 196616 | tf_op jit(solution)/shard_map/ppermute | solution.py:320
  42.3 12.7 %all-to-all-start.2 = ((bf16[16,32,256]{2,1,0:T(8,128)(2,1)}), bf16[16,32,256]{2,1,0:T(8,128)(2,1)S(1)}, u32[]{:S(2)}, u32[]{:S(2)}) async-start(bf16[16,32,256]{2,1,0:T(8,128)(2,1)} %shard_map.96), calls=%async_computation.2 | async-start | bytes 524288 | tf_op jit(solution)/shard_map/all_to_all | solution.py:348
  47.2 7.7 %collective-permute-start.4 = (f32[64,256]{1,0:T(8,128)S(1)}, f32[64,256]{1,0:T(8,128)S(1)}, u32[]{:S(2)}, u32[]{:S(2)}) collective-permute-start(f32[64,256]{1,0:T(8,128)S(1)} %add_add_fusion.near_ref), channel_id=1, source_target_pairs={{0,6},{1,7},{2,4},{3,5},{4,2},{5,3},{6,0},{7,1},{8,14},{9,15},{10,... | collective-permute-start | bytes 196616 | tf_op jit(solution)/shard_map/ppermute | solution.py:324

commit v7 on v6

--- a/solution.py
+++ b/solution.py
@@ -39,7 +39,9 @@
 
 def dot_terms(values, table):
     high, low = two_terms(values)
-    return dot(high, table[0]) + dot(high, table[1]) + dot(low, table[0])
+    both = table[...]
+    terms = both.reshape(both.shape[0] * both.shape[1], both.shape[2])
+    return dot(jnp.concatenate([high, high], axis=1), terms) + dot(low, table[0])
 
 
 def decay_of(rates, tap_rows, taps):
@@ -108,7 +110,8 @@
             for half in range(2)
         ]
         left = jnp.concatenate(halves, axis=1)
-        result = dot(left, table_ref[0]) + dot(left, table_ref[1])
+        pair = jnp.concatenate([left, left], axis=1)
+        result = dot(pair, table_ref[...].reshape(2 * SUB, 2 * SUB))
         for src in range(step):
             for chan in range(per):
                 row = (src * per + chan) * subs
@@ -193,8 +196,8 @@
     for lag in range(lags):
         own = slice(lag * per, (lag + 1) * per)
         for copy in range(2):
-            grad_ref[2 * lag + copy, 0:per, :] = result[own, 0:LANES]
-            grad_ref[2 * lag + copy, per : 2 * per, :] = result[own, LANES:]
+            grad_ref[copy * lags + lag, 0:per, :] = result[own, 0:LANES]
+            grad_ref[copy * lags + lag, per : 2 * per, :] = result[own, LANES:]
 
 
 def inputs_kernel(recv_ref, win_ref, fwd_ref, inv_ref, grad_ref, frows, fspec, mixed, spec):
@@ -268,7 +271,7 @@
     for which, both in enumerate((mine_ref, other_ref)):
         for group in range(groups):
             own = slice(group * per, (group + 1) * per)
-            source = 2 * group + (1 - me if which else me)
+            source = groups * (1 - me if which else me) + group
             held[which, own, 0:LANES] = grad_ref[source, 0:per, :]
             held[which, own, LANES:] = grad_ref[source, per : 2 * per, :]
         decay = decay_of(both[order : order + 1, :], tap_rows, taps)
@@ -288,8 +291,8 @@
     feature_ref[...] = near_ref[...] + far_ref[...]
     for group in range(groups):
         own = slice(group * per, (group + 1) * per)
-        filter_ref[own, 0:LANES] = grad_ref[2 * group + me, 0:per, :]
-        filter_ref[own, LANES:] = grad_ref[2 * group + me, per : 2 * per, :]
+        filter_ref[own, 0:LANES] = grad_ref[groups * me + group, 0:per, :]
+        filter_ref[own, LANES:] = grad_ref[groups * me + group, per : 2 * per, :]
         block = recv_ref[group].astype(F32)
         for half in range(2):
             rows[half, group * span : (group + 1) * span, :] = block[:, half * LANES : (half + 1) * LANES]
@@ -367,7 +370,7 @@
     )(received, forward, backward)
     tap_grads, both = lax.optimization_barrier((tap_grads, both))
     other = lax.ppermute(both, "x_hi", [(0, 1), (1, 0)])
-    tap_grads = exchanged(tap_grads, ("ctx", "x_hi"))
+    tap_grads = exchanged(tap_grads, ("x_hi", "ctx"))
     x_parts = call(
         inputs_kernel,
         shape((groups, per * subs, SUB), BF16),

time: 56.2 us -> 56.1 us (level)
  no operation moved by 1% of the time
where the time goes in v7:
time: 56.1 us; the launch traced here: 55.8 us
  starting transfers between devices  21.4 us (38%)
  blocking collectives  17.1 us (30%)
  Pallas kernels  10.6 us (19%)
  waiting for transfers between devices  5.95 us (11%)
  between operations  0.71 us (1%)
    all_to_all x1, blocking collectives, exchanged(): return lax.all_to_all(values, axes, 0, 0, tiled=True)  17.1 us
    all_to_all x2, starting transfers between devices, exchanged(): return lax.all_to_all(values, axes, 0, 0, tiled=True)  8.62 us
    ppermute x3, starting transfers between devices, swapped(): lax.ppermute(values, axis, [(i, i ^ mask) for i in range(lax.axis_size(ax...  4.82 us
    ppermute x1, starting transfers between devices, paired(): return lax.ppermute(values, axis, list(enumerate(partner)))  4.58 us
    pallas_call x1, Pallas kernels, shards(): call(taps_kernel, (shape((2 * per, 2, blocks + lags, LANES), F32), shape(...  3.76 us
    ppermute x1, starting transfers between devices, shards(): other = lax.ppermute(both, 'x_hi', [(0, 1), (1, 0)])  3.39 us
    pallas_call x1, Pallas kernels, shards(): call(inputs_kernel, shape((groups, per * subs, SUB), BF16), [(groups * 16...  3.27 us
    ppermute x1, waiting for transfers between devices, paired(): return lax.ppermute(values, axis, list(enumerate(partner)))  3.02 us
  transfers between devices with their start and end apart: 7, of which 3 were waited for; matrix products, arithmetic and copies ran while one was open for 0% of the time, Pallas kernels for 6%

profile of v7, /device:TPU:32, one launch (start us, length us, event | category | flops | bytes accessed | tf_op | source)
XLA Modules:
  0.0 55.8 jit_solution(3566450335845592036)
XLA Ops:
  0.6 0.0 copy-start.1
  0.6 0.0 copy-start.2
  0.7 2.4 %shard_map.94 = (bf16[16,144,128]{2,1,0:T(8,128)(2,1)}, f32[72,64]{1,0:T(8,128)}) custom-call(f32[64,256]{1,0:T(8,128)} %refs_0_.1, f32[64,64]{1,0:T(8,128)} %refs_1_.1, f32[1,64]{1,0:T(1,128)} %bitcast.1, bf16[64,2048]{1,0:T(8,128)(2,1)} %refs_3_.1, bf16[64,2048]{1,0:T(8,128)(2,1)} %refs_4_.1), custom_call_target="tpu_custom_call" | custom-call | flops 4194304 | bytes 1048576 | tf_op jit(solution)/shard_map/pallas_call | solution.py:354
  3.0 17.1 %all_to_all.15.recv_ref = bf16[16,144,128]{2,1,0:T(8,128)(2,1)S(1)} all-to-all(bf16[16,144,128]{2,1,0:T(8,128)(2,1)} %get-tuple-element.14), channel_id=1, replica_groups=mesh['ctx'=16,'x_hi'=2,'z'=8] {'ctx'}, dimensions={0} | all-to-all | bytes 1179648 | tf_op jit(solution)/shard_map/all_to_all | solution.py:351
  20.1 0.0 copy-done.1
  20.1 0.0 copy-done.2
  20.2 3.8 %shard_map.95 = (f32[8,2,144,128]{3,2,1,0:T(8,128)S(1)}, f32[32,8,128]{2,1,0:T(8,128)}) custom-call(bf16[16,144,128]{2,1,0:T(8,128)(2,1)S(1)} %all_to_all.15.recv_ref, bf16[2,256,512]{2,1,0:T(8,128)(2,1)S(1)} %copy-done.2, bf16[2,512,256]{2,1,0:T(8,128)(2,1)S(1)} %copy-done.1), custom_call_target="tpu_custom_call" | custom-call | flops 4294967296 | bytes 1048576 | tf_op jit(solution)/shard_map/pallas_call | solution.py:365
  23.9 5.1 %all-to-all-start.1 = ((f32[32,8,128]{2,1,0:T(8,128)}), f32[32,8,128]{2,1,0:T(8,128)S(1)}, u32[]{:S(2)}, u32[]{:S(2)}) async-start(f32[32,8,128]{2,1,0:T(8,128)} %get-tuple-element.17), calls=%async_computation.1 | async-start | bytes 262144 | tf_op jit(solution)/shard_map/all_to_all | solution.py:351
  29.0 3.4 %collective-permute-start = (f32[72,64]{1,0:T(8,128)S(1)}, f32[72,64]{1,0:T(8,128)S(1)}, u32[]{:S(2)}, u32[]{:S(2)}) collective-permute-start(f32[72,64]{1,0:T(8,128)S(1)} %copy-done), channel_id=1, source_target_pairs={{0,8},{8,0},{1,9},{9,1},{2,10},{10,2},{3,11},{11,3},{4,12},{12,4},... | collective-permute-start | bytes 55304 | tf_op jit(solution)/shard_map/ppermute | solution.py:372
  32.4 3.3 %shard_map.96 = bf16[16,32,256]{2,1,0:T(8,128)(2,1)} custom-call(bf16[16,144,128]{2,1,0:T(8,128)(2,1)S(1)} %all_to_all.15.recv_ref, f32[8,2,144,128]{3,2,1,0:T(8,128)S(1)} %get-tuple-element.18.win_ref, bf16[2,256,512]{2,1,0:T(8,128)(2,1)S(1)} %copy-done.2, bf16[2,512,256]{2,1,0:T(8,128)(2,1)S(1)} %copy-done.1), custom_call_target="tpu_custom_call" | custom-call | flops 4294967296 | bytes 1048576 | tf_op jit(solution)/shard_map/pallas_call | solution.py:374
  35.7 0.0 collective-permute-done.refs_2_
  35.7 1.3 %all-to-all-done.1.refs_0_.grad_ref = f32[32,8,128]{2,1,0:T(8,128)S(1)} async-done(((f32[32,8,128]{2,1,0:T(8,128)}), f32[32,8,128]{2,1,0:T(8,128)S(1)}, u32[]{:S(2)}, u32[]{:S(2)}) %all-to-all-start.1) | async-done | bytes 131104 | tf_op jit(solution)/shard_map/all_to_all | solution.py:351
  37.0 0.3 shard_map.97
  37.3 2.0 %collective-permute-start.3 = (f32[64,256]{1,0:T(8,128)S(1)}, f32[64,256]{1,0:T(8,128)S(1)}, u32[]{:S(2)}, u32[]{:S(2)}) collective-permute-start(f32[64,256]{1,0:T(8,128)S(1)} %shard_map.97), channel_id=1, source_target_pairs={{0,3},{1,2},{2,1},{3,0},{4,7},{5,6},{6,5},{7,4},{8,11},{9,10},{10,... | collective-permute-start | bytes 196616 | tf_op jit(solution)/shard_map/ppermute | solution.py:323
  39.3 1.4 %collective-permute-start.2 = (f32[64,256]{1,0:T(8,128)S(1)}, f32[64,256]{1,0:T(8,128)S(1)}, u32[]{:S(2)}, u32[]{:S(2)}) collective-permute-start(f32[64,256]{1,0:T(8,128)S(1)} %shard_map.97), channel_id=1, source_target_pairs={{0,2},{1,3},{2,0},{3,1},{4,6},{5,7},{6,4},{7,5},{8,10},{9,11},{10,... | collective-permute-start | bytes 196616 | tf_op jit(solution)/shard_map/ppermute | solution.py:323
  40.7 1.4 %collective-permute-start.1 = (f32[64,256]{1,0:T(8,128)S(1)}, f32[64,256]{1,0:T(8,128)S(1)}, u32[]{:S(2)}, u32[]{:S(2)}) collective-permute-start(f32[64,256]{1,0:T(8,128)S(1)} %shard_map.97), channel_id=1, source_target_pairs={{0,1},{1,0},{2,3},{3,2},{4,5},{5,4},{6,7},{7,6},{8,9},{9,8},{10,11... | collective-permute-start | bytes 196616 | tf_op jit(solution)/shard_map/ppermute | solution.py:323
  42.1 3.5 %all-to-all-start.2 = ((bf16[16,32,256]{2,1,0:T(8,128)(2,1)}), bf16[16,32,256]{2,1,0:T(8,128)(2,1)S(1)}, u32[]{:S(2)}, u32[]{:S(2)}) async-start(bf16[16,32,256]{2,1,0:T(8,128)(2,1)} %shard_map.96), calls=%async_computation.2 | async-start | bytes 524288 | tf_op jit(solution)/shard_map/all_to_all | solution.py:351
  45.7 0.0 collective-permute-done.3
  45.7 0.0 collective-permute-done.2
  45.7 1.6 %collective-permute-done.1 = f32[64,256]{1,0:T(8,128)S(1)} collective-permute-done((f32[64,256]{1,0:T(8,128)S(1)}, f32[64,256]{1,0:T(8,128)S(1)}, u32[]{:S(2)}, u32[]{:S(2)}) %collective-permute-start.1) | collective-permute-done | bytes 65568 | tf_op jit(solution)/shard_map/ppermute | solution.py:323
  47.3 4.6 %collective-permute-start.4 = (f32[64,256]{1,0:T(8,128)S(1)}, f32[64,256]{1,0:T(8,128)S(1)}, u32[]{:S(2)}, u32[]{:S(2)}) collective-permute-start(f32[64,256]{1,0:T(8,128)S(1)} %add_add_fusion.near_ref), channel_id=1, source_target_pairs={{0,6},{1,7},{2,4},{3,5},{4,2},{5,3},{6,0},{7,1},{8,14},{9,15},{10,... | collective-permute-start | bytes 196616 | tf_op jit(solution)/shard_map/ppermute | solution.py:327
  51.9 3.0 %collective-permute-done.4.far_ref = f32[64,256]{1,0:T(8,128)S(1)} collective-permute-done((f32[64,256]{1,0:T(8,128)S(1)}, f32[64,256]{1,0:T(8,128)S(1)}, u32[]{:S(2)}, u32[]{:S(2)}) %collective-permute-start.4) | collective-permute-done | bytes 65568 | tf_op jit(solution)/shard_map/ppermute | solution.py:327
  54.9 0.0 all-to-all-done.2.recv_ref
  54.9 0.9 %shard_map.98 = (bf16[64,2048]{1,0:T(8,128)(2,1)}, f32[64,256]{1,0:T(8,128)}, f32[64,256]{1,0:T(8,128)}) custom-call(bf16[16,32,256]{2,1,0:T(8,128)(2,1)S(1)} %all-to-all-done.2.recv_ref, f32[32,8,128]{2,1,0:T(8,128)S(1)} %all-to-all-done.1.refs_0_.grad_ref, f32[64,256]{1,0:T(8,128)S(1)} %add_add_fusion.near_ref, f32[64,256]{1,0:T(8,128)S(1)} %collective-permute-done.4.far_ref), custom_call_target="tpu_custom_call" | custom-call | flops 4194304 | bytes 1048576 | tf_op jit(solution)/shard_map/pallas_call | solution.py:389
  (3 shorter events, 0.0 us)
Async XLA Ops:
  0.6 19.5 %copy-start.1 = (bf16[2,512,256]{2,1,0:T(8,128)(2,1)S(1)}, bf16[2,512,256]{2,1,0:T(8,128)(2,1)}, u32[]{:S(2)}) copy-start(bf16[2,512,256]{2,1,0:T(8,128)(2,1)} %constant.5.clone.inv_ref) | copy-start | bytes 1572868
  0.6 19.5 %copy-start.2 = (bf16[2,256,512]{2,1,0:T(8,128)(2,1)S(1)}, bf16[2,256,512]{2,1,0:T(8,128)(2,1)}, u32[]{:S(2)}) copy-start(bf16[2,256,512]{2,1,0:T(8,128)(2,1)} %constant.4.clone.fwd_ref) | copy-start | bytes 1572868
  20.1 8.9 %copy-start = (f32[72,64]{1,0:T(8,128)S(1)}, f32[72,64]{1,0:T(8,128)}, u32[]{:S(2)}) copy-start(f32[72,64]{1,0:T(8,128)} %get-tuple-element.19.refs_1_) | copy-start | bytes 55300
  23.9 13.1 %all-to-all-start.1 = ((f32[32,8,128]{2,1,0:T(8,128)}), f32[32,8,128]{2,1,0:T(8,128)S(1)}, u32[]{:S(2)}, u32[]{:S(2)}) async-start(f32[32,8,128]{2,1,0:T(8,128)} %get-tuple-element.17), calls=%async_computation.1 | async-start | bytes 262144 | tf_op jit(solution)/shard_map/all_to_all | solution.py:351
  29.0 6.7 %collective-permute-start = (f32[72,64]{1,0:T(8,128)S(1)}, f32[72,64]{1,0:T(8,128)S(1)}, u32[]{:S(2)}, u32[]{:S(2)}) collective-permute-start(f32[72,64]{1,0:T(8,128)S(1)} %copy-done), channel_id=1, source_target_pairs={{0,8},{8,0},{1,9},{9,1},{2,10},{10,2},{3,11},{11,3},{4,12},{12,4},... | collective-permute-start | bytes 55304 | tf_op jit(solution)/shard_map/ppermute | solution.py:372
  37.3 8.4 %collective-permute-start.3 = (f32[64,256]{1,0:T(8,128)S(1)}, f32[64,256]{1,0:T(8,128)S(1)}, u32[]{:S(2)}, u32[]{:S(2)}) collective-permute-start(f32[64,256]{1,0:T(8,128)S(1)} %shard_map.97), channel_id=1, source_target_pairs={{0,3},{1,2},{2,1},{3,0},{4,7},{5,6},{6,5},{7,4},{8,11},{9,10},{10,... | collective-permute-start | bytes 196616 | tf_op jit(solution)/shard_map/ppermute | solution.py:323
  39.3 6.4 %collective-permute-start.2 = (f32[64,256]{1,0:T(8,128)S(1)}, f32[64,256]{1,0:T(8,128)S(1)}, u32[]{:S(2)}, u32[]{:S(2)}) collective-permute-start(f32[64,256]{1,0:T(8,128)S(1)} %shard_map.97), channel_id=1, source_target_pairs={{0,2},{1,3},{2,0},{3,1},{4,6},{5,7},{6,4},{7,5},{8,10},{9,11},{10,... | collective-permute-start | bytes 196616 | tf_op jit(solution)/shard_map/ppermute | solution.py:323
  40.7 6.5 %collective-permute-start.1 = (f32[64,256]{1,0:T(8,128)S(1)}, f32[64,256]{1,0:T(8,128)S(1)}, u32[]{:S(2)}, u32[]{:S(2)}) collective-permute-start(f32[64,256]{1,0:T(8,128)S(1)} %shard_map.97), channel_id=1, source_target_pairs={{0,1},{1,0},{2,3},{3,2},{4,5},{5,4},{6,7},{7,6},{8,9},{9,8},{10,11... | collective-permute-start | bytes 196616 | tf_op jit(solution)/shard_map/ppermute | solution.py:323
  42.1 12.8 %all-to-all-start.2 = ((bf16[16,32,256]{2,1,0:T(8,128)(2,1)}), bf16[16,32,256]{2,1,0:T(8,128)(2,1)S(1)}, u32[]{:S(2)}, u32[]{:S(2)}) async-start(bf16[16,32,256]{2,1,0:T(8,128)(2,1)} %shard_map.96), calls=%async_computation.2 | async-start | bytes 524288 | tf_op jit(solution)/shard_map/all_to_all | solution.py:351
  47.3 7.6 %collective-permute-start.4 = (f32[64,256]{1,0:T(8,128)S(1)}, f32[64,256]{1,0:T(8,128)S(1)}, u32[]{:S(2)}, u32[]{:S(2)}) collective-permute-start(f32[64,256]{1,0:T(8,128)S(1)} %add_add_fusion.near_ref), channel_id=1, source_target_pairs={{0,6},{1,7},{2,4},{3,5},{4,2},{5,3},{6,0},{7,1},{8,14},{9,15},{10,... | collective-permute-start | bytes 196616 | tf_op jit(solution)/shard_map/ppermute | solution.py:327

commit v8 on v7

--- a/solution.py
+++ b/solution.py
@@ -331,7 +331,7 @@
 
 
 def halves_of_sum(values, axis):
-    near = [swapped(values, axis, mask) for mask in (1, 2, 3)]
+    near = [swapped(values, axis, mask) for mask in (3, 2, 1)]
     values = values + near[0] + near[1] + near[2]
     return values, paired(values, axis, FAR)
 

time: 56.1 us -> 56.7 us (1.011)
  waiting for transfers between devices: 5.95 us -> 7.52 us
  starting transfers between devices: 21.4 us -> 20.5 us
    ppermute x3, waiting for transfers between devices: 1.62 us -> 2.99 us  [swapped(): lax.ppermute(values, axis, [(i, i ^ mask) for i in range(lax.axis_size(ax...]
    ppermute x3, starting transfers between devices: 4.82 us -> 3.92 us  [swapped(): lax.ppermute(values, axis, [(i, i ^ mask) for i in range(lax.axis_size(ax...]
  transfers between devices with their start and end apart: 7 -> 7, of which waited for: 3 -> 4; matrix products, arithmetic and copies ran while one was open for 0% -> 0% of each run, Pallas kernels for 6% -> 6%
where the time goes in v8:
time: 56.7 us; the launch traced here: 56.4 us
  starting transfers between devices  20.5 us (36%)
  blocking collectives  17.1 us (30%)
  Pallas kernels  10.6 us (19%)
  waiting for transfers between devices  7.52 us (13%)
  between operations  0.71 us (1%)
    all_to_all x1, blocking collectives, exchanged(): return lax.all_to_all(values, axes, 0, 0, tiled=True)  17.1 us
    all_to_all x2, starting transfers between devices, exchanged(): return lax.all_to_all(values, axes, 0, 0, tiled=True)  8.62 us
    ppermute x1, starting transfers between devices, paired(): return lax.ppermute(values, axis, list(enumerate(partner)))  4.52 us
    ppermute x3, starting transfers between devices, swapped(): lax.ppermute(values, axis, [(i, i ^ mask) for i in range(lax.axis_size(ax...  3.92 us
    pallas_call x1, Pallas kernels, shards(): call(taps_kernel, (shape((2 * per, 2, blocks + lags, LANES), F32), shape(...  3.76 us
    ppermute x1, starting transfers between devices, shards(): other = lax.ppermute(both, 'x_hi', [(0, 1), (1, 0)])  3.39 us
    pallas_call x1, Pallas kernels, shards(): call(inputs_kernel, shape((groups, per * subs, SUB), BF16), [(groups * 16...  3.27 us
    ppermute x1, waiting for transfers between devices, paired(): return lax.ppermute(values, axis, list(enumerate(partner)))  3.22 us
  transfers between devices with their start and end apart: 7, of which 4 were waited for; matrix products, arithmetic and copies ran while one was open for 0% of the time, Pallas kernels for 6%

profile of v8, /device:TPU:32, one launch (start us, length us, event | category | flops | bytes accessed | tf_op | source)
XLA Modules:
  0.0 56.4 jit_solution(683901621450571462)
XLA Ops:
  0.6 0.0 copy-start.1
  0.6 0.0 copy-start.2
  0.7 2.4 %shard_map.94 = (bf16[16,144,128]{2,1,0:T(8,128)(2,1)}, f32[72,64]{1,0:T(8,128)}) custom-call(f32[64,256]{1,0:T(8,128)} %refs_0_.1, f32[64,64]{1,0:T(8,128)} %refs_1_.1, f32[1,64]{1,0:T(1,128)} %bitcast.1, bf16[64,2048]{1,0:T(8,128)(2,1)} %refs_3_.1, bf16[64,2048]{1,0:T(8,128)(2,1)} %refs_4_.1), custom_call_target="tpu_custom_call" | custom-call | flops 4194304 | bytes 1048576 | tf_op jit(solution)/shard_map/pallas_call | solution.py:354
  3.0 17.1 %all_to_all.15.recv_ref = bf16[16,144,128]{2,1,0:T(8,128)(2,1)S(1)} all-to-all(bf16[16,144,128]{2,1,0:T(8,128)(2,1)} %get-tuple-element.14), channel_id=1, replica_groups=mesh['ctx'=16,'x_hi'=2,'z'=8] {'ctx'}, dimensions={0} | all-to-all | bytes 1179648 | tf_op jit(solution)/shard_map/all_to_all | solution.py:351
  20.1 0.0 copy-done.1
  20.1 0.0 copy-done.2
  20.2 3.8 %shard_map.95 = (f32[8,2,144,128]{3,2,1,0:T(8,128)S(1)}, f32[32,8,128]{2,1,0:T(8,128)}) custom-call(bf16[16,144,128]{2,1,0:T(8,128)(2,1)S(1)} %all_to_all.15.recv_ref, bf16[2,256,512]{2,1,0:T(8,128)(2,1)S(1)} %copy-done.2, bf16[2,512,256]{2,1,0:T(8,128)(2,1)S(1)} %copy-done.1), custom_call_target="tpu_custom_call" | custom-call | flops 4294967296 | bytes 1048576 | tf_op jit(solution)/shard_map/pallas_call | solution.py:365
  23.9 5.1 %all-to-all-start.1 = ((f32[32,8,128]{2,1,0:T(8,128)}), f32[32,8,128]{2,1,0:T(8,128)S(1)}, u32[]{:S(2)}, u32[]{:S(2)}) async-start(f32[32,8,128]{2,1,0:T(8,128)} %get-tuple-element.17), calls=%async_computation.1 | async-start | bytes 262144 | tf_op jit(solution)/shard_map/all_to_all | solution.py:351
  29.0 3.4 %collective-permute-start = (f32[72,64]{1,0:T(8,128)S(1)}, f32[72,64]{1,0:T(8,128)S(1)}, u32[]{:S(2)}, u32[]{:S(2)}) collective-permute-start(f32[72,64]{1,0:T(8,128)S(1)} %copy-done), channel_id=1, source_target_pairs={{0,8},{8,0},{1,9},{9,1},{2,10},{10,2},{3,11},{11,3},{4,12},{12,4},... | collective-permute-start | bytes 55304 | tf_op jit(solution)/shard_map/ppermute | solution.py:372
  32.4 3.3 %shard_map.96 = bf16[16,32,256]{2,1,0:T(8,128)(2,1)} custom-call(bf16[16,144,128]{2,1,0:T(8,128)(2,1)S(1)} %all_to_all.15.recv_ref, f32[8,2,144,128]{3,2,1,0:T(8,128)S(1)} %get-tuple-element.18.win_ref, bf16[2,256,512]{2,1,0:T(8,128)(2,1)S(1)} %copy-done.2, bf16[2,512,256]{2,1,0:T(8,128)(2,1)S(1)} %copy-done.1), custom_call_target="tpu_custom_call" | custom-call | flops 4294967296 | bytes 1048576 | tf_op jit(solution)/shard_map/pallas_call | solution.py:374
  35.7 0.0 collective-permute-done.refs_2_
  35.7 1.3 %all-to-all-done.1.refs_0_.grad_ref = f32[32,8,128]{2,1,0:T(8,128)S(1)} async-done(((f32[32,8,128]{2,1,0:T(8,128)}), f32[32,8,128]{2,1,0:T(8,128)S(1)}, u32[]{:S(2)}, u32[]{:S(2)}) %all-to-all-start.1) | async-done | bytes 131104 | tf_op jit(solution)/shard_map/all_to_all | solution.py:351
  37.0 0.3 shard_map.97
  37.3 0.2 collective-permute-start.3
  37.5 3.3 %collective-permute-start.2 = (f32[64,256]{1,0:T(8,128)S(1)}, f32[64,256]{1,0:T(8,128)S(1)}, u32[]{:S(2)}, u32[]{:S(2)}) collective-permute-start(f32[64,256]{1,0:T(8,128)S(1)} %shard_map.97), channel_id=1, source_target_pairs={{0,2},{1,3},{2,0},{3,1},{4,6},{5,7},{6,4},{7,5},{8,10},{9,11},{10,... | collective-permute-start | bytes 196616 | tf_op jit(solution)/shard_map/ppermute | solution.py:323
  40.8 0.5 collective-permute-start.1
  41.2 3.5 %all-to-all-start.2 = ((bf16[16,32,256]{2,1,0:T(8,128)(2,1)}), bf16[16,32,256]{2,1,0:T(8,128)(2,1)S(1)}, u32[]{:S(2)}, u32[]{:S(2)}) async-start(bf16[16,32,256]{2,1,0:T(8,128)(2,1)} %shard_map.96), calls=%async_computation.2 | async-start | bytes 524288 | tf_op jit(solution)/shard_map/all_to_all | solution.py:351
  44.8 0.0 collective-permute-done.3
  44.8 1.2 %collective-permute-done.2 = f32[64,256]{1,0:T(8,128)S(1)} collective-permute-done((f32[64,256]{1,0:T(8,128)S(1)}, f32[64,256]{1,0:T(8,128)S(1)}, u32[]{:S(2)}, u32[]{:S(2)}) %collective-permute-start.2) | collective-permute-done | bytes 65568 | tf_op jit(solution)/shard_map/ppermute | solution.py:323
  46.0 1.8 %collective-permute-done.1 = f32[64,256]{1,0:T(8,128)S(1)} collective-permute-done((f32[64,256]{1,0:T(8,128)S(1)}, f32[64,256]{1,0:T(8,128)S(1)}, u32[]{:S(2)}, u32[]{:S(2)}) %collective-permute-start.1) | collective-permute-done | bytes 65568 | tf_op jit(solution)/shard_map/ppermute | solution.py:323
  47.8 4.5 %collective-permute-start.4 = (f32[64,256]{1,0:T(8,128)S(1)}, f32[64,256]{1,0:T(8,128)S(1)}, u32[]{:S(2)}, u32[]{:S(2)}) collective-permute-start(f32[64,256]{1,0:T(8,128)S(1)} %add_add_fusion.near_ref), channel_id=1, source_target_pairs={{0,6},{1,7},{2,4},{3,5},{4,2},{5,3},{6,0},{7,1},{8,14},{9,15},{10,... | collective-permute-start | bytes 196616 | tf_op jit(solution)/shard_map/ppermute | solution.py:327
  52.3 3.2 %collective-permute-done.4.far_ref = f32[64,256]{1,0:T(8,128)S(1)} collective-permute-done((f32[64,256]{1,0:T(8,128)S(1)}, f32[64,256]{1,0:T(8,128)S(1)}, u32[]{:S(2)}, u32[]{:S(2)}) %collective-permute-start.4) | collective-permute-done | bytes 65568 | tf_op jit(solution)/shard_map/ppermute | solution.py:327
  55.5 0.0 all-to-all-done.2.recv_ref
  55.5 0.9 %shard_map.98 = (bf16[64,2048]{1,0:T(8,128)(2,1)}, f32[64,256]{1,0:T(8,128)}, f32[64,256]{1,0:T(8,128)}) custom-call(bf16[16,32,256]{2,1,0:T(8,128)(2,1)S(1)} %all-to-all-done.2.recv_ref, f32[32,8,128]{2,1,0:T(8,128)S(1)} %all-to-all-done.1.refs_0_.grad_ref, f32[64,256]{1,0:T(8,128)S(1)} %add_add_fusion.near_ref, f32[64,256]{1,0:T(8,128)S(1)} %collective-permute-done.4.far_ref), custom_call_target="tpu_custom_call" | custom-call | flops 4194304 | bytes 1048576 | tf_op jit(solution)/shard_map/pallas_call | solution.py:389
  (3 shorter events, 0.0 us)
Async XLA Ops:
  0.6 19.5 %copy-start.1 = (bf16[2,512,256]{2,1,0:T(8,128)(2,1)S(1)}, bf16[2,512,256]{2,1,0:T(8,128)(2,1)}, u32[]{:S(2)}) copy-start(bf16[2,512,256]{2,1,0:T(8,128)(2,1)} %constant.5.clone.inv_ref) | copy-start | bytes 1572868
  0.6 19.5 %copy-start.2 = (bf16[2,256,512]{2,1,0:T(8,128)(2,1)S(1)}, bf16[2,256,512]{2,1,0:T(8,128)(2,1)}, u32[]{:S(2)}) copy-start(bf16[2,256,512]{2,1,0:T(8,128)(2,1)} %constant.4.clone.fwd_ref) | copy-start | bytes 1572868
  20.1 8.9 %copy-start = (f32[72,64]{1,0:T(8,128)S(1)}, f32[72,64]{1,0:T(8,128)}, u32[]{:S(2)}) copy-start(f32[72,64]{1,0:T(8,128)} %get-tuple-element.19.refs_1_) | copy-start | bytes 55300
  23.9 13.1 %all-to-all-start.1 = ((f32[32,8,128]{2,1,0:T(8,128)}), f32[32,8,128]{2,1,0:T(8,128)S(1)}, u32[]{:S(2)}, u32[]{:S(2)}) async-start(f32[32,8,128]{2,1,0:T(8,128)} %get-tuple-element.17), calls=%async_computation.1 | async-start | bytes 262144 | tf_op jit(solution)/shard_map/all_to_all | solution.py:351
  29.0 6.7 %collective-permute-start = (f32[72,64]{1,0:T(8,128)S(1)}, f32[72,64]{1,0:T(8,128)S(1)}, u32[]{:S(2)}, u32[]{:S(2)}) collective-permute-start(f32[72,64]{1,0:T(8,128)S(1)} %copy-done), channel_id=1, source_target_pairs={{0,8},{8,0},{1,9},{9,1},{2,10},{10,2},{3,11},{11,3},{4,12},{12,4},... | collective-permute-start | bytes 55304 | tf_op jit(solution)/shard_map/ppermute | solution.py:372
  37.3 7.5 %collective-permute-start.3 = (f32[64,256]{1,0:T(8,128)S(1)}, f32[64,256]{1,0:T(8,128)S(1)}, u32[]{:S(2)}, u32[]{:S(2)}) collective-permute-start(f32[64,256]{1,0:T(8,128)S(1)} %shard_map.97), channel_id=1, source_target_pairs={{0,1},{1,0},{2,3},{3,2},{4,5},{5,4},{6,7},{7,6},{8,9},{9,8},{10,11... | collective-permute-start | bytes 196616 | tf_op jit(solution)/shard_map/ppermute | solution.py:323
  37.5 8.5 %collective-permute-start.2 = (f32[64,256]{1,0:T(8,128)S(1)}, f32[64,256]{1,0:T(8,128)S(1)}, u32[]{:S(2)}, u32[]{:S(2)}) collective-permute-start(f32[64,256]{1,0:T(8,128)S(1)} %shard_map.97), channel_id=1, source_target_pairs={{0,2},{1,3},{2,0},{3,1},{4,6},{5,7},{6,4},{7,5},{8,10},{9,11},{10,... | collective-permute-start | bytes 196616 | tf_op jit(solution)/shard_map/ppermute | solution.py:323
  40.8 7.0 %collective-permute-start.1 = (f32[64,256]{1,0:T(8,128)S(1)}, f32[64,256]{1,0:T(8,128)S(1)}, u32[]{:S(2)}, u32[]{:S(2)}) collective-permute-start(f32[64,256]{1,0:T(8,128)S(1)} %shard_map.97), channel_id=1, source_target_pairs={{0,3},{1,2},{2,1},{3,0},{4,7},{5,6},{6,5},{7,4},{8,11},{9,10},{10,... | collective-permute-start | bytes 196616 | tf_op jit(solution)/shard_map/ppermute | solution.py:323
  41.2 14.3 %all-to-all-start.2 = ((bf16[16,32,256]{2,1,0:T(8,128)(2,1)}), bf16[16,32,256]{2,1,0:T(8,128)(2,1)S(1)}, u32[]{:S(2)}, u32[]{:S(2)}) async-start(bf16[16,32,256]{2,1,0:T(8,128)(2,1)} %shard_map.96), calls=%async_computation.2 | async-start | bytes 524288 | tf_op jit(solution)/shard_map/all_to_all | solution.py:351
  47.8 7.7 %collective-permute-start.4 = (f32[64,256]{1,0:T(8,128)S(1)}, f32[64,256]{1,0:T(8,128)S(1)}, u32[]{:S(2)}, u32[]{:S(2)}) collective-permute-start(f32[64,256]{1,0:T(8,128)S(1)} %add_add_fusion.near_ref), channel_id=1, source_target_pairs={{0,6},{1,7},{2,4},{3,5},{4,2},{5,3},{6,0},{7,1},{8,14},{9,15},{10,... | collective-permute-start | bytes 196616 | tf_op jit(solution)/shard_map/ppermute | solution.py:327
